TPU v7x, 32 devices: a whole 2x2x4 slice. The times are simulated.
32 devices in a mesh: space: 4 (over z), chan: 8 (over y, x, core).
Axes of the slice: x: 2, y: 2, z: 4, core: 2. Of those that a mesh axis runs over, the one named last changes fastest.
Arguments:
- images: bfloat16 [512, 16, 16, 128], P('chan', None, 'space'), may hold values from -6 to 6
- depth_filter: float32 [27, 512], P(None, 'chan'), may hold values from -1.25 to 1.25
- point_filter: bfloat16 [512, 512], P('chan'), may hold values from -0.25 to 0.25
- grad_out: bfloat16 [512, 16, 16, 128], P('chan', None, 'space'), may hold values from -6 to 6
Outputs:
- block_out: bfloat16 [512, 16, 16, 128], P('chan', None, 'space')
- point_grad: float32 [512, 512], P('chan', 'space')
- input_grad: bfloat16 [512, 16, 16, 128], P('chan', None, 'space')
- depth_grad: float32 [27, 512], P(None, 'chan')
All inputs are finite; a program needn't handle non-finite values.
Results may differ from a plain program's by a relative error of at most 0.0049.
Values may be sent and summed in bfloat16 or wider, within the bound.
No kernel may reach another device: no remote copies, remote signals or barrier semaphores. Data moves between devices by JAX's collectives and lax.ppermute only.
A program may use at most 128 MiB of HBM per device.

v0:
```python
import math

import jax
import jax.numpy as jnp
from jax import lax
from jax.sharding import PartitionSpec as P


def with_halo(cells, sides, width):
    for axis, dim in sides:
        count = lax.axis_size(axis)
        ends = count - 1
        head = lax.slice_in_dim(cells, 0, width, axis=dim)
        tail = lax.slice_in_dim(cells, cells.shape[dim] - width, cells.shape[dim], axis=dim)
        cells = jnp.concatenate(
            [
                lax.ppermute(tail, axis, [(i, (i + 1) % count) for i in range(ends)]),
                cells,
                lax.ppermute(head, axis, [((i + 1) % count, i) for i in range(ends)]),
            ],
            axis=dim,
        )
    return cells


def depth_forward(padded, tap_weights, planes, row_count, col_count):
    summed = jnp.zeros((padded.shape[0], planes, row_count, col_count), jnp.float32)
    for tap_index in range(27):
        plane_off, row_off, col_off = (tap_index // 9, tap_index // 3 % 3, tap_index % 3)
        window = padded[
            :,
            plane_off : plane_off + planes,
            row_off : row_off + row_count,
            col_off : col_off + col_count,
        ]
        summed = summed + tap_weights[tap_index][:, None, None, None] * window.astype(jnp.float32)
    return summed


def depth_backward(padded, tap_weights, planes, row_count, col_count):
    summed = jnp.zeros((padded.shape[0], planes, row_count, col_count), jnp.float32)
    for tap_index in range(27):
        plane_off, row_off, col_off = (
            2 - tap_index // 9,
            2 - tap_index // 3 % 3,
            2 - tap_index % 3,
        )
        window = padded[
            :,
            plane_off : plane_off + planes,
            row_off : row_off + row_count,
            col_off : col_off + col_count,
        ]
        summed = summed + tap_weights[tap_index][:, None, None, None] * window.astype(jnp.float32)
    return summed


def tap_sums(padded, back_hidden, planes, row_count, col_count):
    collected = []
    for tap_index in range(27):
        plane_off, row_off, col_off = (tap_index // 9, tap_index // 3 % 3, tap_index % 3)
        window = padded[
            :,
            plane_off : plane_off + planes,
            row_off : row_off + row_count,
            col_off : col_off + col_count,
        ]
        collected.append(
            jnp.sum(window.astype(jnp.float32) * back_hidden.astype(jnp.float32), axis=(1, 2, 3))
        )
    return jnp.stack(collected)


def with_rims(field):
    rimmed = with_halo(field, (("space", 2),), 1)
    return jnp.pad(rimmed, ((0, 0), (1, 1), (0, 0), (1, 1)))


def body(images, depth_filter, point_filter, grad_out):
    chan_count, planes, row_count, col_count = images.shape
    cell_count = planes * row_count * col_count
    grad_scale = 1.0 / math.sqrt(cell_count * lax.axis_size("space"))
    padded_in = with_rims(images)
    hidden = depth_forward(padded_in, depth_filter, planes, row_count, col_count).astype(
        jnp.bfloat16
    )
    flat_grad = grad_out.reshape(chan_count, cell_count)
    own_start = lax.axis_index("chan") * chan_count
    arriving = lax.all_gather(hidden, "chan", axis=0, tiled=True)
    row_total = arriving.shape[0]
    rows_flat = arriving.reshape(row_total, cell_count)
    columns = point_filter
    mixed_acc = jnp.dot(columns, rows_flat, preferred_element_type=jnp.float32)
    filter_term = lax.dot_general(
        flat_grad, rows_flat, (((1,), (1,)), ((), ())), preferred_element_type=jnp.float32
    )
    block_out = mixed_acc.astype(jnp.bfloat16).reshape(images.shape)
    grad_piece = lax.all_gather(grad_out, "chan", axis=0, tiled=True)
    filter_piece = lax.all_gather(point_filter, "chan", axis=0, tiled=True)
    row_total = grad_piece.shape[0]
    columns = lax.dynamic_slice_in_dim(filter_piece, own_start, chan_count, 1)
    grad_rows = grad_piece.reshape(row_total, cell_count)
    back_sum = lax.dot_general(
        columns, grad_rows, (((0,), (0,)), ((), ())), preferred_element_type=jnp.float32
    )
    back_hidden = back_sum.astype(jnp.bfloat16).reshape(images.shape)
    point_grad = (
        lax.psum_scatter(filter_term, "space", scatter_dimension=1, tiled=True) * grad_scale
    )
    padded_back = with_rims(back_hidden)
    input_grad = depth_backward(padded_back, depth_filter, planes, row_count, col_count).astype(
        jnp.bfloat16
    )
    local_taps = tap_sums(padded_in, back_hidden, planes, row_count, col_count)
    depth_grad = lax.psum(local_taps, "space") * grad_scale
    return (block_out, point_grad, input_grad, depth_grad)


def solution(mesh):
    placed = (
        P("chan", None, "space", None),
        P(None, "chan"),
        P("chan", None),
        P("chan", None, "space", None),
    )
    return jax.shard_map(
        body,
        mesh=mesh,
        in_specs=placed,
        out_specs=(
            P("chan", None, "space", None),
            P("chan", "space"),
            P("chan", None, "space", None),
            P(None, "chan"),
        ),
        check_vma=False,
    )
```

profile of v0, /device:TPU:0, one launch (start us, length us, event | category | flops | bytes accessed | tf_op | source)
XLA Modules:
  0.0 185.9 jit_solution(4554713879828025471)
XLA Ops:
  7.2 2.5 %copy.55 = bf16[64,16,4,128]{3,1,2,0:T(8,128)(2,1)} copy(bf16[64,16,4,128]{3,2,1,0:T(4,128)(2,1)} %param.7) | data formatting | bytes 2097152 | tf_op args[3]
  10.6 4.9 %collective-permute-start = (bf16[64,16,1,128]{3,0,2,1:T(8,128)(2,1)S(1)}, bf16[64,16,1,128]{3,0,2,1:T(8,128)(2,1)S(1)}, u32[]{:S(2)}, u32[]{:S(2)}) collective-permute-start(bf16[64,16,1,128]{3,0,2,1:T(8,128)(2,1)S(1)} %get-tuple-element.55), channel_id=1, source_target_pairs={{0,8},{8,16},{16,24},{1,9},{9,17},{17,25},{2,10},{10,18},{18,26},{... | collective-permute-start | bytes 786440 | tf_op jit(solution)/shard_map/ppermute | solution.py:17
  17.1 4.0 %collective-permute-done = bf16[64,16,1,128]{3,0,2,1:T(8,128)(2,1)S(1)} collective-permute-done((bf16[64,16,1,128]{3,0,2,1:T(8,128)(2,1)S(1)}, bf16[64,16,1,128]{3,0,2,1:T(8,128)(2,1)S(1)}, u32[]{:S(2)}, u32[]{:S(2)}) %collective-permute-start) | collective-permute-done | bytes 262176 | tf_op jit(solution)/shard_map/ppermute | solution.py:17
  21.1 4.1 %collective-permute-done.1 = bf16[64,16,1,128]{3,0,2,1:T(8,128)(2,1)S(1)} collective-permute-done((bf16[64,16,1,128]{3,0,2,1:T(8,128)(2,1)S(1)}, bf16[64,16,1,128]{3,0,2,1:T(8,128)(2,1)S(1)}, u32[]{:S(2)}, u32[]{:S(2)}) %collective-permute-start.1) | collective-permute-done | bytes 262176 | tf_op jit(solution)/shard_map/ppermute | solution.py:19
  25.2 3.0 %select_maximum_fusion.2 = bf16[64,18,6,130]{3,0,2,1:T(8,128)(2,1)S(1)} fusion(bf16[64,16,1,128]{3,0,2,1:T(8,128)(2,1)S(1)} %collective-permute-done.1, bf16[64,16,4,128]{3,0,2,1:T(8,128)(2,1)S(1)} %copy.47, bf16[64,16,1,128]{3,0,2,1:T(8,128)(2,1)S(1)} %collective-permute-done), kind=kLoop, calls=%fused_computation.40 | loop fusion | flops 17072640 | bytes 3369984 | tf_op jit(solution)/shard_map/concatenate | solution.py:15
  28.4 9.6 %fusion.31 = bf16[64,16,4,128]{3,0,2,1:T(8,128)(2,1)} fusion(bf16[64,16,4,128]{3,0,2,1:T(8,128)(2,1)S(1)} %copy.47, bf16[64,16,1,128]{3,0,2,1:T(8,128)(2,1)S(1)} %collective-permute-done.1, bf16[64,16,1,128]{3,0,2,1:T(8,128)(2,1)S(1)} %collective-permute-done, f32[64]{0:T(128)S(1)} %get-tuple-element.82, f32[64]{0:T(128)S(1)} %get-tuple-element.83, ...), kind=kLoop, calls=%fused_computation.96 | loop fusion | flops 43515904 | bytes 27794176 | tf_op jit(solution)/shard_map/convert_element_type | solution.py:84
  38.1 13.8 %all_gather.10 = bf16[512,512]{1,0:T(8,128)(2,1)} all-gather(bf16[64,512]{1,0:T(8,128)(2,1)} %param.6), channel_id=1, replica_groups=mesh['space'=4,'chan'=8] {'chan'}, dimensions={0}, use_global_device_ids=true | all-gather | bytes 589824 | tf_op jit(solution)/shard_map/all_gather | solution.py:99
  52.0 17.4 %all-gather.5.cloned.1.call-done = bf16[512,16,4,128]{3,1,2,0:T(8,128)(2,1)} async-done(((bf16[64,16,4,128]{3,1,2,0:T(8,128)(2,1)}), bf16[512,16,4,128]{3,1,2,0:T(8,128)(2,1)}) %all-gather.5.cloned.1.call-update) | async-done | bytes 8388624 | tf_op jit(solution)/shard_map/all_gather | solution.py:98
  69.4 14.0 %copy.56 = bf16[512,16,4,128]{0,3,2,1:T(8,128)(2,1)} copy(bf16[512,16,4,128]{3,1,2,0:T(8,128)(2,1)} %all-gather.5.cloned.1.call-done) | data formatting | bytes 16777216 | tf_op jit(solution)/shard_map/all_gather | solution.py:98
  83.4 7.2 %convolution_convert_fusion = bf16[64,8192]{1,0:T(8,128)(2,1)} fusion(bf16[512,8192]{0,1:T(8,128)(2,1)} %bitcast.95, bf16[512,512]{1,0:T(8,128)(2,1)} %all_gather.10, s32[]{:T(128)S(6)} %select_n.3), kind=kOutput, calls=%fused_computation.32 | convolution fusion | flops 537395200 | bytes 9568260 | tf_op jit(solution)/shard_map/dot_general | solution.py:103
  90.6 2.6 %reshape.51 = bf16[64,16,4,128]{3,2,1,0:T(4,128)(2,1)} reshape(bf16[64,8192]{1,0:T(8,128)(2,1)} %convolution_convert_fusion) | data formatting | bytes 2097152 | tf_op jit(solution)/shard_map/reshape | solution.py:106
  93.3 2.1 %copy.57 = bf16[64,16,4,128]{3,0,2,1:T(8,128)(2,1)S(1)} copy(bf16[64,16,4,128]{3,2,1,0:T(4,128)(2,1)} %reshape.51) | data formatting | bytes 2097152 | tf_op jit(solution)/shard_map/reshape | solution.py:106
  96.2 4.1 %collective-permute-start.2 = (bf16[64,16,1,128]{3,0,2,1:T(8,128)(2,1)}, bf16[64,16,1,128]{3,0,2,1:T(8,128)(2,1)}, u32[]{:S(2)}, u32[]{:S(2)}) collective-permute-start(bf16[64,16,1,128]{3,0,2,1:T(8,128)(2,1)} %get-tuple-element.53), channel_id=1, source_target_pairs={{0,8},{8,16},{16,24},{1,9},{9,17},{17,25},{2,10},{10,18},{18,26},{... | collective-permute-start | bytes 786440 | tf_op jit(solution)/shard_map/ppermute | solution.py:17
  101.9 5.4 %fusion.62 = (f32[64]{0:T(128)}, f32[64]{0:T(128)}, f32[64]{0:T(128)}, f32[64]{0:T(128)}, f32[64]{0:T(128)}, /*index=5*/f32[64]{0:T(128)}, f32[64]{0:T(128)}, f32[64]{0:T(128)}, f32[64]{0:T(128)}) fusion(bf16[64,16,1,128]{3,0,2,1:T(8,128)(2,1)} %copy-done.8, bf16[64,16,4,128]{3,0,2,1:T(8,128)(2,1)S(1)} %copy-done.1, ...), kind=kLoop, calls=%fused_computation.127 | loop fusion | flops 15728064 | bytes 9963776 | tf_op jit(solution)/shard_map/reduce_sum | solution.py:69
  107.3 8.0 %fusion.72 = (f32[64]{0:T(128)}, f32[64]{0:T(128)}, f32[64]{0:T(128)}, f32[64]{0:T(128)}, f32[64]{0:T(128)}, /*index=5*/f32[64]{0:T(128)}, f32[64]{0:T(128)}, f3...) fusion(bf16[64,18,6,130]{3,0,2,1:T(8,128)(2,1)S(1)} %select_max, ...), kind=kLoop, calls=%fused_computation.137 | loop fusion | flops 28834688 | bytes 19927552 | tf_op jit(solution)/shard_map/reduce_sum | solution.py:69
  115.3 2.8 %stack.111 = f32[27,64]{1,0:T(8,128)S(1)} concatenate(f32[1,64]{1,0:T(1,128)} %bitcast.120, f32[1,64]{1,0:T(1,128)} %bitcast.121, f32[1,64]{1,0:T(1,128)} %bitcast.122, f32[1,64]{1,0:T(1,128)} %bitcast.123, f32[1,64]{1,0:T(1,128)} %bitcast.124, f32[1,64]{1,0:T(1,128)} %bitcast.125, f32[1,64]{1,0:T(1,128)} %bitcast.116, f32[1,64]{1,0:T(1,128)} %bitcast.115, f32[1,64]{1,0:T(1,128)} %bitcast.114, ...), dimensions={0} | concatenate | bytes 13824 | tf_op jit(solution)/shard_map/stack | solution.py:71
  118.1 19.4 %psum.7 = f32[27,64]{1,0:T(8,128)S(1)} all-reduce(f32[27,64]{1,0:T(8,128)S(1)} %stack.111), channel_id=1, replica_groups=mesh['space'=4,'chan'=8] {'space'}, use_global_device_ids=true, to_apply=%region_28.29 | all-reduce | flops 1728 | bytes 13824 | tf_op jit(solution)/shard_map/psum | solution.py:115
  138.1 6.9 %convolution_bitcast_fusion = f32[64,512]{1,0:T(8,128)} fusion(bf16[512,16,4,128]{3,0,2,1:T(8,128)(2,1)} %all-gather.3.cloned.1.call-done, bf16[64,16,4,128]{3,2,1,0:T(4,128)(2,1)} %param.7), kind=kOutput, calls=%fused_computation.139 | convolution fusion | flops 536870912 | bytes 9568256 | tf_op jit(solution)/shard_map/dot_general | solution.py:94
  145.0 12.4 %copy.53 = bf16[512,16,4,128]{0,3,2,1:T(8,128)(2,1)} copy(bf16[512,16,4,128]{3,0,2,1:T(8,128)(2,1)} %all-gather.3.cloned.1.call-done) | data formatting | bytes 16777216 | tf_op jit(solution)/shard_map/all_gather | solution.py:89
  157.6 4.1 %select_maximum_fusion = bf16[64,18,6,130]{3,0,2,1:T(8,128)(2,1)S(1)} fusion(bf16[64,16,1,128]{3,0,2,1:T(8,128)(2,1)} %collective-permute-done.3, bf16[64,16,4,128]{3,0,2,1:T(8,128)(2,1)S(1)} %copy-done.4, bf16[64,16,1,128]{3,0,2,1:T(8,128)(2,1)} %collective-permute-done.2), kind=kLoop, calls=%fused_computation.38 | loop fusion | flops 17072640 | bytes 3369984 | tf_op jit(solution)/shard_map/concatenate | solution.py:15
  162.0 10.0 %fusion.73 = bf16[64,16,4,128]{3,0,2,1:T(8,128)(2,1)S(1)} fusion(bf16[64,16,4,128]{3,0,2,1:T(8,128)(2,1)S(1)} %copy-done.4, bf16[64,18,6,130]{3,0,2,1:T(8,128)(2,1)S(1)} %select_maximum_fusion, bf16[64,16,1,128]{3,0,2,1:T(8,128)(2,1)} %collective-permute-done.2, bf16[64,16,1,128]{3,0,2,1:T(8,128)(2,1)} %collective-permute-done.3, f32[64]{0:T(128)S(1)} %copy-done.16, ...), kind=kLoop, calls=%fused_computation.138 | loop fusion | flops 43515904 | bytes 27794176 | tf_op jit(solution)/shard_map/convert_element_type | solution.py:111
  172.1 2.6 %fusion = bf16[64,8192]{1,0:T(8,128)(2,1)S(1)} fusion(bf16[512,8192]{0,1:T(8,128)(2,1)S(1)} %bitcast.98, bf16[64,512]{1,0:T(8,128)(2,1)S(1)} %copy-done.9), kind=kOutput, calls=%fused_computation.34 | convolution fusion | flops 537395200 | bytes 9502720 | tf_op jit(solution)/shard_map/dot_general | solution.py:93
  174.7 1.5 reshape.49
  176.2 1.8 copy.63
  (138 shorter events, 6.8 us)
Async XLA Ops:
  7.2 62.2 %all-gather.5.cloned.1.call-start = ((), (), s32[]{:S(2)}) async-start(), calls=%async_computation.3 | async-start | bytes 9437184 | tf_op jit(solution)/shard_map/all_gather | solution.py:98
  9.8 128.3 %all-gather.3.cloned.1.call-start = ((), (), s32[]{:S(2)}) async-start(), calls=%async_computation.1 | async-start | bytes 9437184 | tf_op jit(solution)/shard_map/all_gather | solution.py:89
  10.5 17.7 %copy-start = (bf16[64,16,4,128]{3,0,2,1:T(8,128)(2,1)}, bf16[64,16,4,128]{3,0,2,1:T(8,128)(2,1)S(1)}, u32[]{:S(2)}) copy-start(bf16[64,16,4,128]{3,0,2,1:T(8,128)(2,1)S(1)} %copy.47) | copy-start | bytes 3145732
  10.6 10.5 %collective-permute-start = (bf16[64,16,1,128]{3,0,2,1:T(8,128)(2,1)S(1)}, bf16[64,16,1,128]{3,0,2,1:T(8,128)(2,1)S(1)}, u32[]{:S(2)}, u32[]{:S(2)}) collective-permute-start(bf16[64,16,1,128]{3,0,2,1:T(8,128)(2,1)S(1)} %get-tuple-element.55), channel_id=1, source_target_pairs={{0,8},{8,16},{16,24},{1,9},{9,17},{17,25},{2,10},{10,18},{18,26},{... | collective-permute-start | bytes 786440 | tf_op jit(solution)/shard_map/ppermute | solution.py:17
  15.5 9.7 %collective-permute-start.1 = (bf16[64,16,1,128]{3,0,2,1:T(8,128)(2,1)S(1)}, bf16[64,16,1,128]{3,0,2,1:T(8,128)(2,1)S(1)}, u32[]{:S(2)}, u32[]{:S(2)}) collective-permute-start(bf16[64,16,1,128]{3,0,2,1:T(8,128)(2,1)S(1)} %get-tuple-element.56), channel_id=1, source_target_pairs={{8,0},{16,8},{24,16},{9,1},{17,9},{25,17},{10,2},{18,10},{26,18},{... | collective-permute-start | bytes 786440 | tf_op jit(solution)/shard_map/ppermute | solution.py:19
  16.9 11.3 %copy-start.11 = (f32[64]{0:T(128)}, f32[64]{0:T(128)S(1)}, u32[]{:S(2)}) copy-start(f32[64]{0:T(128)S(1)} %get-tuple-element.80) | copy-start | bytes 772
  16.9 11.3 %copy-start.13 = (f32[64]{0:T(128)}, f32[64]{0:T(128)S(1)}, u32[]{:S(2)}) copy-start(f32[64]{0:T(128)S(1)} %get-tuple-element.81) | copy-start | bytes 772
  16.9 11.3 %copy-start.15 = (f32[64]{0:T(128)}, f32[64]{0:T(128)S(1)}, u32[]{:S(2)}) copy-start(f32[64]{0:T(128)S(1)} %get-tuple-element.82) | copy-start | bytes 772
  16.9 11.3 %copy-start.17 = (f32[64]{0:T(128)}, f32[64]{0:T(128)S(1)}, u32[]{:S(2)}) copy-start(f32[64]{0:T(128)S(1)} %get-tuple-element.83) | copy-start | bytes 772
  16.9 11.3 %copy-start.19 = (f32[64]{0:T(128)}, f32[64]{0:T(128)S(1)}, u32[]{:S(2)}) copy-start(f32[64]{0:T(128)S(1)} %get-tuple-element.57) | copy-start | bytes 772
  16.9 11.3 %copy-start.21 = (f32[64]{0:T(128)}, f32[64]{0:T(128)S(1)}, u32[]{:S(2)}) copy-start(f32[64]{0:T(128)S(1)} %get-tuple-element.58) | copy-start | bytes 772
  16.9 11.3 %copy-start.23 = (f32[64]{0:T(128)}, f32[64]{0:T(128)S(1)}, u32[]{:S(2)}) copy-start(f32[64]{0:T(128)S(1)} %get-tuple-element.59) | copy-start | bytes 772
  17.0 11.3 %copy-start.25 = (f32[64]{0:T(128)}, f32[64]{0:T(128)S(1)}, u32[]{:S(2)}) copy-start(f32[64]{0:T(128)S(1)} %get-tuple-element.60) | copy-start | bytes 772
  17.0 11.3 %copy-start.27 = (f32[64]{0:T(128)}, f32[64]{0:T(128)S(1)}, u32[]{:S(2)}) copy-start(f32[64]{0:T(128)S(1)} %get-tuple-element.61) | copy-start | bytes 772
  17.0 11.3 %copy-start.29 = (f32[64]{0:T(128)}, f32[64]{0:T(128)S(1)}, u32[]{:S(2)}) copy-start(f32[64]{0:T(128)S(1)} %get-tuple-element.62) | copy-start | bytes 772
  17.0 11.3 %copy-start.31 = (f32[64]{0:T(128)}, f32[64]{0:T(128)S(1)}, u32[]{:S(2)}) copy-start(f32[64]{0:T(128)S(1)} %get-tuple-element.63) | copy-start | bytes 772
  17.0 11.3 %copy-start.33 = (f32[64]{0:T(128)}, f32[64]{0:T(128)S(1)}, u32[]{:S(2)}) copy-start(f32[64]{0:T(128)S(1)} %get-tuple-element.64) | copy-start | bytes 772
  17.0 11.3 %copy-start.35 = (f32[64]{0:T(128)}, f32[64]{0:T(128)S(1)}, u32[]{:S(2)}) copy-start(f32[64]{0:T(128)S(1)} %get-tuple-element.65) | copy-start | bytes 772
  38.1 139.9 %reduce-scatter.2.cloned.1.call-start = ((), (), s32[]{:S(2)}) async-start(), calls=%async_computation.2 | async-start | bytes 163840 | tf_op jit(solution)/shard_map/reduce_scatter | solution.py:108
  95.3 12.0 %copy-start.3 = (bf16[64,16,4,128]{3,0,2,1:T(8,128)(2,1)}, bf16[64,16,4,128]{3,0,2,1:T(8,128)(2,1)S(1)}, u32[]{:S(2)}) copy-start(bf16[64,16,4,128]{3,0,2,1:T(8,128)(2,1)S(1)} %copy.57) | copy-start | bytes 3145732
  96.2 61.4 %collective-permute-start.2 = (bf16[64,16,1,128]{3,0,2,1:T(8,128)(2,1)}, bf16[64,16,1,128]{3,0,2,1:T(8,128)(2,1)}, u32[]{:S(2)}, u32[]{:S(2)}) collective-permute-start(bf16[64,16,1,128]{3,0,2,1:T(8,128)(2,1)} %get-tuple-element.53), channel_id=1, source_target_pairs={{0,8},{8,16},{16,24},{1,9},{9,17},{17,25},{2,10},{10,18},{18,26},{... | collective-permute-start | bytes 786440 | tf_op jit(solution)/shard_map/ppermute | solution.py:17
  100.4 57.2 %collective-permute-start.3 = (bf16[64,16,1,128]{3,0,2,1:T(8,128)(2,1)}, bf16[64,16,1,128]{3,0,2,1:T(8,128)(2,1)}, u32[]{:S(2)}, u32[]{:S(2)}) collective-permute-start(bf16[64,16,1,128]{3,0,2,1:T(8,128)(2,1)} %get-tuple-element.54), channel_id=1, source_target_pairs={{8,0},{16,8},{24,16},{9,1},{17,9},{25,17},{10,2},{18,10},{26,18},{... | collective-permute-start | bytes 786440 | tf_op jit(solution)/shard_map/ppermute | solution.py:19
  145.0 12.6 %copy-start.4 = (bf16[64,16,4,128]{3,0,2,1:T(8,128)(2,1)S(1)}, bf16[64,16,4,128]{3,0,2,1:T(8,128)(2,1)}, u32[]{:S(2)}) copy-start(bf16[64,16,4,128]{3,0,2,1:T(8,128)(2,1)} %copy-done.3) | copy-start | bytes 3145732
  157.6 14.4 %slice-start = ((s8[8388608]{0:T(1024)(128)(4,1)}), s8[4194304]{0:T(1024)(128)(4,1)S(1)}, s32[]{:S(2)}) async-start(s8[8388608]{0:T(1024)(128)(4,1)} %bitcast.96), calls=%async_computation.4 | async-start | bytes 8388608
  (42 other events, 279.9 us)
Sparse Core Ops, SparseCore 0:
  10.5 58.8 all-gather.4
  71.8 54.0 all-gather.2
  145.1 16.2 reduce-scatter.1
where the time goes:
time: 187 us; the launch traced here: 186 us
  other arithmetic  42 us (22%)
  local copies, waits for them, and re-layouts  41.7 us (22%)
  blocking collectives  33.2 us (18%)
  waiting for transfers between devices  25.5 us (14%)
  matrix products  16.7 us (9%)
  between operations  14.7 us (8%)
  starting transfers between devices  12 us (6%)
    psum x1, blocking collectives, body(): depth_grad = lax.psum(local_taps, 'space') * grad_scale  19.4 us
    all_gather x1, waiting for transfers between devices, body(): grad_piece = lax.all_gather(grad_out, 'chan', axis=0, tiled=True)  17.4 us
    all_gather x1, local copies, waits for them, and re-layouts, body(): grad_piece = lax.all_gather(grad_out, 'chan', axis=0, tiled=True)  14 us
    all_gather x1, blocking collectives, body(): filter_piece = lax.all_gather(point_filter, 'chan', axis=0, tiled=True)  13.8 us
    reduce_sum x2, other arithmetic, tap_sums(): jnp.sum(window.astype(jnp.float32) * back_hidden.astype(jnp.float32), axi...  13.4 us
    all_gather x1, local copies, waits for them, and re-layouts, body(): arriving = lax.all_gather(hidden, 'chan', axis=0, tiled=True)  12.4 us
    convert_element_type x1, other arithmetic, body(): depth_backward(padded_back, depth_filter, planes, row_count, col_count)  10 us
    convert_element_type x1, other arithmetic, body(): depth_forward(padded_in, depth_filter, planes, row_count, col_count)  9.6 us
  transfers between devices with their start and end apart: 7, of which 3 were waited for; matrix products, arithmetic and copies ran while one was open for 52% of the time, Pallas kernels for 0%

commit v1 on v0

v1 whole, which is shorter than its diff:
```python
import math

import jax
import jax.numpy as jnp
from jax import lax
from jax.experimental import pallas as pl
from jax.experimental.pallas import tpu as pltpu
from jax.sharding import PartitionSpec as P

F32, BF16 = jnp.float32, jnp.bfloat16
IN_VMEM = pl.BlockSpec(memory_space=pltpu.VMEM)


class Place:
    def __init__(self, count):
        self.mids = 2
        self.his = count // 4
        index = lax.axis_index("chan")
        self.core = index % 2
        self.mid = index // 2 % self.mids
        self.hi = index // 2 // self.mids

    def block(self, hi_back, mid_back, core_flip):
        hi = (self.hi + self.his - hi_back) % self.his
        mid = (self.mid + self.mids - mid_back) % self.mids
        core = 1 - self.core if core_flip else self.core
        return hi, mid, core

    def flat(self, hi, mid, core):
        return (hi * self.mids + mid) * 2 + core


def kernel_call(kernel, outs, args, scratch=(), micros=2.0):
    moved = sum(a.size * a.dtype.itemsize for a in args) + sum(math.prod(o.shape) * o.dtype.itemsize for o in outs)
    return pl.pallas_call(
        kernel,
        out_shape=outs,
        in_specs=[IN_VMEM] * len(args),
        out_specs=[IN_VMEM] * len(outs),
        scratch_shapes=list(scratch),
        compiler_params=pltpu.CompilerParams(vmem_limit_bytes=40 * 2**20),
        cost_estimate=pl.CostEstimate(flops=int(micros * 1e9), bytes_accessed=moved, transcendentals=0),
    )(*args)


def shaped(shape, dtype=BF16):
    return jax.ShapeDtypeStruct(shape, dtype)


def raw_to_cells(raw, flat):
    chans, planes, rows, _ = raw.shape

    @pl.loop(0, chans)
    def _(c):
        for p in range(planes):
            flat[pl.ds(p * rows * chans + c, rows, stride=chans), :] = raw[c, p].astype(F32)


def cells_to_raw(flat, raw):
    chans, planes, rows, _ = raw.shape

    @pl.loop(0, chans)
    def _(c):
        for p in range(planes):
            raw[c, p] = flat[pl.ds(p * rows * chans + c, rows, stride=chans), :].astype(raw.dtype)


def relayout_images(images):
    chans, planes, rows, width = images.shape

    def kernel(raw, cells, top, bottom, flat):
        raw_to_cells(raw, flat)

        @pl.loop(0, planes)
        def _(p):
            for r in range(rows):
                value = flat[pl.ds(pl.multiple_of((p * rows + r) * chans, chans), chans), :].astype(BF16)
                cells[p * rows + r] = value
                if r == 0:
                    top[p] = value
                if r == rows - 1:
                    bottom[p] = value

    edge = shaped((planes, chans, width))
    return kernel_call(
        kernel,
        [shaped((planes * rows, chans, width)), edge, edge],
        [images],
        [pltpu.VMEM((planes * rows * chans, width), F32)],
        1.5,
    )


def relayout_grad(grad_out, count):
    chans, planes, rows, width = grad_out.shape
    half = planes * rows // 2

    def kernel(raw, own, other, flat):
        core = Place(count).core
        raw_to_cells(raw, flat)

        @pl.loop(0, half)
        def _(i):
            for out, which in ((own, core), (other, 1 - core)):
                start = pl.multiple_of((which * half + i) * chans, chans)
                out[i] = flat[pl.ds(start, chans), :].astype(BF16)

    part = shaped((half, chans, width))
    return kernel_call(
        kernel, [part, part], [grad_out], [pltpu.VMEM((planes * rows * chans, width), F32)], 1.5
    )


def tap_planes(weights, spread, chans, width):
    turned = jnp.concatenate([weights, jnp.zeros((5, chans), F32)], axis=0).T
    for k in range(27):
        spread[k] = jnp.broadcast_to(turned[:, k : k + 1], (chans, width))


def fill_rims(padded, up, down, planes, rows):
    blank = jnp.zeros(padded.shape[1:], F32)
    for r in range(rows + 2):
        padded[r] = blank
        padded[(planes + 1) * (rows + 2) + r] = blank

    @pl.loop(0, planes)
    def _(p):
        padded[(p + 1) * (rows + 2)] = up(p).astype(F32)
        padded[(p + 1) * (rows + 2) + rows + 1] = down(p).astype(F32)


def depthwise(padded, spread, first, count, rows, store, flipped):
    _, chans, width = padded.shape
    lane = lax.broadcasted_iota(jnp.int32, (16, width), 1)

    @pl.loop(0, count)
    def _(i):
        for start in range(0, chans, 16):
            group = slice(start, start + 16)
            sums = [[None] * 3 for _ in range(rows)]
            for a in range(3):
                for line in range(rows + 2):
                    cells = padded[(first + i + a) * (rows + 2) + line, group]
                    for b in range(3):
                        r = line - b
                        if 0 <= r < rows:
                            for e in range(3):
                                tap = 9 * a + 3 * b + e
                                term = spread[26 - tap if flipped else tap, group] * cells
                                sums[r][e] = term if sums[r][e] is None else sums[r][e] + term
            for r in range(rows):
                before = jnp.where(lane == 0, 0.0, pltpu.roll(sums[r][0], 1, 1))
                after = jnp.where(lane == width - 1, 0.0, pltpu.roll(sums[r][2], width - 1, 1))
                store(i, r, group, sums[r][1] + before + after)


def hidden_halves(cells, up, down, weights, count, planes, rows):
    _, chans, width = cells.shape
    half = planes // 2

    def kernel(cells, up, down, weights, own, other, padded, spread):
        core = Place(count).core
        tap_planes(weights[...], spread, chans, width)
        fill_rims(padded, lambda p: up[p], lambda p: down[p], planes, rows)

        @pl.loop(0, planes)
        def _(p):
            for r in range(rows):
                padded[(p + 1) * (rows + 2) + r + 1] = cells[p * rows + r].astype(F32)

        for out, which in ((own, core), (other, 1 - core)):

            def store(i, r, group, value, out=out):
                out[i * rows + r, group] = value.astype(BF16)

            depthwise(padded, spread, which * half, half, rows, store, False)

    part = shaped((half * rows, chans, width))
    return kernel_call(
        kernel,
        [part, part],
        [cells, up, down, weights],
        [pltpu.VMEM(((planes + 2) * (rows + 2), chans, width), F32), pltpu.VMEM((27, chans, width), F32)],
        5.0,
    )


def picked(table, starts, chans):
    total, wide = table.shape[1], len(starts) * chans
    col = lax.broadcasted_iota(jnp.int32, (total, wide), 1)
    row = lax.broadcasted_iota(jnp.int32, (total, wide), 0)
    want = jnp.zeros((total, wide), jnp.int32)
    for b, start in enumerate(starts):
        want = jnp.where((col >= b * chans) & (col < (b + 1) * chans), start + col - b * chans, want)
    choice = jnp.where(row == want, 1.0, 0.0).astype(BF16)
    return jnp.dot(table, choice, preferred_element_type=F32).astype(BF16)


def pack_grad(own, arrived, filter_own, filter_arrived, count):
    half, chans, width = own.shape
    part = half // 2
    his, mids = count // 4, 2
    hi_slices, mid_slices = mids * 2 * chans // width, his * 2 * chans // width

    def kernel(own, arrived, filter_own, filter_arrived, *outs):
        place = Place(count)
        table = jnp.concatenate([filter_own[...], filter_arrived[...]], axis=0)
        to_hi, to_mid = outs[: his - 1], outs[his - 1 : his + mids - 2]
        mine_hi, mine_mid = outs[-2:]

        def columns(for_hi, hi, mid):
            if for_hi:
                cells = [(hi, (mid + mids - t) % mids) for t in range(mids)]
            else:
                cells = [((hi + his - s) % his, mid) for s in range(his)]
            starts = [
                place.flat(hi_, mid_, place.core if q == 0 else 1 - place.core) * chans
                for hi_, mid_ in cells
                for q in range(2)
            ]
            return picked(table, starts, chans)

        def put(out, base, value):
            for i in range(value.shape[1] // width):
                out[base + i] = value[:, i * width : (i + 1) * width]

        for refs, offset in ((to_hi, 0), (to_mid, part)):

            @pl.loop(0, part)
            def _(i):
                for ref in refs:
                    ref[i, :chans] = own[offset + i]
                    ref[i, chans:] = arrived[offset + i]

        for s, ref in enumerate(to_hi, 1):
            put(ref, part, columns(True, (place.hi + s) % his, place.mid))
        for t, ref in enumerate(to_mid, 1):
            put(ref, part, columns(False, place.hi, (place.mid + t) % mids))
        put(mine_hi, 0, columns(True, place.hi, place.mid))
        put(mine_mid, 0, columns(False, place.hi, place.mid))

    outs = (
        [shaped((part + hi_slices, 2 * chans, width))] * (his - 1)
        + [shaped((part + mid_slices, 2 * chans, width))] * (mids - 1)
        + [shaped((hi_slices, 2 * chans, width)), shaped((mid_slices, 2 * chans, width))]
    )
    outs = kernel_call(kernel, outs, [own, arrived, filter_own, filter_arrived], (), 1.5)
    return outs[: his - 1], outs[his - 1 : his + mids - 2], outs[-2], outs[-1]


def back_terms(mine, arrived, filter_mine, sends):
    slices, both, width = filter_mine.shape
    part = mine.shape[0] - slices
    sources = 1 + len(arrived)
    wide = slices * width
    step = math.gcd(part, 4)

    def kernel(mine, filter_mine, *refs):
        blocks = [mine, *refs[: sources - 1]]
        outs, block_ref = refs[sources - 1 : -1], refs[-1]
        rows = [jnp.concatenate([filter_mine[i] for i in range(slices)], axis=1)]
        for ref in blocks[1:]:
            rows.append(jnp.concatenate([ref[part + i] for i in range(slices)], axis=1))
        block = jnp.concatenate(rows, axis=0)
        block_ref[...] = block
        turned = block.astype(F32).T.astype(BF16)

        @pl.loop(0, part // step)
        def _(i):
            cells = jnp.concatenate(
                [jnp.concatenate([ref[i * step + j] for ref in blocks], axis=0) for j in range(step)], axis=1
            )
            product = jnp.dot(turned, cells, preferred_element_type=F32).astype(BF16)
            for n, out in enumerate(outs):
                for j in range(step):
                    out[i * step + j] = product[n * both : (n + 1) * both, j * width : (j + 1) * width]

    term = shaped((part, both, width))
    outs = kernel_call(
        kernel,
        [term] * (sends + 1) + [shaped((sources * both, wide))],
        [mine, filter_mine, *arrived],
        (),
        2.0,
    )
    return outs[0], outs[1:-1], outs[-1]


def summed_halves(first, second):
    part, both, width = first[0].shape
    chans = both // 2

    def kernel(*refs):
        own, other = refs[-2:]
        for base, terms in ((0, refs[: len(first)]), (part, refs[len(first) : -2])):

            @pl.loop(0, part)
            def _(i):
                total = terms[0][i].astype(F32)
                for term in terms[1:]:
                    total = total + term[i].astype(F32)
                own[base + i] = total[:chans].astype(BF16)
                other[base + i] = total[chans:].astype(BF16)

    out = shaped((2 * part, chans, width))
    return kernel_call(kernel, [out, out], [*first, *second], (), 0.8)


def edge_rows(own, arrived, rows):
    half, chans, width = own.shape
    planes = half // rows

    def kernel(own, arrived, top, bottom):
        @pl.loop(0, planes)
        def _(p):
            for ref, base in ((own, 0), (arrived, planes)):
                top[base + p] = ref[p * rows]
                bottom[base + p] = ref[p * rows + rows - 1]

    edge = shaped((2 * planes, chans, width))
    return kernel_call(kernel, [edge, edge], [own, arrived], (), 0.5)


def joined(own, arrived):
    half, chans, width = own.shape
    part = half // 2

    def kernel(own, arrived, first, second):
        @pl.loop(0, part)
        def _(i):
            for out, base in ((first, 0), (second, part)):
                out[i, :chans] = own[base + i]
                out[i, chans:] = arrived[base + i]

    out = shaped((part, 2 * chans, width))
    return kernel_call(kernel, [out, out], [own, arrived], (), 0.8)


def out_terms(filter_block, hiddens, grads, count, over_mid):
    part, both, width = hiddens[0].shape
    chans = both // 2
    step = math.gcd(part, 4)
    rows_of, cols_of = len(grads), len(hiddens)

    def kernel(block, *refs):
        place = Place(count)
        hidden, grad = refs[:cols_of], refs[cols_of : cols_of + rows_of]
        outs = refs[cols_of + rows_of : cols_of + 2 * rows_of]
        pg_own, pg_other, ordered, lined = refs[cols_of + 2 * rows_of :]
        for j in range(part):
            span = slice(j * width, (j + 1) * width)
            for n, ref in enumerate(hidden):
                hi, mid, _ = place.block(0, n, 0) if over_mid else place.block(n, 0, 0)
                for q in range(2):
                    core = 1 - place.core if q else place.core
                    at = pl.multiple_of(((mid if over_mid else hi) * 2 + core) * chans, chans)
                    ordered[pl.ds(at, chans), span] = ref[j, q * chans : (q + 1) * chans]
            for n, ref in enumerate(grad):
                for q in range(2):
                    lined[q, n * chans : (n + 1) * chans, span] = ref[j, q * chans : (q + 1) * chans]

        weights = block[...]

        @pl.loop(0, part // step)
        def _(i):
            cells = jnp.concatenate(
                [jnp.concatenate([ref[i * step + j] for ref in hidden], axis=0) for j in range(step)], axis=1
            )
            product = jnp.dot(weights, cells, preferred_element_type=F32).astype(BF16)
            for n, out in enumerate(outs):
                for j in range(step):
                    out[i * step + j] = product[n * both : (n + 1) * both, j * width : (j + 1) * width]

        for q, out in enumerate((pg_own, pg_other)):
            out[...] = lax.dot_general(
                lined[q], ordered[...], (((1,), (1,)), ((), ())), preferred_element_type=F32
            )

    term = shaped((part, both, width))
    grad_term = shaped((rows_of * chans, cols_of * both), F32)
    outs = kernel_call(
        kernel,
        [term] * rows_of + [grad_term, grad_term],
        [filter_block, *hiddens, *grads],
        [pltpu.VMEM((cols_of * both, part * width), BF16), pltpu.VMEM((2, rows_of * chans, part * width), BF16)],
        3.0,
    )
    return outs[0], outs[1:rows_of], outs[-2], outs[-1]


def to_raw(own, arrived, count, planes, rows):
    half, chans, width = own.shape

    def kernel(own, arrived, raw, flat):
        core = Place(count).core

        @pl.loop(0, half)
        def _(i):
            for ref, which in ((own, core), (arrived, 1 - core)):
                start = pl.multiple_of((which * half + i) * chans, chans)
                flat[pl.ds(start, chans), :] = ref[i].astype(F32)

        cells_to_raw(flat, raw)

    return kernel_call(
        kernel,
        [shaped((chans, planes, rows, width))],
        [own, arrived],
        [pltpu.VMEM((planes * rows * chans, width), F32)],
        1.5,
    )[0]


def input_gradient(own, arrived, up, down, weights, count, planes, rows):
    half, chans, width = own.shape

    def kernel(own, arrived, up, down, weights, raw, padded, spread, flat):
        core = Place(count).core
        tap_planes(weights[...], spread, chans, width)

        def turned(ref):
            return lambda p: ref[(p + core * (planes // 2)) % planes]

        fill_rims(padded, turned(up), turned(down), planes, rows)

        @pl.loop(0, planes // 2)
        def _(p):
            for ref, which in ((own, core), (arrived, 1 - core)):
                plane = which * (planes // 2) + p
                for r in range(rows):
                    padded[(plane + 1) * (rows + 2) + r + 1] = ref[p * rows + r].astype(F32)

        def store(i, r, group, value):
            start = pl.multiple_of((i * rows + r) * chans + group.start, 16)
            flat[pl.ds(start, 16), :] = value

        depthwise(padded, spread, 0, planes, rows, store, True)
        cells_to_raw(flat, raw)

    return kernel_call(
        kernel,
        [shaped((chans, planes, rows, width))],
        [own, arrived, up, down, weights],
        [
            pltpu.VMEM(((planes + 2) * (rows + 2), chans, width), F32),
            pltpu.VMEM((27, chans, width), F32),
            pltpu.VMEM((planes * rows * chans, width), F32),
        ],
        6.0,
    )[0]


def tap_gradient(cells, up, down, own, arrived, count, planes, rows):
    _, chans, width = cells.shape

    def kernel(cells, up, down, own, arrived, out, padded, back, sums):
        core = Place(count).core
        fill_rims(padded, lambda p: up[p], lambda p: down[p], planes, rows)

        @pl.loop(0, planes)
        def _(p):
            for r in range(rows):
                padded[(p + 1) * (rows + 2) + r + 1] = cells[p * rows + r].astype(F32)

        @pl.loop(0, planes // 2)
        def _(p):
            for ref, which in ((own, core), (arrived, 1 - core)):
                plane = which * (planes // 2) + p
                for r in range(rows):
                    back[plane * rows + r] = ref[p * rows + r].astype(F32)

        lane = lax.broadcasted_iota(jnp.int32, (8, width), 1)

        @pl.loop(0, chans // 8)
        def _(g):
            group = pl.ds(pl.multiple_of(g * 8, 8), 8)

            def step(p, totals):
                totals = list(totals)
                for r in range(rows):
                    here = back[p * rows + r, group]
                    later = jnp.where(lane == width - 1, 0.0, pltpu.roll(here, width - 1, 1))
                    earlier = jnp.where(lane == 0, 0.0, pltpu.roll(here, 1, 1))
                    for a in range(3):
                        for b in range(3):
                            image = padded[(p + a) * (rows + 2) + r + b, group]
                            for e, moved in enumerate((later, here, earlier)):
                                tap = 9 * a + 3 * b + e
                                totals[tap] = totals[tap] + image * moved
                return tuple(totals)

            totals = lax.fori_loop(0, planes, step, tuple(jnp.zeros((8, width), F32) for _ in range(27)))
            for tap in range(27):
                sums[tap, group] = totals[tap]

        out[...] = lax.dot_general(
            jnp.ones((8, width), F32),
            sums[...].reshape(27 * chans, width),
            (((1,), (1,)), ((), ())),
            precision=lax.Precision.HIGHEST,
            preferred_element_type=F32,
        )

    return kernel_call(
        kernel,
        [shaped((8, 27 * chans), F32)],
        [cells, up, down, own, arrived],
        [
            pltpu.VMEM(((planes + 2) * (rows + 2), chans, width), F32),
            pltpu.VMEM((planes * rows, chans, width), F32),
            pltpu.VMEM((27, chans, width), F32),
        ],
        6.0,
    )[0]


def body(images, depth_filter, point_filter, grad_out):
    chans, planes, rows, width = images.shape
    count, slabs = lax.axis_size("chan"), lax.axis_size("space")
    his, mids = count // 4, 2
    place = Place(count)
    grad_scale = 1.0 / math.sqrt(planes * rows * width * slabs)

    def moved(value, target):
        pairs = []
        for i in range(count):
            hi, mid, core = target(i // 2 // mids, i // 2 % mids, i % 2)
            pairs.append((i, (hi % his * mids + mid % mids) * 2 + core))
        return lax.ppermute(value, "chan", pairs)

    def to_core(value):
        return moved(value, lambda hi, mid, core: (hi, mid, 1 - core))

    def along_hi(value, by):
        return moved(value, lambda hi, mid, core: (hi + by, mid, core))

    def along_mid(value, by):
        return moved(value, lambda hi, mid, core: (hi, mid + by, core))

    def halo(top, bottom):
        up = lax.ppermute(bottom, "space", [(i, i + 1) for i in range(slabs - 1)])
        down = lax.ppermute(top, "space", [(i + 1, i) for i in range(slabs - 1)])
        return up, down

    filter_arrived = to_core(point_filter)
    grad_own, grad_other = relayout_grad(grad_out, count)
    grad_arrived = to_core(grad_other)
    to_hi, to_mid, filter_hi, filter_mid = pack_grad(grad_own, grad_arrived, point_filter, filter_arrived, count)
    grads_hi = [along_hi(value, s) for s, value in enumerate(to_hi, 1)]
    grads_mid = [along_mid(value, t) for t, value in enumerate(to_mid, 1)]

    cells, top, bottom = relayout_images(images)
    image_up, image_down = halo(top, bottom)
    hidden_own, hidden_other = hidden_halves(cells, image_up, image_down, depth_filter, count, planes, rows)
    hidden_first, hidden_second = joined(hidden_own, to_core(hidden_other))
    hiddens_mid = [hidden_first] + [along_mid(hidden_first, t) for t in range(1, mids)]
    hiddens_hi = [hidden_second] + [along_hi(hidden_second, s) for s in range(1, his)]

    keep_first, send_first, block_first = back_terms(to_hi[0], grads_hi, filter_hi, mids - 1)
    keep_second, send_second, block_second = back_terms(to_mid[0], grads_mid, filter_mid, his - 1)
    back_first = [keep_first] + [along_mid(value, -t) for t, value in enumerate(send_first, 1)]
    back_second = [keep_second] + [along_hi(value, -s) for s, value in enumerate(send_second, 1)]
    back_own, back_other = summed_halves(back_first, back_second)
    back_arrived = to_core(back_other)
    back_up, back_down = halo(*edge_rows(back_own, back_arrived, rows))

    keep_first, send_first, pg_first, pg_first_other = out_terms(
        block_first, hiddens_mid, [to_hi[0], *grads_hi], count, True
    )
    keep_second, send_second, pg_second, pg_second_other = out_terms(
        block_second, hiddens_hi, [to_mid[0], *grads_mid], count, False
    )
    out_first = [keep_first] + [along_hi(value, -s) for s, value in enumerate(send_first, 1)]
    out_second = [keep_second] + [along_mid(value, -t) for t, value in enumerate(send_second, 1)]
    out_own, out_other = summed_halves(out_first, out_second)
    block_out = to_raw(out_own, to_core(out_other), count, planes, rows)

    pg_first = pg_first + to_core(pg_first_other)
    pg_second = pg_second + to_core(pg_second_other)
    pg = jnp.zeros((chans, his, mids, 2 * chans), F32)
    for s in range(his):
        piece = pg_first[s * chans : (s + 1) * chans]
        if s:
            piece = along_hi(piece, -s)
        piece = piece.reshape(chans, 1, mids, 2 * chans)
        pg = lax.dynamic_update_slice_in_dim(pg, piece, (place.hi + s) % his, 1)
    pg_more = jnp.zeros((chans, his, mids, 2 * chans), F32)
    for t in range(mids):
        piece = pg_second[t * chans : (t + 1) * chans]
        if t:
            piece = along_mid(piece, -t)
        piece = piece.reshape(chans, his, 1, 2 * chans)
        pg_more = lax.dynamic_update_slice_in_dim(pg_more, piece, (place.mid + t) % mids, 2)
    pg = (pg + pg_more).reshape(chans, -1)

    taps = tap_gradient(cells, image_up, image_down, back_own, back_arrived, count, planes, rows)[0]
    input_grad = input_gradient(back_own, back_arrived, back_up, back_down, depth_filter, count, planes, rows)

    slab = lax.axis_index("space")
    apart = slabs // 2
    while apart:
        low, high = jnp.split(pg, 2, axis=1)
        upper = (slab & apart) != 0
        pairs = [(i, i ^ apart) for i in range(slabs)]
        pg = jnp.where(upper, high, low) + lax.ppermute(jnp.where(upper, low, high), "space", pairs)
        taps = taps + lax.ppermute(taps, "space", pairs)
        apart //= 2
    return block_out, pg * grad_scale, input_grad, taps.reshape(27, chans) * grad_scale


def solution(mesh):
    placed = (
        P("chan", None, "space", None),
        P(None, "chan"),
        P("chan", None),
        P("chan", None, "space", None),
    )
    return jax.shard_map(
        body,
        mesh=mesh,
        in_specs=placed,
        out_specs=(
            P("chan", None, "space", None),
            P("chan", "space"),
            P("chan", None, "space", None),
            P(None, "chan"),
        ),
        check_vma=False,
    )
```

time: 187 us -> 131 us (0.70)
  Pallas kernels: 0 us -> 47.8 us
  other arithmetic: 42 us -> 0.77 us
  blocking collectives: 33.2 us -> 0 us
  local copies, waits for them, and re-layouts: 41.7 us -> 9.93 us
  starting transfers between devices: 12 us -> 32.1 us
  matrix products: 16.7 us -> 0 us
  between operations: 14.7 us -> 1.11 us
  waiting for transfers between devices: 25.5 us -> 38.6 us
    pallas_call x0 -> x15, Pallas kernels: none -> 47.8 us  [kernel_call(): pl.pallas_call(kernel, out_shape=outs, in_specs=[IN_VMEM] * len(args), ou...]
    ppermute x4 -> x25, waiting for transfers between devices: 8.08 us -> 38.6 us  [the longest x17 30.2 us: moved(): return lax.ppermute(value, 'chan', pairs)]
    all_gather x2 -> x0, local copies, waits for them, and re-layouts: 26.4 us -> none  [the longest x1 14 us: body(): grad_piece = lax.all_gather(grad_out, 'chan', axis=0, tiled=True)]
    ppermute x4 -> x25, starting transfers between devices: 11.8 us -> 32.1 us  [the longest x17 13.8 us: moved(): return lax.ppermute(value, 'chan', pairs)]
    convert_element_type x2 -> x0, other arithmetic: 19.6 us -> none  [the longest x1 10 us: body(): depth_backward(padded_back, depth_filter, planes, row_count, col_count)]
    psum x1 -> x0, blocking collectives: 19.4 us -> none  [body(): depth_grad = lax.psum(local_taps, 'space') * grad_scale]
    all_gather x2 -> x0, waiting for transfers between devices: 17.4 us -> none  [the longest x1 17.4 us: body(): grad_piece = lax.all_gather(grad_out, 'chan', axis=0, tiled=True)]
    dot_general x3 -> x0, matrix products: 16.7 us -> none  [the longest x1 7.21 us: body(): lax.dot_general(columns, grad_rows, (((0,), (0,)), ((), ())), preferred_e...]
  transfers between devices with their start and end apart: 7 -> 25, of which waited for: 3 -> 8; matrix products, arithmetic and copies ran while one was open for 52% -> 4% of each run, Pallas kernels for 0% -> 28%
where the time goes in v1:
time: 131 us; the launch traced here: 130 us
  Pallas kernels  47.8 us (36%)
  waiting for transfers between devices  38.6 us (29%)
  starting transfers between devices  32.1 us (25%)
  local copies, waits for them, and re-layouts  9.93 us (8%)
    pallas_call x15, Pallas kernels, kernel_call(): pl.pallas_call(kernel, out_shape=outs, in_specs=[IN_VMEM] * len(args), ou...  47.8 us
    ppermute x17, waiting for transfers between devices, moved(): return lax.ppermute(value, 'chan', pairs)  30.2 us
    ppermute x17, starting transfers between devices, moved(): return lax.ppermute(value, 'chan', pairs)  13.8 us
    ppermute x2, starting transfers between devices, halo(): up = lax.ppermute(bottom, 'space', [(i, i + 1) for i in range(slabs - 1)])  7.33 us
    ppermute x2, waiting for transfers between devices, halo(): down = lax.ppermute(top, 'space', [(i + 1, i) for i in range(slabs - 1)])  6.03 us
    unnamed x40, local copies, waits for them, and re-layouts  6.01 us
    ppermute x2, starting transfers between devices, body(): taps = taps + lax.ppermute(taps, 'space', pairs)  4.19 us
    ppermute x2, starting transfers between devices, body(): lax.ppermute(jnp.where(upper, low, high), 'space', pairs)  4.07 us
  transfers between devices with their start and end apart: 25, of which 8 were waited for; matrix products, arithmetic and copies ran while one was open for 4% of the time, Pallas kernels for 28%

profile of v1, /device:TPU:0, one launch (start us, length us, event | category | flops | bytes accessed | tf_op | source)
XLA Modules:
  0.0 130.4 jit_solution(15196546499735540966)
XLA Ops:
  1.9 2.3 %shard_map.78 = (bf16[64,64,128]{2,1,0:T(8,128)(2,1)S(1)}, bf16[16,64,128]{2,1,0:T(8,128)(2,1)S(1)}, bf16[16,64,128]{2,1,0:T(8,128)(2,1)S(1)}) custom-call(bf16[64,16,4,128]{3,2,1,0:T(4,128)(2,1)S(1)} %copy-done), custom_call_target="tpu_custom_call" | custom-call | flops 1500000000 | bytes 2621440 | tf_op jit(solution)/shard_map/pallas_call | solution.py:35
  4.2 4.9 %collective-permute-start.3 = (bf16[16,64,128]{2,1,0:T(8,128)(2,1)S(1)}, bf16[16,64,128]{2,1,0:T(8,128)(2,1)S(1)}, u32[]{:S(2)}, u32[]{:S(2)}) collective-permute-start(bf16[16,64,128]{2,1,0:T(8,128)(2,1)S(1)} %get-tuple-element.43), channel_id=1, source_target_pairs={{0,8},{8,16},{16,24},{1,9},{9,17},{17,25},{2,10},{10,18},{18,26},{... | collective-permute-start | bytes 786440 | tf_op jit(solution)/shard_map/ppermute | solution.py:541
  10.6 2.4 %shard_map.75 = (bf16[32,64,128]{2,1,0:T(8,128)(2,1)S(1)}, bf16[32,64,128]{2,1,0:T(8,128)(2,1)S(1)}) custom-call(bf16[64,16,4,128]{3,2,1,0:T(4,128)(2,1)S(1)} %copy-done.1), custom_call_target="tpu_custom_call" | custom-call | flops 1500000000 | bytes 2097152 | tf_op jit(solution)/shard_map/pallas_call | solution.py:35
  14.7 4.3 %collective-permute-done.4.down = bf16[16,64,128]{2,1,0:T(8,128)(2,1)S(1)} collective-permute-done((bf16[16,64,128]{2,1,0:T(8,128)(2,1)S(1)}, bf16[16,64,128]{2,1,0:T(8,128)(2,1)S(1)}, u32[]{:S(2)}, u32[]{:S(2)}) %collective-permute-start.4) | collective-permute-done | bytes 262176 | tf_op jit(solution)/shard_map/ppermute | solution.py:542
  19.0 5.1 %shard_map.79 = (bf16[32,64,128]{2,1,0:T(8,128)(2,1)S(1)}, bf16[32,64,128]{2,1,0:T(8,128)(2,1)S(1)}) custom-call(bf16[64,64,128]{2,1,0:T(8,128)(2,1)S(1)} %get-tuple-element.42.cells, bf16[16,64,128]{2,1,0:T(8,128)(2,1)S(1)} %collective-permute-done.3.up, bf16[16,64,128]{2,1,0:T(8,128)(2,1)S(1)} %collective-permute-done.4.down, f32[27,64]{1,0:T(8,128)S(1)} %copy-done.7), custom_call_target="tpu_custom_call" | custom-call | flops 5000000000 | bytes 2628352 | tf_op jit(solution)/shard_map/pallas_call | solution.py:35
  24.8 1.6 %collective-permute-start.8 = (bf16[18,128,128]{2,1,0:T(8,128)(2,1)S(1)}, bf16[18,128,128]{2,1,0:T(8,128)(2,1)S(1)}, u32[]{:S(2)}, u32[]{:S(2)}) collective-permute-start(bf16[18,128,128]{2,1,0:T(8,128)(2,1)S(1)} %get-tuple-element.50.mine.refs_2_), channel_id=1, source_target_pairs={{0,2},{1,3},{2,0},{3,1},{4,6},{5,7},{6,4},{7,5},{8,10},{9,11},{10,... | collective-permute-start | bytes 1769480 | tf_op jit(solution)/shard_map/ppermute | solution.py:529
  29.3 11.7 %collective-permute-done.8.refs_0_.refs_3_ = bf16[18,128,128]{2,1,0:T(8,128)(2,1)S(1)} collective-permute-done((bf16[18,128,128]{2,1,0:T(8,128)(2,1)S(1)}, bf16[18,128,128]{2,1,0:T(8,128)(2,1)S(1)}, u32[]{:S(2)}, u32[]{:S(2)}) %collective-permute-start.8) | collective-permute-done | bytes 589856 | tf_op jit(solution)/shard_map/ppermute | solution.py:529
  41.0 1.8 %shard_map.82 = (bf16[16,128,128]{2,1,0:T(8,128)(2,1)S(1)}, bf16[16,128,128]{2,1,0:T(8,128)(2,1)}, bf16[256,256]{1,0:T(8,128)(2,1)S(1)}) custom-call(bf16[18,128,128]{2,1,0:T(8,128)(2,1)S(1)} %get-tuple-element.50.mine.refs_2_, bf16[2,128,128]{2,1,0:T(8,128)(2,1)S(1)} %get-tuple-element.51.filter_mine, ...), custom_call_target="tpu_custom_call" | custom-call | flops 2000000000 | bytes 2424832 | tf_op jit(solution)/shard_map/pallas_call | solution.py:35
  44.4 1.8 %shard_map.77 = (bf16[16,128,128]{2,1,0:T(8,128)(2,1)S(1)}, bf16[16,128,128]{2,1,0:T(8,128)(2,1)}, bf16[256,256]{1,0:T(8,128)(2,1)S(1)}) custom-call(bf16[18,128,128]{2,1,0:T(8,128)(2,1)S(1)} %get-tuple-element.39.mine.refs_2_, bf16[2,128,128]{2,1,0:T(8,128)(2,1)S(1)} %get-tuple-element.40.filter_mine, ...), custom_call_target="tpu_custom_call" | custom-call | flops 2000000000 | bytes 2424832 | tf_op jit(solution)/shard_map/pallas_call | solution.py:35
  48.5 5.4 %collective-permute-done.9.refs_1_ = bf16[16,128,128]{2,1,0:T(8,128)(2,1)} collective-permute-done((bf16[16,128,128]{2,1,0:T(8,128)(2,1)S(1)}, bf16[16,128,128]{2,1,0:T(8,128)(2,1)}, u32[]{:S(2)}, u32[]{:S(2)}) %collective-permute-start.9) | collective-permute-done | bytes 524320 | tf_op jit(solution)/shard_map/ppermute | solution.py:529
  53.9 3.4 %shard_map.83 = (bf16[16,128,128]{2,1,0:T(8,128)(2,1)S(1)}, bf16[16,128,128]{2,1,0:T(8,128)(2,1)}, f32[128,256]{1,0:T(8,128)S(1)}, f32[128,256]{1,0:T(8,128)S(1)}) custom-call(bf16[256,256]{1,0:T(8,128)(2,1)S(1)} %get-tuple-element.52.block, bf16[16,128,128]{2,1,0:T(8,128)(2,1)S(1)} %get-tuple-element.53.refs_0_, ...), custom_call_target="tpu_custom_call" | custom-call | flops 3000000000 | bytes 3670016 | tf_op jit(solution)/shard_map/pallas_call | solution.py:35
  58.0 2.3 %shard_map.81 = (bf16[16,128,128]{2,1,0:T(8,128)(2,1)S(1)}, bf16[16,128,128]{2,1,0:T(8,128)(2,1)S(1)}, f32[128,256]{1,0:T(8,128)S(1)}, f32[128,256]{1,0:T(8,128)S(1)}) custom-call(bf16[256,256]{1,0:T(8,128)(2,1)S(1)} %get-tuple-element.41.block, bf16[16,128,128]{2,1,0:T(8,128)(2,1)S(1)} %get-tuple-element.47.refs_0_, ...), custom_call_target="tpu_custom_call" | custom-call | flops 3000000000 | bytes 3670016 | tf_op jit(solution)/shard_map/pallas_call | solution.py:35
  63.2 1.6 %collective-permute-start.13 = (f32[64,256]{1,0:T(8,128)S(1)}, f32[64,256]{1,0:T(8,128)S(1)}, u32[]{:S(2)}, u32[]{:S(2)}) collective-permute-start(f32[64,256]{1,0:T(8,128)S(1)} %get-tuple-element.72), channel_id=1, source_target_pairs={{0,4},{1,5},{2,6},{3,7},{4,0},{5,1},{6,2},{7,3},{8,12},{9,13},{10,... | collective-permute-start | bytes 196616 | tf_op jit(solution)/shard_map/ppermute | solution.py:529
  66.3 10.2 %collective-permute-done.15 = f32[64,256]{1,0:T(8,128)S(1)} collective-permute-done((f32[64,256]{1,0:T(8,128)S(1)}, f32[64,256]{1,0:T(8,128)S(1)}, u32[]{:S(2)}, u32[]{:S(2)}) %collective-permute-start.15) | collective-permute-done | bytes 65568 | tf_op jit(solution)/shard_map/ppermute | solution.py:529
  79.7 2.7 %collective-permute-start.16 = (f32[64,256]{1,0:T(8,128)S(1)}, f32[64,256]{1,0:T(8,128)S(1)}, u32[]{:S(2)}, u32[]{:S(2)}) collective-permute-start(f32[64,256]{1,0:T(8,128)S(1)} %slice_select_fusion), channel_id=1, source_target_pairs={{0,16},{8,24},{16,0},{24,8},{1,17},{9,25},{17,1},{25,9},{2,18},{10... | collective-permute-start | bytes 196616 | tf_op jit(solution)/shard_map/ppermute | solution.py:605
  83.4 1.7 %shard_map.86 = (bf16[32,64,128]{2,1,0:T(8,128)(2,1)S(1)}, bf16[32,64,128]{2,1,0:T(8,128)(2,1)S(1)}) custom-call(bf16[16,128,128]{2,1,0:T(8,128)(2,1)S(1)} %copy-done.15, bf16[16,128,128]{2,1,0:T(8,128)(2,1)} %collective-permute-done.18.refs_1_, bf16[16,128,128]{2,1,0:T(8,128)(2,1)S(1)} %copy-done.11, bf16[16,128,128]{2,1,0:T(8,128)(2,1)} %collective-permute-done.19.refs_3_), custom_call_target="tpu_custom_call" | custom-call | flops 800000000 | bytes 3145728 | tf_op jit(solution)/shard_map/pallas_call | solution.py:35
  86.6 2.9 %collective-permute-done.7.refs_1_ = bf16[16,128,128]{2,1,0:T(8,128)(2,1)S(1)} collective-permute-done((bf16[16,128,128]{2,1,0:T(8,128)(2,1)S(1)}, bf16[16,128,128]{2,1,0:T(8,128)(2,1)S(1)}, u32[]{:S(2)}, u32[]{:S(2)}) %collective-permute-start.7) | collective-permute-done | bytes 524320 | tf_op jit(solution)/shard_map/ppermute | solution.py:529
  91.0 13.3 %shard_map.89 = f32[8,1728]{1,0:T(8,128)S(1)} custom-call(bf16[64,64,128]{2,1,0:T(8,128)(2,1)S(1)} %copy-done.19, bf16[16,64,128]{2,1,0:T(8,128)(2,1)S(1)} %copy-done.3, bf16[16,64,128]{2,1,0:T(8,128)(2,1)S(1)} %copy-done.5, bf16[32,64,128]{2,1,0:T(8,128)(2,1)S(1)} %get-tuple-element.66.own, bf16[32,64,128]{2,1,0:T(8,128)(2,1)S(1)} %collective-permute-done.20.arrived), custom_call_target="tpu_custom_call" | custom-call | flops 6000000000 | bytes 2676736 | tf_op jit(solution)/shard_map/pallas_call | solution.py:35
  104.4 2.6 %collective-permute-start.23 = (f32[1728]{0:T(1024)S(1)}, f32[1728]{0:T(1024)S(1)}, u32[]{:S(2)}, u32[]{:S(2)}) collective-permute-start(f32[1728]{0:T(1024)S(1)} %slice_reduce_fusion), channel_id=1, source_target_pairs={{0,16},{8,24},{16,0},{24,8},{1,17},{9,25},{17,1},{25,9},{2,18},{10... | collective-permute-start | bytes 20744 | tf_op jit(solution)/shard_map/ppermute | solution.py:606
  109.0 1.6 %collective-permute-start.24 = (f32[1728]{0:T(1024)S(1)}, f32[1728]{0:T(1024)S(1)}, u32[]{:S(2)}, u32[]{:S(2)}) collective-permute-start(f32[1728]{0:T(1024)S(1)} %add.73), channel_id=1, source_target_pairs={{0,8},{8,0},{16,24},{24,16},{1,9},{9,1},{17,25},{25,17},{2,10},{10... | collective-permute-start | bytes 20744 | tf_op jit(solution)/shard_map/ppermute | solution.py:606
  110.6 2.4 %collective-permute-start.21 = (bf16[16,64,128]{2,1,0:T(8,128)(2,1)S(1)}, bf16[16,64,128]{2,1,0:T(8,128)(2,1)S(1)}, u32[]{:S(2)}, u32[]{:S(2)}) collective-permute-start(bf16[16,64,128]{2,1,0:T(8,128)(2,1)S(1)} %get-tuple-element.68), channel_id=1, source_target_pairs={{0,8},{8,16},{16,24},{1,9},{9,17},{17,25},{2,10},{10,18},{18,26},{... | collective-permute-start | bytes 786440 | tf_op jit(solution)/shard_map/ppermute | solution.py:541
  116.1 3.8 %shard_map.85 = bf16[64,16,4,128]{3,2,1,0:T(4,128)(2,1)} custom-call(bf16[32,64,128]{2,1,0:T(8,128)(2,1)S(1)} %copy-done.17, bf16[32,64,128]{2,1,0:T(8,128)(2,1)S(1)} %collective-permute-done.11.arrived), custom_call_target="tpu_custom_call" | custom-call | flops 1500000000 | bytes 2097152 | tf_op jit(solution)/shard_map/pallas_call | solution.py:35
  119.9 1.8 %collective-permute-done.22.down = bf16[16,64,128]{2,1,0:T(8,128)(2,1)S(1)} collective-permute-done((bf16[16,64,128]{2,1,0:T(8,128)(2,1)S(1)}, bf16[16,64,128]{2,1,0:T(8,128)(2,1)S(1)}, u32[]{:S(2)}, u32[]{:S(2)}) %collective-permute-start.22) | collective-permute-done | bytes 262176 | tf_op jit(solution)/shard_map/ppermute | solution.py:542
  121.7 8.7 %shard_map.88 = bf16[64,16,4,128]{3,2,1,0:T(4,128)(2,1)} custom-call(bf16[32,64,128]{2,1,0:T(8,128)(2,1)S(1)} %get-tuple-element.66.own, bf16[32,64,128]{2,1,0:T(8,128)(2,1)S(1)} %collective-permute-done.20.arrived, bf16[16,64,128]{2,1,0:T(8,128)(2,1)S(1)} %collective-permute-done.21.up, bf16[16,64,128]{2,1,0:T(8,128)(2,1)S(1)} %collective-permute-done.22.down, ...), custom_call_target="tpu_custom_call" | custom-call | flops 6000000000 | bytes 2628352 | tf_op jit(solution)/shard_map/pallas_call | solution.py:35
  (105 shorter events, 29.1 us)
Async XLA Ops:
  4.2 10.5 %collective-permute-start.3 = (bf16[16,64,128]{2,1,0:T(8,128)(2,1)S(1)}, bf16[16,64,128]{2,1,0:T(8,128)(2,1)S(1)}, u32[]{:S(2)}, u32[]{:S(2)}) collective-permute-start(bf16[16,64,128]{2,1,0:T(8,128)(2,1)S(1)} %get-tuple-element.43), channel_id=1, source_target_pairs={{0,8},{8,16},{16,24},{1,9},{9,17},{17,25},{2,10},{10,18},{18,26},{... | collective-permute-start | bytes 786440 | tf_op jit(solution)/shard_map/ppermute | solution.py:541
  9.2 9.8 %collective-permute-start.4 = (bf16[16,64,128]{2,1,0:T(8,128)(2,1)S(1)}, bf16[16,64,128]{2,1,0:T(8,128)(2,1)S(1)}, u32[]{:S(2)}, u32[]{:S(2)}) collective-permute-start(bf16[16,64,128]{2,1,0:T(8,128)(2,1)S(1)} %get-tuple-element.44), channel_id=1, source_target_pairs={{8,0},{16,8},{24,16},{9,1},{17,9},{25,17},{10,2},{18,10},{26,18},{... | collective-permute-start | bytes 786440 | tf_op jit(solution)/shard_map/ppermute | solution.py:542
  13.1 11.1 %collective-permute-start = (bf16[32,64,128]{2,1,0:T(8,128)(2,1)S(1)}, bf16[32,64,128]{2,1,0:T(8,128)(2,1)S(1)}, u32[]{:S(2)}, u32[]{:S(2)}) collective-permute-start(bf16[32,64,128]{2,1,0:T(8,128)(2,1)S(1)} %get-tuple-element.38), channel_id=1, source_target_pairs={{0,1},{1,0},{2,3},{3,2},{4,5},{5,4},{6,7},{7,6},{8,9},{9,8},{10,11... | collective-permute-start | bytes 1572872 | tf_op jit(solution)/shard_map/ppermute | solution.py:529
  13.2 11.0 %collective-permute-start.1 = (bf16[64,512]{1,0:T(8,128)(2,1)S(1)}, bf16[64,512]{1,0:T(8,128)(2,1)S(1)}, u32[]{:S(2)}, u32[]{:S(2)}) collective-permute-start(bf16[64,512]{1,0:T(8,128)(2,1)S(1)} %copy-done.6), channel_id=1, source_target_pairs={{0,1},{1,0},{2,3},{3,2},{4,5},{5,4},{6,7},{7,6},{8,9},{9,8},{10,11... | collective-permute-start | bytes 196616 | tf_op jit(solution)/shard_map/ppermute | solution.py:529
  24.1 3.8 %collective-permute-start.5 = (bf16[32,64,128]{2,1,0:T(8,128)(2,1)S(1)}, bf16[32,64,128]{2,1,0:T(8,128)(2,1)S(1)}, u32[]{:S(2)}, u32[]{:S(2)}) collective-permute-start(bf16[32,64,128]{2,1,0:T(8,128)(2,1)S(1)} %get-tuple-element.46), channel_id=1, source_target_pairs={{0,1},{1,0},{2,3},{3,2},{4,5},{5,4},{6,7},{7,6},{8,9},{9,8},{10,11... | collective-permute-start | bytes 1572872 | tf_op jit(solution)/shard_map/ppermute | solution.py:529
  24.8 16.2 %collective-permute-start.8 = (bf16[18,128,128]{2,1,0:T(8,128)(2,1)S(1)}, bf16[18,128,128]{2,1,0:T(8,128)(2,1)S(1)}, u32[]{:S(2)}, u32[]{:S(2)}) collective-permute-start(bf16[18,128,128]{2,1,0:T(8,128)(2,1)S(1)} %get-tuple-element.50.mine.refs_2_), channel_id=1, source_target_pairs={{0,2},{1,3},{2,0},{3,1},{4,6},{5,7},{6,4},{7,5},{8,10},{9,11},{10,... | collective-permute-start | bytes 1769480 | tf_op jit(solution)/shard_map/ppermute | solution.py:529
  26.4 18.0 %collective-permute-start.2 = (bf16[18,128,128]{2,1,0:T(8,128)(2,1)S(1)}, bf16[18,128,128]{2,1,0:T(8,128)(2,1)S(1)}, u32[]{:S(2)}, u32[]{:S(2)}) collective-permute-start(bf16[18,128,128]{2,1,0:T(8,128)(2,1)S(1)} %get-tuple-element.39.mine.refs_2_), channel_id=1, source_target_pairs={{0,4},{1,5},{2,6},{3,7},{4,0},{5,1},{6,2},{7,3},{8,12},{9,13},{10,... | collective-permute-start | bytes 1769480 | tf_op jit(solution)/shard_map/ppermute | solution.py:529
  28.0 25.9 %collective-permute-start.9 = (bf16[16,128,128]{2,1,0:T(8,128)(2,1)S(1)}, bf16[16,128,128]{2,1,0:T(8,128)(2,1)}, u32[]{:S(2)}, u32[]{:S(2)}) collective-permute-start(bf16[16,128,128]{2,1,0:T(8,128)(2,1)S(1)} %get-tuple-element.53.refs_0_), channel_id=1, source_target_pairs={{0,4},{1,5},{2,6},{3,7},{4,0},{5,1},{6,2},{7,3},{8,12},{9,13},{10,... | collective-permute-start | bytes 1572872 | tf_op jit(solution)/shard_map/ppermute | solution.py:529
  28.6 29.4 %collective-permute-start.6 = (bf16[16,128,128]{2,1,0:T(8,128)(2,1)S(1)}, bf16[16,128,128]{2,1,0:T(8,128)(2,1)S(1)}, u32[]{:S(2)}, u32[]{:S(2)}) collective-permute-start(bf16[16,128,128]{2,1,0:T(8,128)(2,1)S(1)} %get-tuple-element.47.refs_0_), channel_id=1, source_target_pairs={{0,2},{1,3},{2,0},{3,1},{4,6},{5,7},{6,4},{7,5},{8,10},{9,11},{10,... | collective-permute-start | bytes 1572872 | tf_op jit(solution)/shard_map/ppermute | solution.py:529
  42.8 39.6 %collective-permute-start.19 = (bf16[16,128,128]{2,1,0:T(8,128)(2,1)}, bf16[16,128,128]{2,1,0:T(8,128)(2,1)}, u32[]{:S(2)}, u32[]{:S(2)}) collective-permute-start(bf16[16,128,128]{2,1,0:T(8,128)(2,1)} %get-tuple-element.65), channel_id=1, source_target_pairs={{0,4},{1,5},{2,6},{3,7},{4,0},{5,1},{6,2},{7,3},{8,12},{9,13},{10,... | collective-permute-start | bytes 1572872 | tf_op jit(solution)/shard_map/ppermute | solution.py:529
  47.0 35.4 %collective-permute-start.18 = (bf16[16,128,128]{2,1,0:T(8,128)(2,1)}, bf16[16,128,128]{2,1,0:T(8,128)(2,1)}, u32[]{:S(2)}, u32[]{:S(2)}) collective-permute-start(bf16[16,128,128]{2,1,0:T(8,128)(2,1)} %get-tuple-element.63), channel_id=1, source_target_pairs={{0,2},{1,3},{2,0},{3,1},{4,6},{5,7},{6,4},{7,5},{8,10},{9,11},{10,... | collective-permute-start | bytes 1572872 | tf_op jit(solution)/shard_map/ppermute | solution.py:529
  58.0 3.5 %collective-permute-start.14 = (f32[128,256]{1,0:T(8,128)S(1)}, f32[128,256]{1,0:T(8,128)S(1)}, u32[]{:S(2)}, u32[]{:S(2)}) collective-permute-start(f32[128,256]{1,0:T(8,128)S(1)} %get-tuple-element.61), channel_id=1, source_target_pairs={{0,1},{1,0},{2,3},{3,2},{4,5},{5,4},{6,7},{7,6},{8,9},{9,8},{10,11... | collective-permute-start | bytes 393224 | tf_op jit(solution)/shard_map/ppermute | solution.py:529
  60.9 25.7 %collective-permute-start.10 = (bf16[16,128,128]{2,1,0:T(8,128)(2,1)}, bf16[16,128,128]{2,1,0:T(8,128)(2,1)S(1)}, u32[]{:S(2)}, u32[]{:S(2)}) collective-permute-start(bf16[16,128,128]{2,1,0:T(8,128)(2,1)} %get-tuple-element.55), channel_id=1, source_target_pairs={{0,2},{1,3},{2,0},{3,1},{4,6},{5,7},{6,4},{7,5},{8,10},{9,11},{10,... | collective-permute-start | bytes 1572872 | tf_op jit(solution)/shard_map/ppermute | solution.py:529
  61.5 14.9 %collective-permute-start.15 = (f32[64,256]{1,0:T(8,128)S(1)}, f32[64,256]{1,0:T(8,128)S(1)}, u32[]{:S(2)}, u32[]{:S(2)}) collective-permute-start(f32[64,256]{1,0:T(8,128)S(1)} %get-tuple-element.70), channel_id=1, source_target_pairs={{0,2},{1,3},{2,0},{3,1},{4,6},{5,7},{6,4},{7,5},{8,10},{9,11},{10,... | collective-permute-start | bytes 196616 | tf_op jit(solution)/shard_map/ppermute | solution.py:529
  63.2 16.2 %collective-permute-start.13 = (f32[64,256]{1,0:T(8,128)S(1)}, f32[64,256]{1,0:T(8,128)S(1)}, u32[]{:S(2)}, u32[]{:S(2)}) collective-permute-start(f32[64,256]{1,0:T(8,128)S(1)} %get-tuple-element.72), channel_id=1, source_target_pairs={{0,4},{1,5},{2,6},{3,7},{4,0},{5,1},{6,2},{7,3},{8,12},{9,13},{10,... | collective-permute-start | bytes 196616 | tf_op jit(solution)/shard_map/ppermute | solution.py:529
  76.5 13.1 %collective-permute-start.7 = (bf16[16,128,128]{2,1,0:T(8,128)(2,1)S(1)}, bf16[16,128,128]{2,1,0:T(8,128)(2,1)S(1)}, u32[]{:S(2)}, u32[]{:S(2)}) collective-permute-start(bf16[16,128,128]{2,1,0:T(8,128)(2,1)S(1)} %get-tuple-element.49), channel_id=1, source_target_pairs={{0,4},{1,5},{2,6},{3,7},{4,0},{5,1},{6,2},{7,3},{8,12},{9,13},{10,... | collective-permute-start | bytes 1572872 | tf_op jit(solution)/shard_map/ppermute | solution.py:529
  79.7 5.5 %collective-permute-start.16 = (f32[64,256]{1,0:T(8,128)S(1)}, f32[64,256]{1,0:T(8,128)S(1)}, u32[]{:S(2)}, u32[]{:S(2)}) collective-permute-start(f32[64,256]{1,0:T(8,128)S(1)} %slice_select_fusion), channel_id=1, source_target_pairs={{0,16},{8,24},{16,0},{24,8},{1,17},{9,25},{17,1},{25,9},{2,18},{10... | collective-permute-start | bytes 196616 | tf_op jit(solution)/shard_map/ppermute | solution.py:605
  85.1 5.6 %collective-permute-start.20 = (bf16[32,64,128]{2,1,0:T(8,128)(2,1)S(1)}, bf16[32,64,128]{2,1,0:T(8,128)(2,1)S(1)}, u32[]{:S(2)}, u32[]{:S(2)}) collective-permute-start(bf16[32,64,128]{2,1,0:T(8,128)(2,1)S(1)} %get-tuple-element.67), channel_id=1, source_target_pairs={{0,1},{1,0},{2,3},{3,2},{4,5},{5,4},{6,7},{7,6},{8,9},{9,8},{10,11... | collective-permute-start | bytes 1572872 | tf_op jit(solution)/shard_map/ppermute | solution.py:529
  85.2 21.8 %collective-permute-start.17 = (f32[64,128]{1,0:T(8,128)S(1)}, f32[64,128]{1,0:T(8,128)S(1)}, u32[]{:S(2)}, u32[]{:S(2)}) collective-permute-start(f32[64,128]{1,0:T(8,128)S(1)} %slice_select_fusion.1), channel_id=1, source_target_pairs={{0,8},{8,0},{16,24},{24,16},{1,9},{9,1},{17,25},{25,17},{2,10},{10... | collective-permute-start | bytes 98312 | tf_op jit(solution)/shard_map/ppermute | solution.py:605
  90.7 24.3 %collective-permute-start.11 = (bf16[32,64,128]{2,1,0:T(8,128)(2,1)S(1)}, bf16[32,64,128]{2,1,0:T(8,128)(2,1)S(1)}, u32[]{:S(2)}, u32[]{:S(2)}) collective-permute-start(bf16[32,64,128]{2,1,0:T(8,128)(2,1)S(1)} %get-tuple-element.57), channel_id=1, source_target_pairs={{0,1},{1,0},{2,3},{3,2},{4,5},{5,4},{6,7},{7,6},{8,9},{9,8},{10,11... | collective-permute-start | bytes 1572872 | tf_op jit(solution)/shard_map/ppermute | solution.py:529
  104.4 4.6 %collective-permute-start.23 = (f32[1728]{0:T(1024)S(1)}, f32[1728]{0:T(1024)S(1)}, u32[]{:S(2)}, u32[]{:S(2)}) collective-permute-start(f32[1728]{0:T(1024)S(1)} %slice_reduce_fusion), channel_id=1, source_target_pairs={{0,16},{8,24},{16,0},{24,8},{1,17},{9,25},{17,1},{25,9},{2,18},{10... | collective-permute-start | bytes 20744 | tf_op jit(solution)/shard_map/ppermute | solution.py:606
  109.0 5.3 %collective-permute-start.24 = (f32[1728]{0:T(1024)S(1)}, f32[1728]{0:T(1024)S(1)}, u32[]{:S(2)}, u32[]{:S(2)}) collective-permute-start(f32[1728]{0:T(1024)S(1)} %add.73), channel_id=1, source_target_pairs={{0,8},{8,0},{16,24},{24,16},{1,9},{9,1},{17,25},{25,17},{2,10},{10... | collective-permute-start | bytes 20744 | tf_op jit(solution)/shard_map/ppermute | solution.py:606
  110.6 9.3 %collective-permute-start.21 = (bf16[16,64,128]{2,1,0:T(8,128)(2,1)S(1)}, bf16[16,64,128]{2,1,0:T(8,128)(2,1)S(1)}, u32[]{:S(2)}, u32[]{:S(2)}) collective-permute-start(bf16[16,64,128]{2,1,0:T(8,128)(2,1)S(1)} %get-tuple-element.68), channel_id=1, source_target_pairs={{0,8},{8,16},{16,24},{1,9},{9,17},{17,25},{2,10},{10,18},{18,26},{... | collective-permute-start | bytes 786440 | tf_op jit(solution)/shard_map/ppermute | solution.py:541
  113.0 8.6 %collective-permute-start.22 = (bf16[16,64,128]{2,1,0:T(8,128)(2,1)S(1)}, bf16[16,64,128]{2,1,0:T(8,128)(2,1)S(1)}, u32[]{:S(2)}, u32[]{:S(2)}) collective-permute-start(bf16[16,64,128]{2,1,0:T(8,128)(2,1)S(1)} %get-tuple-element.69), channel_id=1, source_target_pairs={{8,0},{16,8},{24,16},{9,1},{17,9},{25,17},{10,2},{18,10},{26,18},{... | collective-permute-start | bytes 786440 | tf_op jit(solution)/shard_map/ppermute | solution.py:542
  (21 other events, 85.5 us)

commit v2 on v0

v2 whole, which is shorter than its diff:
```python
import math

import jax
import jax.numpy as jnp
from jax import lax
from jax.experimental import pallas as pl
from jax.experimental.pallas import tpu as pltpu
from jax.sharding import PartitionSpec as P

F32, BF16 = jnp.float32, jnp.bfloat16
HINTS = dict(
    inner=0.1, outer=20, back=0.1, out=0.1, filter=0.1, sums=0.1, out_sums=0.1, taps=0.1, late_taps=0.1, input=20, pack=0.1, last=0.1
)
RATE = 10**9
IN_VMEM = pl.BlockSpec(memory_space=pltpu.VMEM)
ANYWHERE = pl.BlockSpec(memory_space=pl.ANY)


class Place:
    def __init__(self, count):
        self.mids = 2
        self.his = count // 4
        index = lax.axis_index("chan")
        self.core = index % 2
        self.mid = index // 2 % self.mids
        self.hi = index // 2 // self.mids

    def block(self, hi_back, mid_back, core_flip):
        hi = (self.hi + self.his - hi_back) % self.his
        mid = (self.mid + self.mids - mid_back) % self.mids
        core = 1 - self.core if core_flip else self.core
        return hi, mid, core

    def flat(self, hi, mid, core):
        return (hi * self.mids + mid) * 2 + core


def size_of(shape, dtype):
    return math.prod(shape) * jnp.dtype(dtype).itemsize


def rims(near, far):
    odd = lax.axis_index("space") % 2 == 1

    def up(p):
        return jnp.where(odd, near[p].astype(F32), far[p].astype(F32))

    def down(p):
        return jnp.where(odd, far[p].astype(F32), near[p].astype(F32))

    return up, down


def kernel_call(kernel, outs, args, scratch=(), after=(), micros=0.1, places=None):
    used = len(args)

    def run(*refs):
        kernel(*refs[:used], *refs[used + len(after) :])

    held = [x for x in (*args, *outs, *scratch) if jnp.issubdtype(x.dtype, jnp.floating)]
    room = sum(size_of(x.shape, x.dtype) for x in held)
    return pl.pallas_call(
        run,
        out_shape=outs,
        in_specs=[IN_VMEM] * used + [ANYWHERE] * len(after),
        out_specs=places or [IN_VMEM] * len(outs),
        scratch_shapes=list(scratch),
        compiler_params=pltpu.CompilerParams(vmem_limit_bytes=room + 4 * 2**20),
        cost_estimate=pl.CostEstimate(flops=int(micros * RATE), bytes_accessed=0, transcendentals=0),
    )(*args, *after)


def shaped(shape, dtype=BF16):
    return jax.ShapeDtypeStruct(shape, dtype)


def line_home(line, rows):
    plane, row = divmod(line, rows)
    quarter = rows // 4
    core = row // (2 * quarter)
    outer = (row // quarter) in (0, 3)
    return core, outer, plane * quarter + row % quarter


def raw_to_cells(raw, chans, store):
    lines = raw.shape[0] // chans

    @pl.loop(0, chans // 16)
    def _(g):
        group = pl.ds(pl.multiple_of(g * 16, 16), 16)
        for first in range(0, lines, 16):
            block = [raw[pl.ds(pl.multiple_of((g * 16 + c) * lines + first, 16), 16), :] for c in range(16)]
            turned = jnp.swapaxes(jnp.stack([b.astype(F32) for b in block]), 0, 1).astype(BF16)
            for i in range(16):
                store(first + i, group, turned[i])


def write_raw(load, raw, room, sems, chans, lines):
    def copy(start):
        rows = slice(start * lines, (start + 16) * lines)
        return pltpu.make_async_copy(room.at[rows], raw.at[rows], sems.at[start // 16])

    for start in range(0, chans, 16):
        group = slice(start, start + 16)
        for first in range(0, lines, 16):
            block = jnp.stack([load(first + i, group).astype(F32) for i in range(16)])
            turned = jnp.swapaxes(block, 0, 1).astype(BF16)
            for c in range(16):
                at = (start + c) * lines + first
                room[at : at + 16] = turned[c]
        copy(start).start()
    for start in range(0, chans, 16):
        copy(start).wait()


def relayout_images(images, after=()):
    chans, planes, rows, width = images.shape

    def kernel(raw, cells, near, far):
        odd = lax.axis_index("space") % 2 == 1

        def store(line, group, value):
            cells[line, group] = value

        raw_to_cells(raw, chans, store)
        for parity, (first, last) in enumerate(((far, near), (near, far))):

            @pl.when(odd == bool(parity))
            def _():
                @pl.loop(0, planes)
                def _(p):
                    first[p] = cells[p * rows]
                    last[p] = cells[p * rows + rows - 1]

    edge = shaped((planes, chans, width))
    return kernel_call(
        kernel,
        [shaped((planes * rows, chans, width)), edge, edge],
        [images.reshape(-1, width)],
        (),
        after,
    )


def relayout_grad(grad_out, count, after=()):
    chans, planes, rows, width = grad_out.shape
    half = planes * rows // 2

    def kernel(raw, own, other):
        core = Place(count).core
        for mine in range(2):

            @pl.when(core == mine)
            def _():
                def store(line, group, value):
                    home, outer, at = line_home(line, rows)
                    out = own if home == mine else other
                    out[outer * (half // 2) + at, group] = value

                raw_to_cells(raw, chans, store)

    part = shaped((half, chans, width))
    return kernel_call(kernel, [part, part], [grad_out.reshape(-1, width)], (), after, 0.5)


def tap_planes(weights, spread, chans, width):
    turned = jnp.concatenate([weights, jnp.zeros((5, chans), F32)], axis=0).T
    for k in range(27):
        spread[k] = jnp.broadcast_to(turned[:, k : k + 1], (chans, width))


def fill_window(padded, line, up, down, planes, rows):
    zero = jnp.zeros(padded.shape[1:], F32)
    for n in range(rows + 2):
        padded[n] = zero
        padded[(planes + 1) * (rows + 2) + n] = zero

    @pl.loop(0, planes)
    def _(p):
        base = (p + 1) * (rows + 2)
        if up is not None:
            padded[base] = up(p)
            padded[base + rows + 1] = down(p)
        for r in range(rows):
            padded[base + 1 + r] = line(p, r).astype(F32)


def depthwise(padded, spread, planes, rows, wanted, store, flipped):
    _, chans, width = padded.shape
    lane = lax.broadcasted_iota(jnp.int32, (8, width), 1)
    deep = 4 // len(wanted)

    def summed(first, group):
        sums = {(d, r): [None] * 3 for d in range(deep) for r in wanted}
        for a in range(3):
            taps = [[spread[26 - 9 * a - 3 * b - e if flipped else 9 * a + 3 * b + e, group] for e in range(3)] for b in range(3)]
            for d in range(deep):
                for line in sorted({r + b for r in wanted for b in range(3)}):
                    cells = padded[(first + d + a) * (rows + 2) + line, group]
                    for b in range(3):
                        if line - b in wanted:
                            held = sums[d, line - b]
                            for e in range(3):
                                term = taps[b][e] * cells
                                held[e] = term if held[e] is None else held[e] + term
        for place, held in sums.items():
            before = jnp.where(lane == 0, 0.0, pltpu.roll(held[0], 1, 1))
            after = jnp.where(lane == width - 1, 0.0, pltpu.roll(held[2], width - 1, 1))
            sums[place] = held[1] + before + after
        return sums

    @pl.loop(0, planes // deep)
    def _(i):
        for start in range(0, chans, 16):
            low = summed(i * deep, slice(start, start + 8))
            high = summed(i * deep, slice(start + 8, start + 16))
            for d, r in low:
                both = jnp.concatenate([low[d, r], high[d, r]], axis=0)
                store(i * deep + d, r, slice(start, start + 16), both)


def hidden_part(cells, up, down, weights, count, planes, rows, outer, after=()):
    _, chans, width = cells.shape
    quarter = rows // 4
    args = [cells, up, down, weights] if outer else [cells, weights]
    wanted = [r for r in range(rows) if ((r // quarter) in (0, 3)) == outer]

    def kernel(cells, *refs):
        weights, own, other, padded, spread, both = refs[-6:]
        up, down = rims(*refs[:2]) if outer else (None, None)
        core = Place(count).core
        tap_planes(weights[...], spread, chans, width)
        fill_window(
            padded,
            lambda p, r: cells[p * rows + r],
            up,
            down,
            planes,
            rows,
        )

        def put(p, r, group, value):
            home, _, at = line_home(r, rows)
            both[home, p * quarter + at, group] = value.astype(BF16)

        depthwise(padded, spread, planes, rows, wanted, put, False)

        @pl.loop(0, planes * quarter)
        def _(i):
            own[i] = both[core, i]
            other[i] = both[1 - core, i]

    part = shaped((planes * quarter, chans, width))
    return kernel_call(
        kernel,
        [part, part],
        args,
        [
            pltpu.VMEM(((planes + 2) * (rows + 2), chans, width), F32),
            pltpu.VMEM((27, chans, width), F32),
            pltpu.VMEM((2, planes * quarter, chans, width), BF16),
        ],
        after,
        HINTS["outer" if outer else "inner"],
    )


def picked(table, starts, chans):
    total, wide = table.shape[1], len(starts) * chans
    col = lax.broadcasted_iota(jnp.int32, (total, wide), 1)
    row = lax.broadcasted_iota(jnp.int32, (total, wide), 0)
    want = jnp.zeros((total, wide), jnp.int32)
    for b, start in enumerate(starts):
        want = jnp.where((col >= b * chans) & (col < (b + 1) * chans), start + col - b * chans, want)
    choice = jnp.where(row == want, 1.0, 0.0).astype(BF16)
    return jnp.dot(table, choice, preferred_element_type=F32).astype(BF16)


def pack_grad(own, arrived, filter_own, filter_arrived, count, after=()):
    half, chans, width = own.shape
    part = half // 2
    his, mids = count // 4, 2
    hi_slices, mid_slices = mids * 2 * chans // width, his * 2 * chans // width

    def kernel(own, arrived, filter_own, filter_arrived, *outs):
        place = Place(count)
        table = jnp.concatenate([filter_own[...], filter_arrived[...]], axis=0)
        to_hi, to_mid = outs[: his - 1], outs[his - 1 : his + mids - 2]
        mine_hi, mine_mid = outs[-2:]

        def columns(for_hi, hi, mid):
            if for_hi:
                cells = [(hi, (mid + mids - t) % mids) for t in range(mids)]
            else:
                cells = [((hi + his - s) % his, mid) for s in range(his)]
            starts = [
                place.flat(hi_, mid_, place.core if q == 0 else 1 - place.core) * chans
                for hi_, mid_ in cells
                for q in range(2)
            ]
            return picked(table, starts, chans)

        def put(out, base, value):
            for i in range(value.shape[1] // width):
                out[base + i] = value[:, i * width : (i + 1) * width]

        for refs, offset in ((to_hi, 0), (to_mid, part)):

            @pl.loop(0, part)
            def _(i):
                for ref in refs:
                    ref[i, :chans] = own[offset + i]
                    ref[i, chans:] = arrived[offset + i]

        for s, ref in enumerate(to_hi, 1):
            put(ref, part, columns(True, (place.hi + s) % his, place.mid))
        for t, ref in enumerate(to_mid, 1):
            put(ref, part, columns(False, place.hi, (place.mid + t) % mids))
        put(mine_hi, 0, columns(True, place.hi, place.mid))
        put(mine_mid, 0, columns(False, place.hi, place.mid))

    outs = (
        [shaped((part + hi_slices, 2 * chans, width))] * (his - 1)
        + [shaped((part + mid_slices, 2 * chans, width))] * (mids - 1)
        + [shaped((hi_slices, 2 * chans, width)), shaped((mid_slices, 2 * chans, width))]
    )
    outs = kernel_call(kernel, outs, [own, arrived, filter_own, filter_arrived], (), after, micros=HINTS["pack"])
    return outs[: his - 1], outs[his - 1 : his + mids - 2], outs[-2], outs[-1]


def product_terms(weights, blocks, outs, part, both, width):
    step = math.gcd(part, 4)

    @pl.loop(0, part // step)
    def _(i):
        cells = jnp.concatenate(
            [jnp.concatenate([ref[i * step + j] for ref in blocks], axis=0) for j in range(step)], axis=1
        )
        product = jnp.dot(weights, cells, preferred_element_type=F32).astype(BF16)
        for n, out in enumerate(outs):
            for j in range(step):
                out[i * step + j] = product[n * both : (n + 1) * both, j * width : (j + 1) * width]


def back_terms(parts, after=()):
    args, outs, plans = [], [], []
    for mine, arrived, filter_mine, sends in parts:
        slices, both, width = filter_mine.shape
        part = mine.shape[0] - slices
        plans.append((len(args), len(outs), len(arrived), sends, slices, part))
        args += [mine, filter_mine, *arrived]
        outs += [shaped((part, both, width))] * (sends + 1) + [shaped(((1 + len(arrived)) * both, slices * width))]
    used = len(args)

    def kernel(*refs):
        for start, out, many, sends, slices, part in plans:
            mine, filter_mine, *arrived = refs[start : start + 2 + many]
            rows = [jnp.concatenate([filter_mine[i] for i in range(slices)], axis=1)]
            for ref in arrived:
                rows.append(jnp.concatenate([ref[part + i] for i in range(slices)], axis=1))
            block = jnp.concatenate(rows, axis=0)
            refs[used + out + sends + 1][...] = block
            turned = block.astype(F32).T.astype(BF16)
            product_terms(turned, [mine, *arrived], refs[used + out : used + out + sends + 1], part, both, width)

    done = kernel_call(kernel, outs, args, (), after, micros=HINTS["back"])
    return [(done[o], done[o + 1 : o + 1 + sends], done[o + 1 + sends]) for _, o, _, sends, _, _ in plans]


def summed_parts(first, second, after=(), name="sums"):
    part, both, width = first[0].shape
    chans = both // 2

    def kernel(*refs):
        outs = refs[-4:]
        for n, terms in enumerate((refs[: len(first)], refs[len(first) : -4])):

            @pl.loop(0, part)
            def _(i):
                total = terms[0][i].astype(F32)
                for term in terms[1:]:
                    total = total + term[i].astype(F32)
                outs[n][i] = total[:chans].astype(BF16)
                outs[2 + n][i] = total[chans:].astype(BF16)

    done = kernel_call(kernel, [shaped((part, chans, width))] * 4, [*first, *second], (), after, HINTS[name])
    return done[:2], done[2:]


def edge_rows(own, arrived, count, rows, after=()):
    part, chans, width = own.shape
    quarter = rows // 4
    planes = part // quarter

    def kernel(own, arrived, near, far):
        core = Place(count).core
        odd = lax.axis_index("space") % 2
        for mine in range(2):
            for parity in range(2):

                @pl.when((core == mine) & (odd == parity))
                def _():
                    first, last = (own, arrived) if mine == 0 else (arrived, own)
                    to_first, to_last = (near, far) if parity else (far, near)

                    @pl.loop(0, planes)
                    def _(p):
                        to_first[p] = first[p * quarter]
                        to_last[p] = last[p * quarter + quarter - 1]

    edge = shaped((planes, chans, width))
    return kernel_call(kernel, [edge, edge], [own, arrived], (), after)


def joined(own, arrived, after=()):
    part, chans, width = own[0].shape
    many = len(own)

    def kernel(*refs):
        @pl.loop(0, part)
        def _(i):
            for a, b, out in zip(refs[:many], refs[many : 2 * many], refs[2 * many :]):
                out[i, :chans] = a[i]
                out[i, chans:] = b[i]

    return kernel_call(kernel, [shaped((part, 2 * chans, width))] * many, [*own, *arrived], (), after)


def out_terms(parts, after=()):
    args, outs, plans = [], [], []
    for block, hiddens, terms in parts:
        plans.append((len(args), len(outs), len(hiddens), terms))
        args += [block, *hiddens]
        outs += [shaped(hiddens[0].shape)] * terms
    used = len(args)

    def kernel(*refs):
        for start, out, many, terms in plans:
            part, both, width = refs[start + 1].shape
            product_terms(
                refs[start][...],
                refs[start + 1 : start + 1 + many],
                refs[used + out : used + out + terms],
                part,
                both,
                width,
            )

    done = kernel_call(kernel, outs, args, (), after, micros=HINTS["out"])
    return [done[o : o + terms] for _, o, _, terms in plans]


def filter_terms(parts, count, after=()):
    args, plans, outs, scratch = [], [], [], []
    for hiddens, grads, over_mid in parts:
        part, both, width = hiddens[0].shape
        chans = both // 2
        plans.append((len(args), len(outs), len(hiddens), len(grads), over_mid))
        args += [*hiddens, *grads]
        outs += [shaped((both, len(hiddens) * both), F32)] * len(grads)
        scratch += [
            pltpu.VMEM((len(hiddens) * both, part * width), BF16),
            pltpu.VMEM((len(grads) * both, part * width), BF16),
        ]
    used = len(args)

    def kernel(*refs):
        place = Place(count)
        results, rooms = refs[used : used + len(outs)], refs[used + len(outs) :]
        for n, (start, out, cols_of, rows_of, over_mid) in enumerate(plans):
            hidden = refs[start : start + cols_of]
            grad = refs[start + cols_of : start + cols_of + rows_of]
            ordered, lined = rooms[2 * n], rooms[2 * n + 1]
            for j in range(part):
                span = slice(j * width, (j + 1) * width)
                for i, ref in enumerate(hidden):
                    hi, mid, _ = place.block(0, i, 0) if over_mid else place.block(i, 0, 0)
                    for q in range(2):
                        core = 1 - place.core if q else place.core
                        at = pl.multiple_of(((mid if over_mid else hi) * 2 + core) * chans, chans)
                        ordered[pl.ds(at, chans), span] = ref[j, q * chans : (q + 1) * chans]
                for i, ref in enumerate(grad):
                    lined[i * both : (i + 1) * both, span] = ref[j]
            pairs = lax.dot_general(lined[...], ordered[...], (((1,), (1,)), ((), ())), preferred_element_type=F32)
            for i in range(rows_of):
                results[out + i][...] = pairs[i * both : (i + 1) * both]

    done = kernel_call(kernel, outs, args, scratch, after, HINTS["filter"])
    return [done[out : out + rows_of] for _, out, _, rows_of, _ in plans]


def filter_gathered(for_hi, for_mid, count, after=()):
    his, mids = len(for_hi), len(for_mid)
    chans, wide = for_hi[0].shape[0] // 2, for_hi[0].shape[1]
    pair = wide // mids

    def kernel(*refs):
        place = Place(count)

        def chosen(pieces, at, mine):
            value = pieces[0][...]
            for n, piece in enumerate(pieces[1:], 1):
                value = jnp.where((mine + n) % len(pieces) == at, piece[...], value)
            return value

        by_hi = [chosen(refs[:his], hi, place.hi) for hi in range(his)]
        by_mid = [chosen(refs[his : his + mids], mid, place.mid) for mid in range(mids)]
        for hi in range(his):
            for mid in range(mids):
                block = by_hi[hi][:, mid * pair : (mid + 1) * pair] + by_mid[mid][:, hi * pair : (hi + 1) * pair]
                at = (hi * mids + mid) * chans
                refs[-2][at : at + chans] = block[:chans]
                refs[-1][at : at + chans] = block[chans:]

    out = shaped((his * mids * chans, pair), F32)
    return kernel_call(kernel, [out, out], [*for_hi, *for_mid], (), after)


def slab_pieces(own, arrived, taps, slabs, after=()):
    rows = own.shape[0] // slabs
    wide = own.shape[1]

    def kernel(own, arrived, taps, *outs):
        slab = lax.axis_index("space")
        for apart, out in enumerate(outs):
            at = pl.ds(pl.multiple_of(jnp.bitwise_xor(slab, apart) * rows, rows), rows)
            out[:rows] = own[at] + arrived[at]
            out[rows:] = taps[...]

    piece = shaped((rows + taps.shape[0], wide), F32)
    return kernel_call(kernel, [piece] * slabs, [own, arrived, taps], (), after)


def last_outputs(own, arrived, pieces, count, planes, rows, scale, after=()):
    _, chans, width = own[0].shape
    lines, many = planes * rows, len(pieces)

    def kernel(*refs):
        raw, filter_out, tap_out, room, sems = refs[4 + many :]
        core = Place(count).core
        for mine in range(2):

            @pl.when(core == mine)
            def _():
                def load(line, group):
                    home, outer, at = line_home(line, rows)
                    return refs[outer if home == mine else 2 + outer][at, group]

                write_raw(load, raw, room, sems, chans, lines)

        total = refs[4][...]
        for ref in refs[5 : 4 + many]:
            total = total + ref[...]
        total = total * scale
        filter_out[...] = total[:chans]
        tap_out[...] = total[chans : chans + 27, :chans]

    outs = [
        shaped((chans * lines, width)),
        shaped((chans, pieces[0].shape[1]), F32),
        shaped((27, chans), F32),
    ]
    scratch = [pltpu.VMEM((chans * lines, width), BF16), pltpu.SemaphoreType.DMA((chans // 16,))]
    raw, filter_out, tap_out = kernel_call(
        kernel, outs, [*own, *arrived, *pieces], scratch, after, HINTS["last"], [ANYWHERE, IN_VMEM, IN_VMEM]
    )
    return raw.reshape(chans, planes, rows, width), filter_out, tap_out


def input_gradient(own, arrived, near, far, weights, count, planes, rows, after=()):
    _, chans, width = own[0].shape
    quarter, lines = rows // 4, planes * rows

    def kernel(*refs):
        own, arrived = refs[:2], refs[2:4]
        near, far, weights, raw, token, padded, spread, cells, room, sems = refs[4:]
        core = Place(count).core
        token[...] = jnp.zeros(token.shape, F32)
        tap_planes(weights[...], spread, chans, width)

        def line(p, r):
            home, outer, at = line_home(r, rows)
            place = p * quarter + at
            return jnp.where(core == home, own[outer][place].astype(F32), arrived[outer][place].astype(F32))

        fill_window(padded, line, *rims(near, far), planes, rows)

        def store(p, r, group, value):
            cells[p * rows + r, group] = value.astype(BF16)

        depthwise(padded, spread, planes, rows, list(range(rows)), store, True)
        write_raw(lambda line, group: cells[line, group], raw, room, sems, chans, lines)

    raw, token = kernel_call(
        kernel,
        [shaped((chans * lines, width)), shaped((8, width), F32)],
        [*own, *arrived, near, far, weights],
        [
            pltpu.VMEM(((planes + 2) * (rows + 2), chans, width), F32),
            pltpu.VMEM((27, chans, width), F32),
            pltpu.VMEM((lines, chans, width), BF16),
            pltpu.VMEM((chans * lines, width), BF16),
            pltpu.SemaphoreType.DMA((chans // 16,)),
        ],
        after,
        HINTS["input"],
        [ANYWHERE, IN_VMEM],
    )
    return raw.reshape(chans, planes, rows, width), token


def tap_sums(cells, up, down, back, before, count, planes, rows, others, wide, after=()):
    _, chans, width = cells.shape
    half, quarter = rows // 2, rows // 4
    last = before is not None
    args = [cells, up, down, *back] + ([before] if last else [])

    def kernel(cells, near, far, inner, outside, *refs):
        out, padded, back = refs[-3 - last : len(refs) - last]
        sums = refs[-1] if last else out
        core = Place(count).core
        home = 1 - core if others else core
        fill_window(padded, lambda p, r: cells[p * rows + r], *rims(near, far), planes, rows)
        sums[...] = refs[0][...] if last else jnp.zeros(sums.shape, F32)
        lane = lax.broadcasted_iota(jnp.int32, (8, width), 1)
        deep = max(1, 4 // half)

        @pl.loop(0, planes * quarter)
        def _(i):
            back[0, i] = jnp.where(home == 0, outside[i].astype(F32), inner[i].astype(F32))
            back[1, i] = jnp.where(home == 0, inner[i].astype(F32), outside[i].astype(F32))

        @pl.loop(0, planes // deep)
        def _(i):
            for pair in range(0, chans, 16):
                both = {}
                for d in range(deep):
                    for r in range(half):
                        place = (i * deep + d) * quarter + r % quarter
                        both[d, r] = back[r // quarter, place, pair : pair + 16]
                for n in range(2):
                    group = slice(pair + 8 * n, pair + 8 * n + 8)
                    moved = {}
                    for key, value in both.items():
                        here = value[8 * n : 8 * n + 8]
                        later = jnp.where(lane == width - 1, 0.0, pltpu.roll(here, width - 1, 1))
                        earlier = jnp.where(lane == 0, 0.0, pltpu.roll(here, 1, 1))
                        moved[key] = (later, here, earlier)
                    for a in range(3):
                        images = {}
                        for d in range(deep):
                            base = (i * deep + d + a) * (rows + 2) + home * half
                            for line in range(half + 2):
                                images[d, line] = padded[base + line, group]
                        for b in range(3):
                            for e in range(3):
                                term = None
                                for (d, r), values in moved.items():
                                    product = images[d, r + b] * values[e]
                                    term = product if term is None else term + product
                                sums[9 * a + 3 * b + e, group] += term

        if last:
            row = lax.broadcasted_iota(jnp.int32, (chans, wide), 0)
            col = lax.broadcasted_iota(jnp.int32, (chans, wide), 1)
            for tap in range(27):
                total = jnp.sum(sums[tap], axis=1, keepdims=True)
                out[tap : tap + 1] = jnp.sum(jnp.where(row == col, total, 0.0), axis=0, keepdims=True)
            out[27:] = jnp.zeros((5, wide), F32)

    running = (27, chans, width)
    scratch = [
        pltpu.VMEM(((planes + 2) * (rows + 2), chans, width), F32),
        pltpu.VMEM((2, planes * quarter, chans, width), F32),
    ]
    if last:
        scratch.append(pltpu.VMEM(running, F32))
    outs = [shaped((32, wide) if last else running, F32)]
    return kernel_call(kernel, outs, args, scratch, after, HINTS["late_taps" if last else "taps"])[0]


def body(images, depth_filter, point_filter, grad_out):
    chans, planes, rows, width = images.shape
    count, slabs = lax.axis_size("chan"), lax.axis_size("space")
    his, mids = count // 4, 2
    place = Place(count)
    grad_scale = 1.0 / math.sqrt(planes * rows * width * slabs)

    def moved(value, target):
        pairs = []
        for i in range(count):
            hi, mid, core = target(i // 2 // mids, i // 2 % mids, i % 2)
            pairs.append((i, (hi % his * mids + mid % mids) * 2 + core))
        return lax.ppermute(value, "chan", pairs)

    def to_core(value):
        return moved(value, lambda hi, mid, core: (hi, mid, 1 - core))

    def along_hi(value, by):
        return moved(value, lambda hi, mid, core: (hi + by, mid, core))

    def along_mid(value, by):
        return moved(value, lambda hi, mid, core: (hi, mid + by, core))

    def halo(near, far):
        swaps = [[(i + d, i + 1 - d) for i in range(first, slabs - 1, 2) for d in range(2)] for first in range(2)]
        return lax.ppermute(near, "space", swaps[0]), lax.ppermute(far, "space", swaps[1])

    def exchanged(value, apart):
        return lax.ppermute(value, "space", [(i, i ^ apart) for i in range(slabs)])

    filter_arrived = to_core(point_filter)
    grad_own, grad_other = relayout_grad(grad_out, count)
    grad_arrived = to_core(grad_other)
    cells, near, far = relayout_images(images, [grad_own])
    image_rims = halo(near, far)
    to_hi, to_mid, filter_hi, filter_mid = pack_grad(
        grad_own, grad_arrived, point_filter, filter_arrived, count, [cells]
    )
    grads_hi = [along_hi(value, s) for s, value in enumerate(to_hi, 1)]
    grads_mid = [along_mid(value, t) for t, value in enumerate(to_mid, 1)]

    windows = (cells, *image_rims)
    plan = (count, planes, rows)
    inner_own, inner_other = hidden_part(*windows, depth_filter, *plan, False, [to_hi[0]])
    inner_arrived = to_core(inner_other)
    (keep_first, send_first, block_first), (keep_second, send_second, block_second) = back_terms(
        [(to_hi[0], grads_hi, filter_hi, mids - 1), (to_mid[0], grads_mid, filter_mid, his - 1)], [inner_own]
    )
    back_first = [keep_first] + [along_mid(value, -t) for t, value in enumerate(send_first, 1)]
    back_second = [keep_second] + [along_hi(value, -s) for s, value in enumerate(send_second, 1)]

    outer_own, outer_other = hidden_part(*windows, depth_filter, *plan, True, [keep_first])
    outer_arrived = to_core(outer_other)
    hidden_first, hidden_second = joined([inner_own, outer_own], [inner_arrived, outer_arrived])
    hiddens_mid = [hidden_first] + [along_mid(hidden_first, t) for t in range(1, mids)]
    hiddens_hi = [hidden_second] + [along_hi(hidden_second, s) for s in range(1, his)]

    back_own, back_other = summed_parts(back_first, back_second, [hidden_first])
    back_arrived = [to_core(value) for value in back_other]
    wide = his * mids * 2 * chans // slabs
    taps = tap_sums(*windows, back_own, None, *plan, False, wide, [back_own[0]])
    edges = edge_rows(back_own[1], back_arrived[1], count, rows, [taps])
    back_rims = halo(*edges)

    for_hi, for_mid = filter_terms(
        [(hiddens_mid, [to_hi[0], *grads_hi], True), (hiddens_hi, [to_mid[0], *grads_mid], False)], count, [edges[0]]
    )
    owned = for_hi[0]
    for_hi = [for_hi[0]] + [along_hi(piece, -s) for s, piece in enumerate(for_hi[1:], 1)]
    for_mid = [for_mid[0]] + [along_mid(piece, -t) for t, piece in enumerate(for_mid[1:], 1)]
    out_first, out_second = out_terms(
        [(block_first, hiddens_mid, his), (block_second, hiddens_hi, mids)], [owned]
    )
    latest = out_first[0]
    out_first = [out_first[0]] + [along_hi(value, -s) for s, value in enumerate(out_first[1:], 1)]
    out_second = [out_second[0]] + [along_mid(value, -t) for t, value in enumerate(out_second[1:], 1)]

    input_grad, latest = input_gradient(back_own, back_arrived, *back_rims, depth_filter, *plan, [latest])
    taps = tap_sums(*windows, back_arrived, taps, *plan, True, wide, [latest])
    own, other = filter_gathered(for_hi, for_mid, count, [taps])
    chip_arrived = to_core(other)
    if own.shape[1] != wide:

        def by_slab(value):
            value = value.reshape(his * mids, chans, -1).swapaxes(0, 1).reshape(chans, slabs, wide)
            return value.swapaxes(0, 1).reshape(-1, wide)

        own, chip_arrived = by_slab(own), by_slab(chip_arrived)
    pieces = slab_pieces(own, chip_arrived, taps, slabs)
    latest = pieces[0]
    pieces = [pieces[0]] + [exchanged(piece, apart) for apart, piece in enumerate(pieces[1:], 1)]
    out_own, out_other = summed_parts(out_first, out_second, [latest], "out_sums")
    out_arrived = [to_core(value) for value in out_other]
    block_out, point_grad, depth_grad = last_outputs(out_own, out_arrived, pieces, *plan, grad_scale)
    return block_out, point_grad, input_grad, depth_grad


def solution(mesh):
    placed = (
        P("chan", None, "space", None),
        P(None, "chan"),
        P("chan", None),
        P("chan", None, "space", None),
    )
    return jax.shard_map(
        body,
        mesh=mesh,
        in_specs=placed,
        out_specs=(
            P("chan", None, "space", None),
            P("chan", "space"),
            P("chan", None, "space", None),
            P(None, "chan"),
        ),
        check_vma=False,
    )
```

time: 187 us -> 82.9 us (0.44)
  other arithmetic: 42 us -> 0 us
  local copies, waits for them, and re-layouts: 41.7 us -> 1.32 us
  blocking collectives: 33.2 us -> 0 us
  Pallas kernels: 0 us -> 29.9 us
  matrix products: 16.7 us -> 0 us
  between operations: 14.7 us -> 0.9 us
  starting transfers between devices: 12 us -> 24.1 us
    pallas_call x0 -> x18, Pallas kernels: none -> 29.9 us  [kernel_call(): pl.pallas_call(run, out_shape=outs, in_specs=[IN_VMEM] * used + [ANYWHERE...]
    all_gather x2 -> x0, local copies, waits for them, and re-layouts: 26.4 us -> none  [the longest x1 14 us: body(): grad_piece = lax.all_gather(grad_out, 'chan', axis=0, tiled=True)]
    convert_element_type x2 -> x0, other arithmetic: 19.6 us -> none  [the longest x1 10 us: body(): depth_backward(padded_back, depth_filter, planes, row_count, col_count)]
    psum x1 -> x0, blocking collectives: 19.4 us -> none  [body(): depth_grad = lax.psum(local_taps, 'space') * grad_scale]
    ppermute x4 -> x26, waiting for transfers between devices: 8.08 us -> 26.6 us  [the longest x19 21.1 us: moved(): return lax.ppermute(value, 'chan', pairs)]
    all_gather x2 -> x0, waiting for transfers between devices: 17.4 us -> none  [the longest x1 17.4 us: body(): grad_piece = lax.all_gather(grad_out, 'chan', axis=0, tiled=True)]
    dot_general x3 -> x0, matrix products: 16.7 us -> none  [the longest x1 7.21 us: body(): lax.dot_general(columns, grad_rows, (((0,), (0,)), ((), ())), preferred_e...]
    all_gather x1 -> x0, blocking collectives: 13.8 us -> none  [body(): filter_piece = lax.all_gather(point_filter, 'chan', axis=0, tiled=True)]
  transfers between devices with their start and end apart: 7 -> 26, of which waited for: 3 -> 11; matrix products, arithmetic and copies ran while one was open for 52% -> 0% of each run, Pallas kernels for 0% -> 32%
where the time goes in v2:
time: 82.9 us; the launch traced here: 82.7 us
  Pallas kernels  29.9 us (36%)
  waiting for transfers between devices  26.6 us (32%)
  starting transfers between devices  24.1 us (29%)
  local copies, waits for them, and re-layouts  1.32 us (2%)
  between operations  0.9 us (1%)
    pallas_call x18, Pallas kernels, kernel_call(): pl.pallas_call(run, out_shape=outs, in_specs=[IN_VMEM] * used + [ANYWHERE...  29.9 us
    ppermute x19, waiting for transfers between devices, moved(): return lax.ppermute(value, 'chan', pairs)  21.1 us
    ppermute x19, starting transfers between devices, moved(): return lax.ppermute(value, 'chan', pairs)  15 us
    ppermute x3, waiting for transfers between devices, exchanged(): return lax.ppermute(value, 'space', [(i, i ^ apart) for i in range(slabs)])  5.51 us
    ppermute x3, starting transfers between devices, exchanged(): return lax.ppermute(value, 'space', [(i, i ^ apart) for i in range(slabs)])  4.56 us
    ppermute x2, starting transfers between devices, halo(): lax.ppermute(near, 'space', swaps[0])  3.22 us
  transfers between devices with their start and end apart: 26, of which 11 were waited for; matrix products, arithmetic and copies ran while one was open for 0% of the time, Pallas kernels for 32%

profile of v2, /device:TPU:0, one launch (start us, length us, event | category | flops | bytes accessed | tf_op | source)
XLA Modules:
  0.0 82.7 jit_solution(4393099034256939014)
XLA Ops:
  5.2 3.0 %collective-permute-start.2 = (bf16[18,128,128]{2,1,0:T(8,128)(2,1)S(1)}, bf16[18,128,128]{2,1,0:T(8,128)(2,1)S(1)}, u32[]{:S(2)}, u32[]{:S(2)}) collective-permute-start(bf16[18,128,128]{2,1,0:T(8,128)(2,1)S(1)} %get-tuple-element.57.refs_2_.refs_0_), channel_id=1, source_target_pairs={{0,4},{1,5},{2,6},{3,7},{4,0},{5,1},{6,2},{7,3},{8,12},{9,13},{10,... | collective-permute-start | bytes 1769480 | tf_op jit(solution)/shard_map/ppermute | solution.py:694
  8.1 1.5 %collective-permute-start.3 = (bf16[18,128,128]{2,1,0:T(8,128)(2,1)S(1)}, bf16[18,128,128]{2,1,0:T(8,128)(2,1)S(1)}, u32[]{:S(2)}, u32[]{:S(2)}) collective-permute-start(bf16[18,128,128]{2,1,0:T(8,128)(2,1)S(1)} %get-tuple-element.59.refs_3_.refs_6_), channel_id=1, source_target_pairs={{0,2},{1,3},{2,0},{3,1},{4,6},{5,7},{6,4},{7,5},{8,10},{9,11},{10,... | collective-permute-start | bytes 1769480 | tf_op jit(solution)/shard_map/ppermute | solution.py:694
  9.6 1.6 %collective-permute-start.4 = (bf16[16,64,128]{2,1,0:T(8,128)(2,1)S(1)}, bf16[16,64,128]{2,1,0:T(8,128)(2,1)S(1)}, u32[]{:S(2)}, u32[]{:S(2)}) collective-permute-start(bf16[16,64,128]{2,1,0:T(8,128)(2,1)S(1)} %get-tuple-element.63), channel_id=1, source_target_pairs={{0,8},{8,0},{16,24},{24,16},{1,9},{9,1},{17,25},{25,17},{2,10},{10... | collective-permute-start | bytes 786440 | tf_op jit(solution)/shard_map/ppermute | solution.py:707
  11.9 3.1 %shard_map.78 = (bf16[16,64,128]{2,1,0:T(8,128)(2,1)S(1)}, bf16[16,64,128]{2,1,0:T(8,128)(2,1)S(1)}) custom-call(bf16[64,64,128]{2,1,0:T(8,128)(2,1)S(1)} %get-tuple-element.56.refs_4_.refs_0_, f32[27,64]{1,0:T(8,128)S(1)} %copy-done.2, bf16[18,128,128]{2,1,0:T(8,128)(2,1)S(1)} %get-tuple-element.57.refs_2_.refs_0_), custom_call_target="tpu_custom_call" | custom-call | flops 100000000 | tf_op jit(solution)/shard_map/pallas_call | solution.py:62
  15.1 6.7 %collective-permute-done.2.refs_2_.refs_3_ = bf16[18,128,128]{2,1,0:T(8,128)(2,1)S(1)} collective-permute-done((bf16[18,128,128]{2,1,0:T(8,128)(2,1)S(1)}, bf16[18,128,128]{2,1,0:T(8,128)(2,1)S(1)}, u32[]{:S(2)}, u32[]{:S(2)}) %collective-permute-start.2) | collective-permute-done | bytes 589856 | tf_op jit(solution)/shard_map/ppermute | solution.py:694
  21.8 1.5 %collective-permute-done.3.refs_5_.refs_7_ = bf16[18,128,128]{2,1,0:T(8,128)(2,1)S(1)} collective-permute-done((bf16[18,128,128]{2,1,0:T(8,128)(2,1)S(1)}, bf16[18,128,128]{2,1,0:T(8,128)(2,1)S(1)}, u32[]{:S(2)}, u32[]{:S(2)}) %collective-permute-start.3) | collective-permute-done | bytes 589856 | tf_op jit(solution)/shard_map/ppermute | solution.py:694
  23.2 2.0 %shard_map.79 = (bf16[16,128,128]{2,1,0:T(8,128)(2,1)S(1)}, bf16[16,128,128]{2,1,0:T(8,128)(2,1)S(1)}, bf16[256,256]{1,0:T(8,128)(2,1)S(1)}, bf16[16,128,128]{2,...) custom-call(bf16[18,128,128]{2,1,0:T(8,128)(2,1)S(1)} %get-tuple-element.57.refs_2_.refs_0_, ...), custom_call_target="tpu_custom_call" | custom-call | flops 100000000 | tf_op jit(solution)/shard_map/pallas_call | solution.py:62
  25.3 1.5 %collective-permute-start.10 = (bf16[16,128,128]{2,1,0:T(8,128)(2,1)S(1)}, bf16[16,128,128]{2,1,0:T(8,128)(2,1)S(1)}, u32[]{:S(2)}, u32[]{:S(2)}) collective-permute-start(bf16[16,128,128]{2,1,0:T(8,128)(2,1)S(1)} %get-tuple-element.72), channel_id=1, source_target_pairs={{0,2},{1,3},{2,0},{3,1},{4,6},{5,7},{6,4},{7,5},{8,10},{9,11},{10,... | collective-permute-start | bytes 1572872 | tf_op jit(solution)/shard_map/ppermute | solution.py:694
  27.3 3.4 %shard_map.80 = (bf16[16,64,128]{2,1,0:T(8,128)(2,1)S(1)}, bf16[16,64,128]{2,1,0:T(8,128)(2,1)S(1)}) custom-call(bf16[64,64,128]{2,1,0:T(8,128)(2,1)S(1)} %get-tuple-element.56.refs_4_.refs_0_, bf16[16,64,128]{2,1,0:T(8,128)(2,1)S(1)} %collective-permute-done.4.refs_1_, bf16[16,64,128]{2,1,0:T(8,128)(2,1)S(1)} %collective-permute-done.5.refs_2_, ...), custom_call_target="tpu_custom_call" | custom-call | flops 20000000000 | tf_op jit(solution)/shard_map/pallas_call | solution.py:62
  30.9 1.5 %collective-permute-done.7.refs_3_ = bf16[16,64,128]{2,1,0:T(8,128)(2,1)S(1)} collective-permute-done((bf16[16,64,128]{2,1,0:T(8,128)(2,1)S(1)}, bf16[16,64,128]{2,1,0:T(8,128)(2,1)S(1)}, u32[]{:S(2)}, u32[]{:S(2)}) %collective-permute-start.7) | collective-permute-done | bytes 262176 | tf_op jit(solution)/shard_map/ppermute | solution.py:694
  32.9 1.7 %collective-permute-start.9 = (bf16[16,128,128]{2,1,0:T(8,128)(2,1)S(1)}, bf16[16,128,128]{2,1,0:T(8,128)(2,1)S(1)}, u32[]{:S(2)}, u32[]{:S(2)}) collective-permute-start(bf16[16,128,128]{2,1,0:T(8,128)(2,1)S(1)} %get-tuple-element.71.refs_4_), channel_id=1, source_target_pairs={{0,4},{1,5},{2,6},{3,7},{4,0},{5,1},{6,2},{7,3},{8,12},{9,13},{10,... | collective-permute-start | bytes 1572872 | tf_op jit(solution)/shard_map/ppermute | solution.py:694
  34.6 5.6 %collective-permute-done.10.refs_1_ = bf16[16,128,128]{2,1,0:T(8,128)(2,1)S(1)} collective-permute-done((bf16[16,128,128]{2,1,0:T(8,128)(2,1)S(1)}, bf16[16,128,128]{2,1,0:T(8,128)(2,1)S(1)}, u32[]{:S(2)}, u32[]{:S(2)}) %collective-permute-start.10) | collective-permute-done | bytes 524320 | tf_op jit(solution)/shard_map/ppermute | solution.py:694
  40.2 1.5 %collective-permute-done.11.refs_3_ = bf16[16,128,128]{2,1,0:T(8,128)(2,1)S(1)} collective-permute-done((bf16[16,128,128]{2,1,0:T(8,128)(2,1)S(1)}, bf16[16,128,128]{2,1,0:T(8,128)(2,1)S(1)}, u32[]{:S(2)}, u32[]{:S(2)}) %collective-permute-start.11) | collective-permute-done | bytes 524320 | tf_op jit(solution)/shard_map/ppermute | solution.py:694
  42.6 3.2 %shard_map.83.refs_2_.refs_5_ = f32[27,64,128]{2,1,0:T(8,128)S(1)} custom-call(bf16[64,64,128]{2,1,0:T(8,128)(2,1)S(1)} %get-tuple-element.56.refs_4_.refs_0_, bf16[16,64,128]{2,1,0:T(8,128)(2,1)S(1)} %collective-permute-done.4.refs_1_, bf16[16,64,128]{2,1,0:T(8,128)(2,1)S(1)} %collective-permute-done.5.refs_2_, ...), custom_call_target="tpu_custom_call" | custom-call | flops 100000000 | tf_op jit(solution)/shard_map/pallas_call | solution.py:62
  46.0 1.6 %collective-permute-start.18 = (bf16[16,64,128]{2,1,0:T(8,128)(2,1)S(1)}, bf16[16,64,128]{2,1,0:T(8,128)(2,1)S(1)}, u32[]{:S(2)}, u32[]{:S(2)}) collective-permute-start(bf16[16,64,128]{2,1,0:T(8,128)(2,1)S(1)} %get-tuple-element.78.refs_8_), channel_id=1, source_target_pairs={{0,8},{8,0},{16,24},{24,16},{1,9},{9,1},{17,25},{25,17},{2,10},{10... | collective-permute-start | bytes 786440 | tf_op jit(solution)/shard_map/ppermute | solution.py:707
  53.2 1.9 %shard_map.86 = (bf16[16,128,128]{2,1,0:T(8,128)(2,1)S(1)}, bf16[16,128,128]{2,1,0:T(8,128)(2,1)S(1)}, bf16[16,128,128]{2,1,0:T(8,128)(2,1)S(1)}, bf16[16,128,128]{2,1,0:T(8,128)(2,1)S(1)}) custom-call(bf16[256,256]{1,0:T(8,128)(2,1)S(1)} %get-tuple-element.62.refs_0_, bf16[16,128,128]{2,1,0:T(8,128)(2,1)S(1)} %get-tuple-element.69.refs_4_.refs_0_.refs_1_, ...), custom_call_target="tpu_custom_call" | custom-call | flops 100000000 | tf_op jit(solution)/shard_map/pallas_call | solution.py:62
  56.5 1.5 %collective-permute-start.14 = (bf16[16,128,128]{2,1,0:T(8,128)(2,1)S(1)}, bf16[16,128,128]{2,1,0:T(8,128)(2,1)S(1)}, u32[]{:S(2)}, u32[]{:S(2)}) collective-permute-start(bf16[16,128,128]{2,1,0:T(8,128)(2,1)S(1)} %get-tuple-element.83), channel_id=1, source_target_pairs={{0,2},{1,3},{2,0},{3,1},{4,6},{5,7},{6,4},{7,5},{8,10},{9,11},{10,... | collective-permute-start | bytes 1572872 | tf_op jit(solution)/shard_map/ppermute | solution.py:694
  58.0 6.8 %shard_map.87 = (bf16[4096,128]{1,0:T(8,128)(2,1)}, f32[8,128]{1,0:T(8,128)S(1)}) custom-call(bf16[16,64,128]{2,1,0:T(8,128)(2,1)S(1)} %get-tuple-element.77.refs_3_.refs_5_.refs_0_, bf16[16,64,128]{2,1,0:T(8,128)(2,1)S(1)} %get-tuple-element.75.refs_4_.refs_0_.refs_1_, bf16[16,64,128]{2,1,0:T(8,128)(2,1)S(1)} %collective-permute-done.17.refs_2_.refs_3_, ...), custom_call_target="tpu_custom_call" | custom-call | flops 20000000000 | tf_op jit(solution)/shard_map/pallas_call | solution.py:62
  64.8 3.5 %shard_map.88.refs_4_.refs_2_ = f32[32,128]{1,0:T(8,128)S(1)} custom-call(bf16[64,64,128]{2,1,0:T(8,128)(2,1)S(1)} %get-tuple-element.56.refs_4_.refs_0_, bf16[16,64,128]{2,1,0:T(8,128)(2,1)S(1)} %collective-permute-done.4.refs_1_, bf16[16,64,128]{2,1,0:T(8,128)(2,1)S(1)} %collective-permute-done.5.refs_2_, ...), custom_call_target="tpu_custom_call" | custom-call | flops 100000000 | tf_op jit(solution)/shard_map/pallas_call | solution.py:62
  70.8 2.2 %collective-permute-start.23 = (f32[96,128]{1,0:T(8,128)S(1)}, f32[96,128]{1,0:T(8,128)S(1)}, u32[]{:S(2)}, u32[]{:S(2)}) collective-permute-start(f32[96,128]{1,0:T(8,128)S(1)} %get-tuple-element.97), channel_id=1, source_target_pairs={{0,8},{8,0},{16,24},{24,16},{1,9},{9,1},{17,25},{25,17},{2,10},{10... | collective-permute-start | bytes 147464 | tf_op jit(solution)/shard_map/ppermute | solution.py:710
  73.0 2.0 %collective-permute-start.24 = (f32[96,128]{1,0:T(8,128)S(1)}, f32[96,128]{1,0:T(8,128)S(1)}, u32[]{:S(2)}, u32[]{:S(2)}) collective-permute-start(f32[96,128]{1,0:T(8,128)S(1)} %get-tuple-element.98), channel_id=1, source_target_pairs={{0,16},{8,24},{16,0},{24,8},{1,17},{9,25},{17,1},{25,9},{2,18},{10... | collective-permute-start | bytes 147464 | tf_op jit(solution)/shard_map/ppermute | solution.py:710
  75.4 3.4 %collective-permute-done.24.refs_6_ = f32[96,128]{1,0:T(8,128)S(1)} collective-permute-done((f32[96,128]{1,0:T(8,128)S(1)}, f32[96,128]{1,0:T(8,128)S(1)}, u32[]{:S(2)}, u32[]{:S(2)}) %collective-permute-start.24) | collective-permute-done | bytes 49184 | tf_op jit(solution)/shard_map/ppermute | solution.py:710
  78.8 2.1 %collective-permute-done.25.refs_7_ = f32[96,128]{1,0:T(8,128)S(1)} collective-permute-done((f32[96,128]{1,0:T(8,128)S(1)}, f32[96,128]{1,0:T(8,128)S(1)}, u32[]{:S(2)}, u32[]{:S(2)}) %collective-permute-start.25) | collective-permute-done | bytes 49184 | tf_op jit(solution)/shard_map/ppermute | solution.py:710
  80.9 1.8 %shard_map.92 = (bf16[4096,128]{1,0:T(8,128)(2,1)}, f32[64,128]{1,0:T(8,128)}, f32[27,64]{1,0:T(8,128)}) custom-call(bf16[16,64,128]{2,1,0:T(8,128)(2,1)S(1)} %get-tuple-element.93.refs_0_, bf16[16,64,128]{2,1,0:T(8,128)(2,1)S(1)} %get-tuple-element.94.refs_1_, bf16[16,64,128]{2,1,0:T(8,128)(2,1)S(1)} %collective-permute-done.21.refs_2_, ...), custom_call_target="tpu_custom_call" | custom-call | flops 100000000 | tf_op jit(solution)/shard_map/pallas_call | solution.py:62
  (54 shorter events, 17.2 us)
Async XLA Ops:
  2.5 2.1 %collective-permute-start = (bf16[32,64,128]{2,1,0:T(8,128)(2,1)S(1)}, bf16[32,64,128]{2,1,0:T(8,128)(2,1)S(1)}, u32[]{:S(2)}, u32[]{:S(2)}) collective-permute-start(bf16[32,64,128]{2,1,0:T(8,128)(2,1)S(1)} %get-tuple-element.55), channel_id=1, source_target_pairs={{0,1},{1,0},{2,3},{3,2},{4,5},{5,4},{6,7},{7,6},{8,9},{9,8},{10,11... | collective-permute-start | bytes 1572872 | tf_op jit(solution)/shard_map/ppermute | solution.py:694
  3.0 1.6 %collective-permute-start.1 = (bf16[64,512]{1,0:T(8,128)(2,1)S(1)}, bf16[64,512]{1,0:T(8,128)(2,1)S(1)}, u32[]{:S(2)}, u32[]{:S(2)}) collective-permute-start(bf16[64,512]{1,0:T(8,128)(2,1)S(1)} %copy-done.1), channel_id=1, source_target_pairs={{0,1},{1,0},{2,3},{3,2},{4,5},{5,4},{6,7},{7,6},{8,9},{9,8},{10,11... | collective-permute-start | bytes 196616 | tf_op jit(solution)/shard_map/ppermute | solution.py:694
  5.2 16.6 %collective-permute-start.2 = (bf16[18,128,128]{2,1,0:T(8,128)(2,1)S(1)}, bf16[18,128,128]{2,1,0:T(8,128)(2,1)S(1)}, u32[]{:S(2)}, u32[]{:S(2)}) collective-permute-start(bf16[18,128,128]{2,1,0:T(8,128)(2,1)S(1)} %get-tuple-element.57.refs_2_.refs_0_), channel_id=1, source_target_pairs={{0,4},{1,5},{2,6},{3,7},{4,0},{5,1},{6,2},{7,3},{8,12},{9,13},{10,... | collective-permute-start | bytes 1769480 | tf_op jit(solution)/shard_map/ppermute | solution.py:694
  8.1 15.1 %collective-permute-start.3 = (bf16[18,128,128]{2,1,0:T(8,128)(2,1)S(1)}, bf16[18,128,128]{2,1,0:T(8,128)(2,1)S(1)}, u32[]{:S(2)}, u32[]{:S(2)}) collective-permute-start(bf16[18,128,128]{2,1,0:T(8,128)(2,1)S(1)} %get-tuple-element.59.refs_3_.refs_6_), channel_id=1, source_target_pairs={{0,2},{1,3},{2,0},{3,1},{4,6},{5,7},{6,4},{7,5},{8,10},{9,11},{10,... | collective-permute-start | bytes 1769480 | tf_op jit(solution)/shard_map/ppermute | solution.py:694
  9.6 17.7 %collective-permute-start.4 = (bf16[16,64,128]{2,1,0:T(8,128)(2,1)S(1)}, bf16[16,64,128]{2,1,0:T(8,128)(2,1)S(1)}, u32[]{:S(2)}, u32[]{:S(2)}) collective-permute-start(bf16[16,64,128]{2,1,0:T(8,128)(2,1)S(1)} %get-tuple-element.63), channel_id=1, source_target_pairs={{0,8},{8,0},{16,24},{24,16},{1,9},{9,1},{17,25},{25,17},{2,10},{10... | collective-permute-start | bytes 786440 | tf_op jit(solution)/shard_map/ppermute | solution.py:707
  11.2 16.1 %collective-permute-start.5 = (bf16[16,64,128]{2,1,0:T(8,128)(2,1)S(1)}, bf16[16,64,128]{2,1,0:T(8,128)(2,1)S(1)}, u32[]{:S(2)}, u32[]{:S(2)}) collective-permute-start(bf16[16,64,128]{2,1,0:T(8,128)(2,1)S(1)} %get-tuple-element.64), channel_id=1, source_target_pairs={{8,16},{16,8},{9,17},{17,9},{10,18},{18,10},{11,19},{19,11},{12,20... | collective-permute-start | bytes 786440 | tf_op jit(solution)/shard_map/ppermute | solution.py:707
  15.0 15.9 %collective-permute-start.6 = (bf16[16,64,128]{2,1,0:T(8,128)(2,1)S(1)}, bf16[16,64,128]{2,1,0:T(8,128)(2,1)S(1)}, u32[]{:S(2)}, u32[]{:S(2)}) collective-permute-start(bf16[16,64,128]{2,1,0:T(8,128)(2,1)S(1)} %get-tuple-element.67), channel_id=1, source_target_pairs={{0,1},{1,0},{2,3},{3,2},{4,5},{5,4},{6,7},{7,6},{8,9},{9,8},{10,11... | collective-permute-start | bytes 786440 | tf_op jit(solution)/shard_map/ppermute | solution.py:694
  25.3 14.9 %collective-permute-start.10 = (bf16[16,128,128]{2,1,0:T(8,128)(2,1)S(1)}, bf16[16,128,128]{2,1,0:T(8,128)(2,1)S(1)}, u32[]{:S(2)}, u32[]{:S(2)}) collective-permute-start(bf16[16,128,128]{2,1,0:T(8,128)(2,1)S(1)} %get-tuple-element.72), channel_id=1, source_target_pairs={{0,2},{1,3},{2,0},{3,1},{4,6},{5,7},{6,4},{7,5},{8,10},{9,11},{10,... | collective-permute-start | bytes 1572872 | tf_op jit(solution)/shard_map/ppermute | solution.py:694
  26.8 14.9 %collective-permute-start.11 = (bf16[16,128,128]{2,1,0:T(8,128)(2,1)S(1)}, bf16[16,128,128]{2,1,0:T(8,128)(2,1)S(1)}, u32[]{:S(2)}, u32[]{:S(2)}) collective-permute-start(bf16[16,128,128]{2,1,0:T(8,128)(2,1)S(1)} %get-tuple-element.74), channel_id=1, source_target_pairs={{0,4},{1,5},{2,6},{3,7},{4,0},{5,1},{6,2},{7,3},{8,12},{9,13},{10,... | collective-permute-start | bytes 1572872 | tf_op jit(solution)/shard_map/ppermute | solution.py:694
  32.5 16.9 %collective-permute-start.8 = (bf16[16,128,128]{2,1,0:T(8,128)(2,1)S(1)}, bf16[16,128,128]{2,1,0:T(8,128)(2,1)S(1)}, u32[]{:S(2)}, u32[]{:S(2)}) collective-permute-start(bf16[16,128,128]{2,1,0:T(8,128)(2,1)S(1)} %get-tuple-element.69.refs_4_.refs_0_.refs_1_), channel_id=1, source_target_pairs={{0,2},{1,3},{2,0},{3,1},{4,6},{5,7},{6,4},{7,5},{8,10},{9,11},{10,... | collective-permute-start | bytes 1572872 | tf_op jit(solution)/shard_map/ppermute | solution.py:694
  32.9 17.7 %collective-permute-start.9 = (bf16[16,128,128]{2,1,0:T(8,128)(2,1)S(1)}, bf16[16,128,128]{2,1,0:T(8,128)(2,1)S(1)}, u32[]{:S(2)}, u32[]{:S(2)}) collective-permute-start(bf16[16,128,128]{2,1,0:T(8,128)(2,1)S(1)} %get-tuple-element.71.refs_4_), channel_id=1, source_target_pairs={{0,4},{1,5},{2,6},{3,7},{4,0},{5,1},{6,2},{7,3},{8,12},{9,13},{10,... | collective-permute-start | bytes 1572872 | tf_op jit(solution)/shard_map/ppermute | solution.py:694
  42.1 3.8 %collective-permute-start.12 = (bf16[16,64,128]{2,1,0:T(8,128)(2,1)S(1)}, bf16[16,64,128]{2,1,0:T(8,128)(2,1)S(1)}, u32[]{:S(2)}, u32[]{:S(2)}) collective-permute-start(bf16[16,64,128]{2,1,0:T(8,128)(2,1)S(1)} %get-tuple-element.76), channel_id=1, source_target_pairs={{0,1},{1,0},{2,3},{3,2},{4,5},{5,4},{6,7},{7,6},{8,9},{9,8},{10,11... | collective-permute-start | bytes 786440 | tf_op jit(solution)/shard_map/ppermute | solution.py:694
  42.1 12.9 %collective-permute-start.17 = (bf16[16,64,128]{2,1,0:T(8,128)(2,1)S(1)}, bf16[16,64,128]{2,1,0:T(8,128)(2,1)S(1)}, u32[]{:S(2)}, u32[]{:S(2)}) collective-permute-start(bf16[16,64,128]{2,1,0:T(8,128)(2,1)S(1)} %get-tuple-element.87), channel_id=1, source_target_pairs={{0,1},{1,0},{2,3},{3,2},{4,5},{5,4},{6,7},{7,6},{8,9},{9,8},{10,11... | collective-permute-start | bytes 786440 | tf_op jit(solution)/shard_map/ppermute | solution.py:694
  46.0 10.5 %collective-permute-start.18 = (bf16[16,64,128]{2,1,0:T(8,128)(2,1)S(1)}, bf16[16,64,128]{2,1,0:T(8,128)(2,1)S(1)}, u32[]{:S(2)}, u32[]{:S(2)}) collective-permute-start(bf16[16,64,128]{2,1,0:T(8,128)(2,1)S(1)} %get-tuple-element.78.refs_8_), channel_id=1, source_target_pairs={{0,8},{8,0},{16,24},{24,16},{1,9},{9,1},{17,25},{25,17},{2,10},{10... | collective-permute-start | bytes 786440 | tf_op jit(solution)/shard_map/ppermute | solution.py:707
  47.7 10.3 %collective-permute-start.19 = (bf16[16,64,128]{2,1,0:T(8,128)(2,1)S(1)}, bf16[16,64,128]{2,1,0:T(8,128)(2,1)S(1)}, u32[]{:S(2)}, u32[]{:S(2)}) collective-permute-start(bf16[16,64,128]{2,1,0:T(8,128)(2,1)S(1)} %get-tuple-element.88), channel_id=1, source_target_pairs={{8,16},{16,8},{9,17},{17,9},{10,18},{18,10},{11,19},{19,11},{12,20... | collective-permute-start | bytes 786440 | tf_op jit(solution)/shard_map/ppermute | solution.py:707
  51.9 16.4 %collective-permute-start.15 = (f32[128,256]{1,0:T(8,128)S(1)}, f32[128,256]{1,0:T(8,128)S(1)}, u32[]{:S(2)}, u32[]{:S(2)}) collective-permute-start(f32[128,256]{1,0:T(8,128)S(1)} %get-tuple-element.84), channel_id=1, source_target_pairs={{0,4},{1,5},{2,6},{3,7},{4,0},{5,1},{6,2},{7,3},{8,12},{9,13},{10,... | collective-permute-start | bytes 393224 | tf_op jit(solution)/shard_map/ppermute | solution.py:694
  52.6 15.7 %collective-permute-start.16 = (f32[128,256]{1,0:T(8,128)S(1)}, f32[128,256]{1,0:T(8,128)S(1)}, u32[]{:S(2)}, u32[]{:S(2)}) collective-permute-start(f32[128,256]{1,0:T(8,128)S(1)} %get-tuple-element.86), channel_id=1, source_target_pairs={{0,2},{1,3},{2,0},{3,1},{4,6},{5,7},{6,4},{7,5},{8,10},{9,11},{10,... | collective-permute-start | bytes 393224 | tf_op jit(solution)/shard_map/ppermute | solution.py:694
  55.1 14.8 %collective-permute-start.13 = (bf16[16,128,128]{2,1,0:T(8,128)(2,1)S(1)}, bf16[16,128,128]{2,1,0:T(8,128)(2,1)S(1)}, u32[]{:S(2)}, u32[]{:S(2)}) collective-permute-start(bf16[16,128,128]{2,1,0:T(8,128)(2,1)S(1)} %get-tuple-element.81), channel_id=1, source_target_pairs={{0,4},{1,5},{2,6},{3,7},{4,0},{5,1},{6,2},{7,3},{8,12},{9,13},{10,... | collective-permute-start | bytes 1572872 | tf_op jit(solution)/shard_map/ppermute | solution.py:694
  56.5 13.4 %collective-permute-start.14 = (bf16[16,128,128]{2,1,0:T(8,128)(2,1)S(1)}, bf16[16,128,128]{2,1,0:T(8,128)(2,1)S(1)}, u32[]{:S(2)}, u32[]{:S(2)}) collective-permute-start(bf16[16,128,128]{2,1,0:T(8,128)(2,1)S(1)} %get-tuple-element.83), channel_id=1, source_target_pairs={{0,2},{1,3},{2,0},{3,1},{4,6},{5,7},{6,4},{7,5},{8,10},{9,11},{10,... | collective-permute-start | bytes 1572872 | tf_op jit(solution)/shard_map/ppermute | solution.py:694
  70.3 10.6 %collective-permute-start.21 = (bf16[16,64,128]{2,1,0:T(8,128)(2,1)S(1)}, bf16[16,64,128]{2,1,0:T(8,128)(2,1)S(1)}, u32[]{:S(2)}, u32[]{:S(2)}) collective-permute-start(bf16[16,64,128]{2,1,0:T(8,128)(2,1)S(1)} %get-tuple-element.95), channel_id=1, source_target_pairs={{0,1},{1,0},{2,3},{3,2},{4,5},{5,4},{6,7},{7,6},{8,9},{9,8},{10,11... | collective-permute-start | bytes 786440 | tf_op jit(solution)/shard_map/ppermute | solution.py:694
  70.5 10.4 %collective-permute-start.22 = (bf16[16,64,128]{2,1,0:T(8,128)(2,1)S(1)}, bf16[16,64,128]{2,1,0:T(8,128)(2,1)S(1)}, u32[]{:S(2)}, u32[]{:S(2)}) collective-permute-start(bf16[16,64,128]{2,1,0:T(8,128)(2,1)S(1)} %get-tuple-element.96), channel_id=1, source_target_pairs={{0,1},{1,0},{2,3},{3,2},{4,5},{5,4},{6,7},{7,6},{8,9},{9,8},{10,11... | collective-permute-start | bytes 786440 | tf_op jit(solution)/shard_map/ppermute | solution.py:694
  70.8 4.6 %collective-permute-start.23 = (f32[96,128]{1,0:T(8,128)S(1)}, f32[96,128]{1,0:T(8,128)S(1)}, u32[]{:S(2)}, u32[]{:S(2)}) collective-permute-start(f32[96,128]{1,0:T(8,128)S(1)} %get-tuple-element.97), channel_id=1, source_target_pairs={{0,8},{8,0},{16,24},{24,16},{1,9},{9,1},{17,25},{25,17},{2,10},{10... | collective-permute-start | bytes 147464 | tf_op jit(solution)/shard_map/ppermute | solution.py:710
  73.0 5.7 %collective-permute-start.24 = (f32[96,128]{1,0:T(8,128)S(1)}, f32[96,128]{1,0:T(8,128)S(1)}, u32[]{:S(2)}, u32[]{:S(2)}) collective-permute-start(f32[96,128]{1,0:T(8,128)S(1)} %get-tuple-element.98), channel_id=1, source_target_pairs={{0,16},{8,24},{16,0},{24,8},{1,17},{9,25},{17,1},{25,9},{2,18},{10... | collective-permute-start | bytes 147464 | tf_op jit(solution)/shard_map/ppermute | solution.py:710
  75.0 5.9 %collective-permute-start.25 = (f32[96,128]{1,0:T(8,128)S(1)}, f32[96,128]{1,0:T(8,128)S(1)}, u32[]{:S(2)}, u32[]{:S(2)}) collective-permute-start(f32[96,128]{1,0:T(8,128)S(1)} %get-tuple-element.99), channel_id=1, source_target_pairs={{0,24},{8,16},{16,8},{24,0},{1,25},{9,17},{17,9},{25,1},{2,26},{10... | collective-permute-start | bytes 147464 | tf_op jit(solution)/shard_map/ppermute | solution.py:710
  (6 other events, 15.2 us)

commit v3 on v2

--- a/solution.py
+++ b/solution.py
@@ -9,7 +9,7 @@
 
 F32, BF16 = jnp.float32, jnp.bfloat16
 HINTS = dict(
-    inner=0.1, outer=20, back=0.1, out=0.1, filter=0.1, sums=0.1, out_sums=0.1, taps=0.1, late_taps=0.1, input=20, pack=0.1, last=0.1
+    inner=0.1, outer=0.1, back=0.1, out=0.1, sums=0.1, out_sums=0.1, taps=0.1, late_taps=0.1, input=20, pack=0.1, last=0.1, relayout=1.5
 )
 RATE = 10**9
 IN_VMEM = pl.BlockSpec(memory_space=pltpu.VMEM)
@@ -139,6 +139,7 @@
         [images.reshape(-1, width)],
         (),
         after,
+        HINTS["relayout"],
     )
 
 
@@ -160,7 +161,7 @@
                 raw_to_cells(raw, chans, store)
 
     part = shaped((half, chans, width))
-    return kernel_call(kernel, [part, part], [grad_out.reshape(-1, width)], (), after, 0.5)
+    return kernel_call(kernel, [part, part], [grad_out.reshape(-1, width)], (), after, HINTS["relayout"])
 
 
 def tap_planes(weights, spread, chans, width):
@@ -219,25 +220,24 @@
                 store(i * deep + d, r, slice(start, start + 16), both)
 
 
-def hidden_part(cells, up, down, weights, count, planes, rows, outer, after=()):
+def hidden_part(cells, near, far, weights, count, planes, rows, outer, after=()):
     _, chans, width = cells.shape
     quarter = rows // 4
-    args = [cells, up, down, weights] if outer else [cells, weights]
+    args = [cells, near, far, weights] if outer else [cells, weights]
     wanted = [r for r in range(rows) if ((r // quarter) in (0, 3)) == outer]
 
-    def kernel(cells, *refs):
-        weights, own, other, padded, spread, both = refs[-6:]
-        up, down = rims(*refs[:2]) if outer else (None, None)
+    def kernel(*refs):
+        cells = refs[0]
+        own, other, extra, both = refs[len(args) : len(args) + 4]
         core = Place(count).core
-        tap_planes(weights[...], spread, chans, width)
-        fill_window(
-            padded,
-            lambda p, r: cells[p * rows + r],
-            up,
-            down,
-            planes,
-            rows,
-        )
+        if outer:
+            padded, spread = extra, refs[3]
+            up, down = rims(*refs[1:3])
+        else:
+            padded, spread = refs[-1], extra
+            up, down = None, None
+            tap_planes(refs[1][...], spread, chans, width)
+        fill_window(padded, lambda p, r: cells[p * rows + r], up, down, planes, rows)
 
         def put(p, r, group, value):
             home, _, at = line_home(r, rows)
@@ -251,18 +251,12 @@
             other[i] = both[1 - core, i]
 
     part = shaped((planes * quarter, chans, width))
-    return kernel_call(
-        kernel,
-        [part, part],
-        args,
-        [
-            pltpu.VMEM(((planes + 2) * (rows + 2), chans, width), F32),
-            pltpu.VMEM((27, chans, width), F32),
-            pltpu.VMEM((2, planes * quarter, chans, width), BF16),
-        ],
-        after,
-        HINTS["outer" if outer else "inner"],
-    )
+    window = ((planes + 2) * (rows + 2), chans, width)
+    outs = [part, part, shaped(window if outer else (27, chans, width), F32)]
+    scratch = [pltpu.VMEM((2, planes * quarter, chans, width), BF16)]
+    if not outer:
+        scratch.append(pltpu.VMEM(window, F32))
+    return kernel_call(kernel, outs, args, scratch, after, HINTS["outer" if outer else "inner"])
 
 
 def picked(table, starts, chans):
@@ -367,7 +361,7 @@
     return [(done[o], done[o + 1 : o + 1 + sends], done[o + 1 + sends]) for _, o, _, sends, _, _ in plans]
 
 
-def summed_parts(first, second, after=(), name="sums"):
+def summed_parts(first, second, after=()):
     part, both, width = first[0].shape
     chans = both // 2
 
@@ -383,7 +377,7 @@
                 outs[n][i] = total[:chans].astype(BF16)
                 outs[2 + n][i] = total[chans:].astype(BF16)
 
-    done = kernel_call(kernel, [shaped((part, chans, width))] * 4, [*first, *second], (), after, HINTS[name])
+    done = kernel_call(kernel, [shaped((part, chans, width))] * 4, [*first, *second], (), after, HINTS["sums"])
     return done[:2], done[2:]
 
 
@@ -426,51 +420,27 @@
     return kernel_call(kernel, [shaped((part, 2 * chans, width))] * many, [*own, *arrived], (), after)
 
 
-def out_terms(parts, after=()):
-    args, outs, plans = [], [], []
-    for block, hiddens, terms in parts:
-        plans.append((len(args), len(outs), len(hiddens), terms))
-        args += [block, *hiddens]
-        outs += [shaped(hiddens[0].shape)] * terms
-    used = len(args)
-
-    def kernel(*refs):
-        for start, out, many, terms in plans:
-            part, both, width = refs[start + 1].shape
-            product_terms(
-                refs[start][...],
-                refs[start + 1 : start + 1 + many],
-                refs[used + out : used + out + terms],
-                part,
-                both,
-                width,
-            )
-
-    done = kernel_call(kernel, outs, args, (), after, micros=HINTS["out"])
-    return [done[o : o + terms] for _, o, _, terms in plans]
-
-
-def filter_terms(parts, count, after=()):
+def out_terms(parts, count, after=()):
     args, plans, outs, scratch = [], [], [], []
-    for hiddens, grads, over_mid in parts:
+    for block, hiddens, grads, over_mid in parts:
         part, both, width = hiddens[0].shape
-        chans = both // 2
+        chans, wide = both // 2, len(hiddens) * both
         plans.append((len(args), len(outs), len(hiddens), len(grads), over_mid))
-        args += [*hiddens, *grads]
-        outs += [shaped((both, len(hiddens) * both), F32)] * len(grads)
-        scratch += [
-            pltpu.VMEM((len(hiddens) * both, part * width), BF16),
-            pltpu.VMEM((len(grads) * both, part * width), BF16),
-        ]
+        args += [block, *hiddens, *grads]
+        outs += [shaped((part, both, width)), shaped((both, wide), F32)]
+        outs += [shaped((part + 2 * wide // width, both, width))] * (len(grads) - 1)
+        scratch += [pltpu.VMEM((wide, part * width), BF16), pltpu.VMEM((len(grads) * both, part * width), BF16)]
     used = len(args)
 
     def kernel(*refs):
         place = Place(count)
-        results, rooms = refs[used : used + len(outs)], refs[used + len(outs) :]
+        rooms = refs[used + len(outs) :]
         for n, (start, out, cols_of, rows_of, over_mid) in enumerate(plans):
-            hidden = refs[start : start + cols_of]
-            grad = refs[start + cols_of : start + cols_of + rows_of]
+            block, hidden = refs[start], refs[start + 1 : start + 1 + cols_of]
+            grad = refs[start + 1 + cols_of : start + 1 + cols_of + rows_of]
+            keep, gradient, *sends = refs[used + out : used + out + rows_of + 1]
             ordered, lined = rooms[2 * n], rooms[2 * n + 1]
+            product_terms(block[...], hidden, [keep, *sends], part, both, width)
             for j in range(part):
                 span = slice(j * width, (j + 1) * width)
                 for i, ref in enumerate(hidden):
@@ -482,38 +452,70 @@
                 for i, ref in enumerate(grad):
                     lined[i * both : (i + 1) * both, span] = ref[j]
             pairs = lax.dot_general(lined[...], ordered[...], (((1,), (1,)), ((), ())), preferred_element_type=F32)
-            for i in range(rows_of):
-                results[out + i][...] = pairs[i * both : (i + 1) * both]
-
-    done = kernel_call(kernel, outs, args, scratch, after, HINTS["filter"])
-    return [done[out : out + rows_of] for _, out, _, rows_of, _ in plans]
-
-
-def filter_gathered(for_hi, for_mid, count, after=()):
-    his, mids = len(for_hi), len(for_mid)
-    chans, wide = for_hi[0].shape[0] // 2, for_hi[0].shape[1]
-    pair = wide // mids
+            gradient[...] = pairs[:both]
+            slices = pairs.shape[1] // width
+            for i, send in enumerate(sends, 1):
+                value = pairs[i * both : (i + 1) * both]
+                high = value.astype(BF16)
+                low = (value - high.astype(F32)).astype(BF16)
+                for t in range(slices):
+                    send[part + t] = high[:, t * width : (t + 1) * width]
+                    send[part + slices + t] = low[:, t * width : (t + 1) * width]
+
+    done = kernel_call(kernel, outs, args, scratch, after, HINTS["out"])
+    return [
+        (done[out], done[out + 1], done[out + 2 : out + 1 + rows_of]) for _, out, _, rows_of, _ in plans
+    ]
+
+
+def out_sums(first, second, filter_first, filter_second, count, after=()):
+    part, both, width = first[0].shape
+    chans, his, mids = both // 2, len(first), len(second)
+    pair = filter_first.shape[1] // mids
 
     def kernel(*refs):
+        terms = (refs[:his], refs[his : his + mids])
+        own_rows, outs = refs[his + mids : his + mids + 2], refs[his + mids + 2 :]
+        for n in range(2):
+
+            @pl.loop(0, part)
+            def _(i):
+                total = terms[n][0][i].astype(F32)
+                for term in terms[n][1:]:
+                    total = total + term[i].astype(F32)
+                outs[n][i] = total[:chans].astype(BF16)
+                outs[2 + n][i] = total[chans:].astype(BF16)
+
         place = Place(count)
 
-        def chosen(pieces, at, mine):
-            value = pieces[0][...]
-            for n, piece in enumerate(pieces[1:], 1):
-                value = jnp.where((mine + n) % len(pieces) == at, piece[...], value)
+        def piece(n, back, columns):
+            if back == 0:
+                return own_rows[n][:, columns]
+            slices = own_rows[n].shape[1] // width
+            value = [
+                terms[n][back][part + t].astype(F32) + terms[n][back][part + slices + t].astype(F32)
+                for t in range(slices)
+            ]
+            return jnp.concatenate(value, axis=1)[:, columns]
+
+        def chosen(n, at, mine, columns):
+            value = piece(n, 0, columns)
+            for back in range(1, len(terms[n])):
+                value = jnp.where((mine + back) % len(terms[n]) == at, piece(n, back, columns), value)
             return value
 
-        by_hi = [chosen(refs[:his], hi, place.hi) for hi in range(his)]
-        by_mid = [chosen(refs[his : his + mids], mid, place.mid) for mid in range(mids)]
         for hi in range(his):
             for mid in range(mids):
-                block = by_hi[hi][:, mid * pair : (mid + 1) * pair] + by_mid[mid][:, hi * pair : (hi + 1) * pair]
+                block = chosen(0, hi, place.hi, slice(mid * pair, (mid + 1) * pair))
+                block = block + chosen(1, mid, place.mid, slice(hi * pair, (hi + 1) * pair))
                 at = (hi * mids + mid) * chans
-                refs[-2][at : at + chans] = block[:chans]
-                refs[-1][at : at + chans] = block[chans:]
-
-    out = shaped((his * mids * chans, pair), F32)
-    return kernel_call(kernel, [out, out], [*for_hi, *for_mid], (), after)
+                outs[4][at : at + chans] = block[:chans]
+                outs[5][at : at + chans] = block[chans:]
+
+    outs = [shaped((part, chans, width))] * 4 + [shaped((his * mids * chans, pair), F32)] * 2
+    args = [*first, *second, filter_first, filter_second]
+    done = kernel_call(kernel, outs, args, (), after, HINTS["out_sums"])
+    return done[:2], done[2:4], done[4], done[5]
 
 
 def slab_pieces(own, arrived, taps, slabs, after=()):
@@ -538,22 +540,21 @@
     def kernel(*refs):
         raw, filter_out, tap_out, room, sems = refs[4 + many :]
         core = Place(count).core
-        for mine in range(2):
-
-            @pl.when(core == mine)
-            def _():
-                def load(line, group):
-                    home, outer, at = line_home(line, rows)
-                    return refs[outer if home == mine else 2 + outer][at, group]
-
-                write_raw(load, raw, room, sems, chans, lines)
-
         total = refs[4][...]
         for ref in refs[5 : 4 + many]:
             total = total + ref[...]
         total = total * scale
         filter_out[...] = total[:chans]
         tap_out[...] = total[chans : chans + 27, :chans]
+        for mine in range(2):
+
+            @pl.when(core == mine)
+            def _():
+                def load(line, group):
+                    home, outer, at = line_home(line, rows)
+                    return refs[outer if home == mine else 2 + outer][at, group]
+
+                write_raw(load, raw, room, sems, chans, lines)
 
     outs = [
         shaped((chans * lines, width)),
@@ -567,21 +568,17 @@
     return raw.reshape(chans, planes, rows, width), filter_out, tap_out
 
 
-def input_gradient(own, arrived, near, far, weights, count, planes, rows, after=()):
-    _, chans, width = own[0].shape
-    quarter, lines = rows // 4, planes * rows
-
-    def kernel(*refs):
-        own, arrived = refs[:2], refs[2:4]
-        near, far, weights, raw, token, padded, spread, cells, room, sems = refs[4:]
+def input_gradient(inner, outer, near, far, spread, count, planes, rows, after=()):
+    _, _, chans, width = inner.shape
+    half, lines = rows // 2, planes * rows
+
+    def kernel(own, arrived, near, far, spread, raw, token, padded, cells, room, sems):
         core = Place(count).core
         token[...] = jnp.zeros(token.shape, F32)
-        tap_planes(weights[...], spread, chans, width)
 
         def line(p, r):
-            home, outer, at = line_home(r, rows)
-            place = p * quarter + at
-            return jnp.where(core == home, own[outer][place].astype(F32), arrived[outer][place].astype(F32))
+            home, at = r // half, r % half
+            return jnp.where(core == home, own[at, p], arrived[at, p])
 
         fill_window(padded, line, *rims(near, far), planes, rows)
 
@@ -594,10 +591,9 @@
     raw, token = kernel_call(
         kernel,
         [shaped((chans * lines, width)), shaped((8, width), F32)],
-        [*own, *arrived, near, far, weights],
+        [inner, outer, near, far, spread],
         [
             pltpu.VMEM(((planes + 2) * (rows + 2), chans, width), F32),
-            pltpu.VMEM((27, chans, width), F32),
             pltpu.VMEM((lines, chans, width), BF16),
             pltpu.VMEM((chans * lines, width), BF16),
             pltpu.SemaphoreType.DMA((chans // 16,)),
@@ -609,56 +605,52 @@
     return raw.reshape(chans, planes, rows, width), token
 
 
-def tap_sums(cells, up, down, back, before, count, planes, rows, others, wide, after=()):
-    _, chans, width = cells.shape
+def tap_sums(padded, back, before, count, planes, rows, others, wide, after=()):
+    _, chans, width = padded.shape
     half, quarter = rows // 2, rows // 4
     last = before is not None
-    args = [cells, up, down, *back] + ([before] if last else [])
-
-    def kernel(cells, near, far, inner, outside, *refs):
-        out, padded, back = refs[-3 - last : len(refs) - last]
+    args = [padded, *back] + ([before] if last else [])
+
+    def kernel(padded, inner, outside, *refs):
+        out, back = refs[-2 - last], refs[-1 - last]
         sums = refs[-1] if last else out
         core = Place(count).core
         home = 1 - core if others else core
-        fill_window(padded, lambda p, r: cells[p * rows + r], *rims(near, far), planes, rows)
         sums[...] = refs[0][...] if last else jnp.zeros(sums.shape, F32)
         lane = lax.broadcasted_iota(jnp.int32, (8, width), 1)
         deep = max(1, 4 // half)
 
-        @pl.loop(0, planes * quarter)
-        def _(i):
-            back[0, i] = jnp.where(home == 0, outside[i].astype(F32), inner[i].astype(F32))
-            back[1, i] = jnp.where(home == 0, inner[i].astype(F32), outside[i].astype(F32))
+        @pl.loop(0, planes)
+        def _(p):
+            for r in range(quarter):
+                i = p * quarter + r
+                back[r, p] = jnp.where(home == 0, outside[i].astype(F32), inner[i].astype(F32))
+                back[quarter + r, p] = jnp.where(home == 0, inner[i].astype(F32), outside[i].astype(F32))
 
         @pl.loop(0, planes // deep)
         def _(i):
-            for pair in range(0, chans, 16):
-                both = {}
+            for start in range(0, chans, 8):
+                group = slice(start, start + 8)
+                moved = {}
                 for d in range(deep):
                     for r in range(half):
-                        place = (i * deep + d) * quarter + r % quarter
-                        both[d, r] = back[r // quarter, place, pair : pair + 16]
-                for n in range(2):
-                    group = slice(pair + 8 * n, pair + 8 * n + 8)
-                    moved = {}
-                    for key, value in both.items():
-                        here = value[8 * n : 8 * n + 8]
+                        here = back[r, i * deep + d, group]
                         later = jnp.where(lane == width - 1, 0.0, pltpu.roll(here, width - 1, 1))
                         earlier = jnp.where(lane == 0, 0.0, pltpu.roll(here, 1, 1))
-                        moved[key] = (later, here, earlier)
-                    for a in range(3):
-                        images = {}
-                        for d in range(deep):
-                            base = (i * deep + d + a) * (rows + 2) + home * half
-                            for line in range(half + 2):
-                                images[d, line] = padded[base + line, group]
-                        for b in range(3):
-                            for e in range(3):
-                                term = None
-                                for (d, r), values in moved.items():
-                                    product = images[d, r + b] * values[e]
-                                    term = product if term is None else term + product
-                                sums[9 * a + 3 * b + e, group] += term
+                        moved[d, r] = (later, here, earlier)
+                for a in range(3):
+                    images = {}
+                    for d in range(deep):
+                        base = (i * deep + d + a) * (rows + 2) + home * half
+                        for line in range(half + 2):
+                            images[d, line] = padded[base + line, group]
+                    for b in range(3):
+                        for e in range(3):
+                            term = None
+                            for (d, r), values in moved.items():
+                                product = images[d, r + b] * values[e]
+                                term = product if term is None else term + product
+                            sums[9 * a + 3 * b + e, group] += term
 
         if last:
             row = lax.broadcasted_iota(jnp.int32, (chans, wide), 0)
@@ -669,14 +661,9 @@
             out[27:] = jnp.zeros((5, wide), F32)
 
     running = (27, chans, width)
-    scratch = [
-        pltpu.VMEM(((planes + 2) * (rows + 2), chans, width), F32),
-        pltpu.VMEM((2, planes * quarter, chans, width), F32),
-    ]
-    if last:
-        scratch.append(pltpu.VMEM(running, F32))
-    outs = [shaped((32, wide) if last else running, F32)]
-    return kernel_call(kernel, outs, args, scratch, after, HINTS["late_taps" if last else "taps"])[0]
+    scratch = [pltpu.VMEM(running, F32)] if last else []
+    outs = [shaped((32, wide) if last else running, F32), shaped((half, planes, chans, width), F32)]
+    return kernel_call(kernel, outs, args, scratch, after, HINTS["late_taps" if last else "taps"])
 
 
 def body(images, depth_filter, point_filter, grad_out):
@@ -712,7 +699,7 @@
     filter_arrived = to_core(point_filter)
     grad_own, grad_other = relayout_grad(grad_out, count)
     grad_arrived = to_core(grad_other)
-    cells, near, far = relayout_images(images, [grad_own])
+    cells, near, far = relayout_images(images, [grad_own, filter_arrived])
     image_rims = halo(near, far)
     to_hi, to_mid, filter_hi, filter_mid = pack_grad(
         grad_own, grad_arrived, point_filter, filter_arrived, count, [cells]
@@ -722,43 +709,41 @@
 
     windows = (cells, *image_rims)
     plan = (count, planes, rows)
-    inner_own, inner_other = hidden_part(*windows, depth_filter, *plan, False, [to_hi[0]])
+    inner_own, inner_other, spread = hidden_part(*windows, depth_filter, *plan, False, [to_hi[0]])
     inner_arrived = to_core(inner_other)
-    (keep_first, send_first, block_first), (keep_second, send_second, block_second) = back_terms(
-        [(to_hi[0], grads_hi, filter_hi, mids - 1), (to_mid[0], grads_mid, filter_mid, his - 1)], [inner_own]
-    )
-    back_first = [keep_first] + [along_mid(value, -t) for t, value in enumerate(send_first, 1)]
-    back_second = [keep_second] + [along_hi(value, -s) for s, value in enumerate(send_second, 1)]
-
-    outer_own, outer_other = hidden_part(*windows, depth_filter, *plan, True, [keep_first])
+    outer_own, outer_other, padded = hidden_part(*windows, spread, *plan, True, [inner_own])
     outer_arrived = to_core(outer_other)
     hidden_first, hidden_second = joined([inner_own, outer_own], [inner_arrived, outer_arrived])
     hiddens_mid = [hidden_first] + [along_mid(hidden_first, t) for t in range(1, mids)]
     hiddens_hi = [hidden_second] + [along_hi(hidden_second, s) for s in range(1, his)]
 
-    back_own, back_other = summed_parts(back_first, back_second, [hidden_first])
+    (keep_first, send_first, block_first), (keep_second, send_second, block_second) = back_terms(
+        [(to_hi[0], grads_hi, filter_hi, mids - 1), (to_mid[0], grads_mid, filter_mid, his - 1)], [hidden_first]
+    )
+    back_first = [keep_first] + [along_mid(value, -t) for t, value in enumerate(send_first, 1)]
+    back_second = [keep_second] + [along_hi(value, -s) for s, value in enumerate(send_second, 1)]
+
+    (out_first, pg_first, send_first), (out_second, pg_second, send_second) = out_terms(
+        [
+            (block_first, hiddens_mid, [to_hi[0], *grads_hi], True),
+            (block_second, hiddens_hi, [to_mid[0], *grads_mid], False),
+        ],
+        count,
+        [keep_first],
+    )
+    latest = out_first
+    out_first = [out_first] + [along_hi(value, -s) for s, value in enumerate(send_first, 1)]
+    out_second = [out_second] + [along_mid(value, -t) for t, value in enumerate(send_second, 1)]
+
+    back_own, back_other = summed_parts(back_first, back_second, [latest])
     back_arrived = [to_core(value) for value in back_other]
     wide = his * mids * 2 * chans // slabs
-    taps = tap_sums(*windows, back_own, None, *plan, False, wide, [back_own[0]])
+    taps, back_own_lines = tap_sums(padded, back_own, None, *plan, False, wide)
     edges = edge_rows(back_own[1], back_arrived[1], count, rows, [taps])
     back_rims = halo(*edges)
-
-    for_hi, for_mid = filter_terms(
-        [(hiddens_mid, [to_hi[0], *grads_hi], True), (hiddens_hi, [to_mid[0], *grads_mid], False)], count, [edges[0]]
-    )
-    owned = for_hi[0]
-    for_hi = [for_hi[0]] + [along_hi(piece, -s) for s, piece in enumerate(for_hi[1:], 1)]
-    for_mid = [for_mid[0]] + [along_mid(piece, -t) for t, piece in enumerate(for_mid[1:], 1)]
-    out_first, out_second = out_terms(
-        [(block_first, hiddens_mid, his), (block_second, hiddens_hi, mids)], [owned]
-    )
-    latest = out_first[0]
-    out_first = [out_first[0]] + [along_hi(value, -s) for s, value in enumerate(out_first[1:], 1)]
-    out_second = [out_second[0]] + [along_mid(value, -t) for t, value in enumerate(out_second[1:], 1)]
-
-    input_grad, latest = input_gradient(back_own, back_arrived, *back_rims, depth_filter, *plan, [latest])
-    taps = tap_sums(*windows, back_arrived, taps, *plan, True, wide, [latest])
-    own, other = filter_gathered(for_hi, for_mid, count, [taps])
+    taps, back_arrived_lines = tap_sums(padded, back_arrived, taps, *plan, True, wide, [edges[0]])
+    out_own, out_other, own, other = out_sums(out_first, out_second, pg_first, pg_second, count, [taps])
+    out_arrived = [to_core(value) for value in out_other]
     chip_arrived = to_core(other)
     if own.shape[1] != wide:
 
@@ -768,11 +753,9 @@
 
         own, chip_arrived = by_slab(own), by_slab(chip_arrived)
     pieces = slab_pieces(own, chip_arrived, taps, slabs)
-    latest = pieces[0]
+    input_grad, latest = input_gradient(back_own_lines, back_arrived_lines, *back_rims, spread, *plan, [pieces[0]])
     pieces = [pieces[0]] + [exchanged(piece, apart) for apart, piece in enumerate(pieces[1:], 1)]
-    out_own, out_other = summed_parts(out_first, out_second, [latest], "out_sums")
-    out_arrived = [to_core(value) for value in out_other]
-    block_out, point_grad, depth_grad = last_outputs(out_own, out_arrived, pieces, *plan, grad_scale)
+    block_out, point_grad, depth_grad = last_outputs(out_own, out_arrived, pieces, *plan, grad_scale, [latest])
     return block_out, point_grad, input_grad, depth_grad
 
 

time: 82.9 us -> 78.7 us (0.949)
  waiting for transfers between devices: 26.6 us -> 21.1 us
  starting transfers between devices: 24.1 us -> 27.8 us
  Pallas kernels: 29.9 us -> 27.5 us
    ppermute x3, waiting for transfers between devices: 5.51 us -> 0.01 us  [exchanged(): return lax.ppermute(value, 'space', [(i, i ^ apart) for i in range(slabs)])]
    ppermute x2, starting transfers between devices: 3.22 us -> 8.72 us  [halo(): lax.ppermute(near, 'space', swaps[0])]
    ppermute x19 -> x17, starting transfers between devices: 15 us -> 12.2 us  [moved(): return lax.ppermute(value, 'chan', pairs)]
    pallas_call x18 -> x16, Pallas kernels: 29.9 us -> 27.5 us  [kernel_call(): pl.pallas_call(run, out_shape=outs, in_specs=[IN_VMEM] * used + [ANYWHERE...]
    ppermute x3, starting transfers between devices: 4.56 us -> 5.5 us  [exchanged(): return lax.ppermute(value, 'space', [(i, i ^ apart) for i in range(slabs)])]
    ppermute x19 -> x17, waiting for transfers between devices: 21.1 us -> 21.1 us  [moved(): return lax.ppermute(value, 'chan', pairs)]
  transfers between devices with their start and end apart: 26 -> 24, of which waited for: 11 -> 8; matrix products, arithmetic and copies ran while one was open for 0% -> 0% of each run, Pallas kernels for 32% -> 32%
where the time goes in v3:
time: 78.7 us; the launch traced here: 78.5 us
  starting transfers between devices  27.8 us (35%)
  Pallas kernels  27.5 us (35%)
  waiting for transfers between devices  21.1 us (27%)
  local copies, waits for them, and re-layouts  1.26 us (2%)
  between operations  0.9 us (1%)
    pallas_call x16, Pallas kernels, kernel_call(): pl.pallas_call(run, out_shape=outs, in_specs=[IN_VMEM] * used + [ANYWHERE...  27.5 us
    ppermute x17, waiting for transfers between devices, moved(): return lax.ppermute(value, 'chan', pairs)  21.1 us
    ppermute x17, starting transfers between devices, moved(): return lax.ppermute(value, 'chan', pairs)  12.2 us
    ppermute x2, starting transfers between devices, halo(): lax.ppermute(near, 'space', swaps[0])  8.72 us
    ppermute x3, starting transfers between devices, exchanged(): return lax.ppermute(value, 'space', [(i, i ^ apart) for i in range(slabs)])  5.5 us
  transfers between devices with their start and end apart: 24, of which 8 were waited for; matrix products, arithmetic and copies ran while one was open for 0% of the time, Pallas kernels for 32%

profile of v3, /device:TPU:0, one launch (start us, length us, event | category | flops | bytes accessed | tf_op | source)
XLA Modules:
  0.0 78.5 jit_solution(15057166700567464887)
XLA Ops:
  0.7 1.2 %copy-done.2 = bf16[64,16,4,128]{3,2,1,0:T(4,128)(2,1)S(1)} copy-done((bf16[64,16,4,128]{3,2,1,0:T(4,128)(2,1)S(1)}, bf16[64,16,4,128]{3,2,1,0:T(4,128)(2,1)}, u32[]{:S(2)}) %copy-start.2) | copy-done | bytes 1048600
  3.0 1.5 %collective-permute-done.1.refs_2_.refs_3_ = bf16[64,512]{1,0:T(8,128)(2,1)S(1)} collective-permute-done((bf16[64,512]{1,0:T(8,128)(2,1)S(1)}, bf16[64,512]{1,0:T(8,128)(2,1)S(1)}, u32[]{:S(2)}, u32[]{:S(2)}) %collective-permute-start.1) | collective-permute-done | bytes 65568 | tf_op jit(solution)/shard_map/ppermute | solution.py:681
  5.1 3.0 %collective-permute-start.4 = (bf16[16,64,128]{2,1,0:T(8,128)(2,1)S(1)}, bf16[16,64,128]{2,1,0:T(8,128)(2,1)S(1)}, u32[]{:S(2)}, u32[]{:S(2)}) collective-permute-start(bf16[16,64,128]{2,1,0:T(8,128)(2,1)S(1)} %get-tuple-element.66), channel_id=1, source_target_pairs={{0,8},{8,0},{16,24},{24,16},{1,9},{9,1},{17,25},{25,17},{2,10},{10... | collective-permute-start | bytes 786440 | tf_op jit(solution)/shard_map/ppermute | solution.py:694
  9.4 1.6 %collective-permute-start.3 = (bf16[18,128,128]{2,1,0:T(8,128)(2,1)S(1)}, bf16[18,128,128]{2,1,0:T(8,128)(2,1)S(1)}, u32[]{:S(2)}, u32[]{:S(2)}) collective-permute-start(bf16[18,128,128]{2,1,0:T(8,128)(2,1)S(1)} %get-tuple-element.63.refs_3_.refs_8_), channel_id=1, source_target_pairs={{0,2},{1,3},{2,0},{3,1},{4,6},{5,7},{6,4},{7,5},{8,10},{9,11},{10,... | collective-permute-start | bytes 1769480 | tf_op jit(solution)/shard_map/ppermute | solution.py:681
  11.0 1.5 %collective-permute-start.2 = (bf16[18,128,128]{2,1,0:T(8,128)(2,1)S(1)}, bf16[18,128,128]{2,1,0:T(8,128)(2,1)S(1)}, u32[]{:S(2)}, u32[]{:S(2)}) collective-permute-start(bf16[18,128,128]{2,1,0:T(8,128)(2,1)S(1)} %get-tuple-element.61.refs_2_.refs_0_.refs_3_), channel_id=1, source_target_pairs={{0,4},{1,5},{2,6},{3,7},{4,0},{5,1},{6,2},{7,3},{8,12},{9,13},{10,... | collective-permute-start | bytes 1769480 | tf_op jit(solution)/shard_map/ppermute | solution.py:681
  12.5 2.8 %shard_map.78 = (bf16[16,64,128]{2,1,0:T(8,128)(2,1)S(1)}, bf16[16,64,128]{2,1,0:T(8,128)(2,1)S(1)}, f32[27,64,128]{2,1,0:T(8,128)S(1)}) custom-call(bf16[64,64,128]{2,1,0:T(8,128)(2,1)S(1)} %get-tuple-element.60.refs_4_.refs_0_, f32[27,64]{1,0:T(8,128)S(1)} %copy-done.1, bf16[18,128,128]{2,1,0:T(8,128)(2,1)S(1)} %get-tuple-element.61.refs_2_.refs_0_.refs_3_), custom_call_target="tpu_custom_call" | custom-call | flops 100000000 | tf_op jit(solution)/shard_map/pallas_call | solution.py:62
  15.5 2.7 %shard_map.79 = (bf16[16,64,128]{2,1,0:T(8,128)(2,1)S(1)}, bf16[16,64,128]{2,1,0:T(8,128)(2,1)S(1)}, f32[108,64,128]{2,1,0:T(8,128)S(1)}) custom-call(bf16[64,64,128]{2,1,0:T(8,128)(2,1)S(1)} %get-tuple-element.60.refs_4_.refs_0_, bf16[16,64,128]{2,1,0:T(8,128)(2,1)S(1)} %collective-permute-done.4.refs_1_, ...), custom_call_target="tpu_custom_call" | custom-call | flops 100000000 | tf_op jit(solution)/shard_map/pallas_call | solution.py:62
  21.0 1.5 %collective-permute-start.8 = (bf16[16,128,128]{2,1,0:T(8,128)(2,1)S(1)}, bf16[16,128,128]{2,1,0:T(8,128)(2,1)S(1)}, u32[]{:S(2)}, u32[]{:S(2)}) collective-permute-start(bf16[16,128,128]{2,1,0:T(8,128)(2,1)S(1)} %get-tuple-element.72.refs_6_.refs_1_), channel_id=1, source_target_pairs={{0,2},{1,3},{2,0},{3,1},{4,6},{5,7},{6,4},{7,5},{8,10},{9,11},{10,... | collective-permute-start | bytes 1572872 | tf_op jit(solution)/shard_map/ppermute | solution.py:681
  22.5 3.2 %collective-permute-done.3.refs_5_.refs_9_ = bf16[18,128,128]{2,1,0:T(8,128)(2,1)S(1)} collective-permute-done((bf16[18,128,128]{2,1,0:T(8,128)(2,1)S(1)}, bf16[18,128,128]{2,1,0:T(8,128)(2,1)S(1)}, u32[]{:S(2)}, u32[]{:S(2)}) %collective-permute-start.3) | collective-permute-done | bytes 589856 | tf_op jit(solution)/shard_map/ppermute | solution.py:681
  25.7 1.5 %collective-permute-done.2.refs_2_.refs_4_ = bf16[18,128,128]{2,1,0:T(8,128)(2,1)S(1)} collective-permute-done((bf16[18,128,128]{2,1,0:T(8,128)(2,1)S(1)}, bf16[18,128,128]{2,1,0:T(8,128)(2,1)S(1)}, u32[]{:S(2)}, u32[]{:S(2)}) %collective-permute-start.2) | collective-permute-done | bytes 589856 | tf_op jit(solution)/shard_map/ppermute | solution.py:681
  27.2 2.0 %shard_map.81 = (bf16[16,128,128]{2,1,0:T(8,128)(2,1)S(1)}, bf16[16,128,128]{2,1,0:T(8,128)(2,1)S(1)}, bf16[256,256]{1,0:T(8,128)(2,1)S(1)}, bf16[16,128,128]{2,...) custom-call(bf16[18,128,128]{2,1,0:T(8,128)(2,1)S(1)} %get-tuple-element.61.refs_2_.refs_0_.refs_3_, ...), custom_call_target="tpu_custom_call" | custom-call | flops 100000000 | tf_op jit(solution)/shard_map/pallas_call | solution.py:62
  29.9 1.5 %collective-permute-start.13 = (bf16[16,128,128]{2,1,0:T(8,128)(2,1)S(1)}, bf16[16,128,128]{2,1,0:T(8,128)(2,1)S(1)}, u32[]{:S(2)}, u32[]{:S(2)}) collective-permute-start(bf16[16,128,128]{2,1,0:T(8,128)(2,1)S(1)} %get-tuple-element.86), channel_id=1, source_target_pairs={{0,4},{1,5},{2,6},{3,7},{4,0},{5,1},{6,2},{7,3},{8,12},{9,13},{10,... | collective-permute-start | bytes 1572872 | tf_op jit(solution)/shard_map/ppermute | solution.py:681
  31.4 7.1 %collective-permute-done.9.refs_7_ = bf16[16,128,128]{2,1,0:T(8,128)(2,1)S(1)} collective-permute-done((bf16[16,128,128]{2,1,0:T(8,128)(2,1)S(1)}, bf16[16,128,128]{2,1,0:T(8,128)(2,1)S(1)}, u32[]{:S(2)}, u32[]{:S(2)}) %collective-permute-start.9) | collective-permute-done | bytes 524320 | tf_op jit(solution)/shard_map/ppermute | solution.py:681
  38.5 3.4 %shard_map.82 = (bf16[16,128,128]{2,1,0:T(8,128)(2,1)S(1)}, f32[128,256]{1,0:T(8,128)S(1)}, bf16[20,128,128]{2,1,0:T(8,128)(2,1)S(1)}, bf16[16,128,128]{2,1,0:T(...) custom-call(bf16[256,256]{1,0:T(8,128)(2,1)S(1)} %get-tuple-element.73.refs_0_, ...), custom_call_target="tpu_custom_call" | custom-call | flops 100000000 | tf_op jit(solution)/shard_map/pallas_call | solution.py:62
  41.8 1.6 %collective-permute-start.10 = (bf16[20,128,128]{2,1,0:T(8,128)(2,1)S(1)}, bf16[20,128,128]{2,1,0:T(8,128)(2,1)S(1)}, u32[]{:S(2)}, u32[]{:S(2)}) collective-permute-start(bf16[20,128,128]{2,1,0:T(8,128)(2,1)S(1)} %get-tuple-element.78), channel_id=1, source_target_pairs={{0,4},{1,5},{2,6},{3,7},{4,0},{5,1},{6,2},{7,3},{8,12},{9,13},{10,... | collective-permute-start | bytes 1966088 | tf_op jit(solution)/shard_map/ppermute | solution.py:681
  44.0 4.2 %collective-permute-done.12.refs_1_ = bf16[16,128,128]{2,1,0:T(8,128)(2,1)S(1)} collective-permute-done((bf16[16,128,128]{2,1,0:T(8,128)(2,1)S(1)}, bf16[16,128,128]{2,1,0:T(8,128)(2,1)S(1)}, u32[]{:S(2)}, u32[]{:S(2)}) %collective-permute-start.12) | collective-permute-done | bytes 524320 | tf_op jit(solution)/shard_map/ppermute | solution.py:681
  48.2 1.5 %collective-permute-done.13.refs_3_ = bf16[16,128,128]{2,1,0:T(8,128)(2,1)S(1)} collective-permute-done((bf16[16,128,128]{2,1,0:T(8,128)(2,1)S(1)}, bf16[16,128,128]{2,1,0:T(8,128)(2,1)S(1)}, u32[]{:S(2)}, u32[]{:S(2)}) %collective-permute-start.13) | collective-permute-done | bytes 524320 | tf_op jit(solution)/shard_map/ppermute | solution.py:681
  50.7 2.9 %shard_map.84 = (f32[27,64,128]{2,1,0:T(8,128)S(1)}, f32[2,16,64,128]{3,2,1,0:T(8,128)S(1)}) custom-call(f32[108,64,128]{2,1,0:T(8,128)S(1)} %get-tuple-element.83.refs_0_, bf16[16,64,128]{2,1,0:T(8,128)(2,1)S(1)} %get-tuple-element.89.refs_1_, bf16[16,64,128]{2,1,0:T(8,128)(2,1)S(1)} %get-tuple-element.90.refs_2_.refs_0_), custom_call_target="tpu_custom_call" | custom-call | flops 100000000 | tf_op jit(solution)/shard_map/pallas_call | solution.py:62
  54.5 5.7 %collective-permute-start.22 = (bf16[16,64,128]{2,1,0:T(8,128)(2,1)S(1)}, bf16[16,64,128]{2,1,0:T(8,128)(2,1)S(1)}, u32[]{:S(2)}, u32[]{:S(2)}) collective-permute-start(bf16[16,64,128]{2,1,0:T(8,128)(2,1)S(1)} %get-tuple-element.92.refs_4_), channel_id=1, source_target_pairs={{0,8},{8,0},{16,24},{24,16},{1,9},{9,1},{17,25},{25,17},{2,10},{10... | collective-permute-start | bytes 786440 | tf_op jit(solution)/shard_map/ppermute | solution.py:694
  60.2 3.2 %shard_map.86 = (f32[32,128]{1,0:T(8,128)S(1)}, f32[2,16,64,128]{3,2,1,0:T(8,128)S(1)}) custom-call(f32[108,64,128]{2,1,0:T(8,128)S(1)} %get-tuple-element.83.refs_0_, bf16[16,64,128]{2,1,0:T(8,128)(2,1)S(1)} %collective-permute-done.14.refs_1_, bf16[16,64,128]{2,1,0:T(8,128)(2,1)S(1)} %collective-permute-done.15.refs_1_.refs_2_, ...), custom_call_target="tpu_custom_call" | custom-call | flops 100000000 | tf_op jit(solution)/shard_map/pallas_call | solution.py:62
  65.3 3.0 %collective-permute-start.19 = (f32[96,128]{1,0:T(8,128)S(1)}, f32[96,128]{1,0:T(8,128)S(1)}, u32[]{:S(2)}, u32[]{:S(2)}) collective-permute-start(f32[96,128]{1,0:T(8,128)S(1)} %get-tuple-element.101), channel_id=1, source_target_pairs={{0,8},{8,0},{16,24},{24,16},{1,9},{9,1},{17,25},{25,17},{2,10},{10... | collective-permute-start | bytes 147464 | tf_op jit(solution)/shard_map/ppermute | solution.py:697
  68.9 2.0 %collective-permute-start.21 = (f32[96,128]{1,0:T(8,128)S(1)}, f32[96,128]{1,0:T(8,128)S(1)}, u32[]{:S(2)}, u32[]{:S(2)}) collective-permute-start(f32[96,128]{1,0:T(8,128)S(1)} %get-tuple-element.103), channel_id=1, source_target_pairs={{0,24},{8,16},{16,8},{24,0},{1,25},{9,17},{17,9},{25,1},{2,26},{10... | collective-permute-start | bytes 147464 | tf_op jit(solution)/shard_map/ppermute | solution.py:697
  70.8 5.8 %shard_map.89 = (bf16[4096,128]{1,0:T(8,128)(2,1)}, f32[8,128]{1,0:T(8,128)S(1)}) custom-call(f32[2,16,64,128]{3,2,1,0:T(8,128)S(1)} %get-tuple-element.104.refs_0_, f32[2,16,64,128]{3,2,1,0:T(8,128)S(1)} %get-tuple-element.105.refs_1_, bf16[16,64,128]{2,1,0:T(8,128)(2,1)S(1)} %collective-permute-done.22.refs_2_, ...), custom_call_target="tpu_custom_call" | custom-call | flops 20000000000 | tf_op jit(solution)/shard_map/pallas_call | solution.py:62
  76.7 1.8 %shard_map.90 = (bf16[4096,128]{1,0:T(8,128)(2,1)}, f32[64,128]{1,0:T(8,128)}, f32[27,64]{1,0:T(8,128)}) custom-call(bf16[16,64,128]{2,1,0:T(8,128)(2,1)S(1)} %get-tuple-element.94.refs_0_, bf16[16,64,128]{2,1,0:T(8,128)(2,1)S(1)} %get-tuple-element.95.refs_1_, bf16[16,64,128]{2,1,0:T(8,128)(2,1)S(1)} %collective-permute-done.16.refs_2_, ...), custom_call_target="tpu_custom_call" | custom-call | flops 100000000 | tf_op jit(solution)/shard_map/pallas_call | solution.py:62
  (48 shorter events, 11.1 us)
Async XLA Ops:
  2.4 6.4 %collective-permute-start = (bf16[32,64,128]{2,1,0:T(8,128)(2,1)S(1)}, bf16[32,64,128]{2,1,0:T(8,128)(2,1)S(1)}, u32[]{:S(2)}, u32[]{:S(2)}) collective-permute-start(bf16[32,64,128]{2,1,0:T(8,128)(2,1)S(1)} %get-tuple-element.59), channel_id=1, source_target_pairs={{0,1},{1,0},{2,3},{3,2},{4,5},{5,4},{6,7},{7,6},{8,9},{9,8},{10,11... | collective-permute-start | bytes 1572872 | tf_op jit(solution)/shard_map/ppermute | solution.py:681
  2.9 1.6 %collective-permute-start.1 = (bf16[64,512]{1,0:T(8,128)(2,1)S(1)}, bf16[64,512]{1,0:T(8,128)(2,1)S(1)}, u32[]{:S(2)}, u32[]{:S(2)}) collective-permute-start(bf16[64,512]{1,0:T(8,128)(2,1)S(1)} %copy-done), channel_id=1, source_target_pairs={{0,1},{1,0},{2,3},{3,2},{4,5},{5,4},{6,7},{7,6},{8,9},{9,8},{10,11... | collective-permute-start | bytes 196616 | tf_op jit(solution)/shard_map/ppermute | solution.py:681
  5.1 10.3 %collective-permute-start.4 = (bf16[16,64,128]{2,1,0:T(8,128)(2,1)S(1)}, bf16[16,64,128]{2,1,0:T(8,128)(2,1)S(1)}, u32[]{:S(2)}, u32[]{:S(2)}) collective-permute-start(bf16[16,64,128]{2,1,0:T(8,128)(2,1)S(1)} %get-tuple-element.66), channel_id=1, source_target_pairs={{0,8},{8,0},{16,24},{24,16},{1,9},{9,1},{17,25},{25,17},{2,10},{10... | collective-permute-start | bytes 786440 | tf_op jit(solution)/shard_map/ppermute | solution.py:694
  8.2 7.3 %collective-permute-start.5 = (bf16[16,64,128]{2,1,0:T(8,128)(2,1)S(1)}, bf16[16,64,128]{2,1,0:T(8,128)(2,1)S(1)}, u32[]{:S(2)}, u32[]{:S(2)}) collective-permute-start(bf16[16,64,128]{2,1,0:T(8,128)(2,1)S(1)} %get-tuple-element.67), channel_id=1, source_target_pairs={{8,16},{16,8},{9,17},{17,9},{10,18},{18,10},{11,19},{19,11},{12,20... | collective-permute-start | bytes 786440 | tf_op jit(solution)/shard_map/ppermute | solution.py:694
  9.4 16.3 %collective-permute-start.3 = (bf16[18,128,128]{2,1,0:T(8,128)(2,1)S(1)}, bf16[18,128,128]{2,1,0:T(8,128)(2,1)S(1)}, u32[]{:S(2)}, u32[]{:S(2)}) collective-permute-start(bf16[18,128,128]{2,1,0:T(8,128)(2,1)S(1)} %get-tuple-element.63.refs_3_.refs_8_), channel_id=1, source_target_pairs={{0,2},{1,3},{2,0},{3,1},{4,6},{5,7},{6,4},{7,5},{8,10},{9,11},{10,... | collective-permute-start | bytes 1769480 | tf_op jit(solution)/shard_map/ppermute | solution.py:681
  11.0 16.3 %collective-permute-start.2 = (bf16[18,128,128]{2,1,0:T(8,128)(2,1)S(1)}, bf16[18,128,128]{2,1,0:T(8,128)(2,1)S(1)}, u32[]{:S(2)}, u32[]{:S(2)}) collective-permute-start(bf16[18,128,128]{2,1,0:T(8,128)(2,1)S(1)} %get-tuple-element.61.refs_2_.refs_0_.refs_3_), channel_id=1, source_target_pairs={{0,4},{1,5},{2,6},{3,7},{4,0},{5,1},{6,2},{7,3},{8,12},{9,13},{10,... | collective-permute-start | bytes 1769480 | tf_op jit(solution)/shard_map/ppermute | solution.py:681
  15.4 3.4 %collective-permute-start.6 = (bf16[16,64,128]{2,1,0:T(8,128)(2,1)S(1)}, bf16[16,64,128]{2,1,0:T(8,128)(2,1)S(1)}, u32[]{:S(2)}, u32[]{:S(2)}) collective-permute-start(bf16[16,64,128]{2,1,0:T(8,128)(2,1)S(1)} %get-tuple-element.70), channel_id=1, source_target_pairs={{0,1},{1,0},{2,3},{3,2},{4,5},{5,4},{6,7},{7,6},{8,9},{9,8},{10,11... | collective-permute-start | bytes 786440 | tf_op jit(solution)/shard_map/ppermute | solution.py:681
  18.2 1.7 %collective-permute-start.7 = (bf16[16,64,128]{2,1,0:T(8,128)(2,1)S(1)}, bf16[16,64,128]{2,1,0:T(8,128)(2,1)S(1)}, u32[]{:S(2)}, u32[]{:S(2)}) collective-permute-start(bf16[16,64,128]{2,1,0:T(8,128)(2,1)S(1)} %get-tuple-element.71), channel_id=1, source_target_pairs={{0,1},{1,0},{2,3},{3,2},{4,5},{5,4},{6,7},{7,6},{8,9},{9,8},{10,11... | collective-permute-start | bytes 786440 | tf_op jit(solution)/shard_map/ppermute | solution.py:681
  20.0 18.5 %collective-permute-start.9 = (bf16[16,128,128]{2,1,0:T(8,128)(2,1)S(1)}, bf16[16,128,128]{2,1,0:T(8,128)(2,1)S(1)}, u32[]{:S(2)}, u32[]{:S(2)}) collective-permute-start(bf16[16,128,128]{2,1,0:T(8,128)(2,1)S(1)} %get-tuple-element.75.refs_6_), channel_id=1, source_target_pairs={{0,4},{1,5},{2,6},{3,7},{4,0},{5,1},{6,2},{7,3},{8,12},{9,13},{10,... | collective-permute-start | bytes 1572872 | tf_op jit(solution)/shard_map/ppermute | solution.py:681
  21.0 17.5 %collective-permute-start.8 = (bf16[16,128,128]{2,1,0:T(8,128)(2,1)S(1)}, bf16[16,128,128]{2,1,0:T(8,128)(2,1)S(1)}, u32[]{:S(2)}, u32[]{:S(2)}) collective-permute-start(bf16[16,128,128]{2,1,0:T(8,128)(2,1)S(1)} %get-tuple-element.72.refs_6_.refs_1_), channel_id=1, source_target_pairs={{0,2},{1,3},{2,0},{3,1},{4,6},{5,7},{6,4},{7,5},{8,10},{9,11},{10,... | collective-permute-start | bytes 1572872 | tf_op jit(solution)/shard_map/ppermute | solution.py:681
  29.3 18.9 %collective-permute-start.12 = (bf16[16,128,128]{2,1,0:T(8,128)(2,1)S(1)}, bf16[16,128,128]{2,1,0:T(8,128)(2,1)S(1)}, u32[]{:S(2)}, u32[]{:S(2)}) collective-permute-start(bf16[16,128,128]{2,1,0:T(8,128)(2,1)S(1)} %get-tuple-element.84), channel_id=1, source_target_pairs={{0,2},{1,3},{2,0},{3,1},{4,6},{5,7},{6,4},{7,5},{8,10},{9,11},{10,... | collective-permute-start | bytes 1572872 | tf_op jit(solution)/shard_map/ppermute | solution.py:681
  29.9 19.8 %collective-permute-start.13 = (bf16[16,128,128]{2,1,0:T(8,128)(2,1)S(1)}, bf16[16,128,128]{2,1,0:T(8,128)(2,1)S(1)}, u32[]{:S(2)}, u32[]{:S(2)}) collective-permute-start(bf16[16,128,128]{2,1,0:T(8,128)(2,1)S(1)} %get-tuple-element.86), channel_id=1, source_target_pairs={{0,4},{1,5},{2,6},{3,7},{4,0},{5,1},{6,2},{7,3},{8,12},{9,13},{10,... | collective-permute-start | bytes 1572872 | tf_op jit(solution)/shard_map/ppermute | solution.py:681
  41.8 21.6 %collective-permute-start.10 = (bf16[20,128,128]{2,1,0:T(8,128)(2,1)S(1)}, bf16[20,128,128]{2,1,0:T(8,128)(2,1)S(1)}, u32[]{:S(2)}, u32[]{:S(2)}) collective-permute-start(bf16[20,128,128]{2,1,0:T(8,128)(2,1)S(1)} %get-tuple-element.78), channel_id=1, source_target_pairs={{0,4},{1,5},{2,6},{3,7},{4,0},{5,1},{6,2},{7,3},{8,12},{9,13},{10,... | collective-permute-start | bytes 1966088 | tf_op jit(solution)/shard_map/ppermute | solution.py:681
  43.4 20.0 %collective-permute-start.11 = (bf16[20,128,128]{2,1,0:T(8,128)(2,1)S(1)}, bf16[20,128,128]{2,1,0:T(8,128)(2,1)S(1)}, u32[]{:S(2)}, u32[]{:S(2)}) collective-permute-start(bf16[20,128,128]{2,1,0:T(8,128)(2,1)S(1)} %get-tuple-element.80), channel_id=1, source_target_pairs={{0,2},{1,3},{2,0},{3,1},{4,6},{5,7},{6,4},{7,5},{8,10},{9,11},{10,... | collective-permute-start | bytes 1966088 | tf_op jit(solution)/shard_map/ppermute | solution.py:681
  50.1 3.5 %collective-permute-start.15 = (bf16[16,64,128]{2,1,0:T(8,128)(2,1)S(1)}, bf16[16,64,128]{2,1,0:T(8,128)(2,1)S(1)}, u32[]{:S(2)}, u32[]{:S(2)}) collective-permute-start(bf16[16,64,128]{2,1,0:T(8,128)(2,1)S(1)} %get-tuple-element.88), channel_id=1, source_target_pairs={{0,1},{1,0},{2,3},{3,2},{4,5},{5,4},{6,7},{7,6},{8,9},{9,8},{10,11... | collective-permute-start | bytes 786440 | tf_op jit(solution)/shard_map/ppermute | solution.py:681
  50.2 10.0 %collective-permute-start.14 = (bf16[16,64,128]{2,1,0:T(8,128)(2,1)S(1)}, bf16[16,64,128]{2,1,0:T(8,128)(2,1)S(1)}, u32[]{:S(2)}, u32[]{:S(2)}) collective-permute-start(bf16[16,64,128]{2,1,0:T(8,128)(2,1)S(1)} %get-tuple-element.87), channel_id=1, source_target_pairs={{0,1},{1,0},{2,3},{3,2},{4,5},{5,4},{6,7},{7,6},{8,9},{9,8},{10,11... | collective-permute-start | bytes 786440 | tf_op jit(solution)/shard_map/ppermute | solution.py:681
  53.8 14.6 %collective-permute-start.23 = (bf16[16,64,128]{2,1,0:T(8,128)(2,1)S(1)}, bf16[16,64,128]{2,1,0:T(8,128)(2,1)S(1)}, u32[]{:S(2)}, u32[]{:S(2)}) collective-permute-start(bf16[16,64,128]{2,1,0:T(8,128)(2,1)S(1)} %get-tuple-element.106), channel_id=1, source_target_pairs={{8,16},{16,8},{9,17},{17,9},{10,18},{18,10},{11,19},{19,11},{12,20... | collective-permute-start | bytes 786440 | tf_op jit(solution)/shard_map/ppermute | solution.py:694
  54.5 14.4 %collective-permute-start.22 = (bf16[16,64,128]{2,1,0:T(8,128)(2,1)S(1)}, bf16[16,64,128]{2,1,0:T(8,128)(2,1)S(1)}, u32[]{:S(2)}, u32[]{:S(2)}) collective-permute-start(bf16[16,64,128]{2,1,0:T(8,128)(2,1)S(1)} %get-tuple-element.92.refs_4_), channel_id=1, source_target_pairs={{0,8},{8,0},{16,24},{24,16},{1,9},{9,1},{17,25},{25,17},{2,10},{10... | collective-permute-start | bytes 786440 | tf_op jit(solution)/shard_map/ppermute | solution.py:694
  63.9 1.4 %collective-permute-start.18 = (f32[256,128]{1,0:T(8,128)S(1)}, f32[256,128]{1,0:T(8,128)S(1)}, u32[]{:S(2)}, u32[]{:S(2)}) collective-permute-start(f32[256,128]{1,0:T(8,128)S(1)} %get-tuple-element.99), channel_id=1, source_target_pairs={{0,1},{1,0},{2,3},{3,2},{4,5},{5,4},{6,7},{7,6},{8,9},{9,8},{10,11... | collective-permute-start | bytes 393224 | tf_op jit(solution)/shard_map/ppermute | solution.py:681
  64.0 12.7 %collective-permute-start.16 = (bf16[16,64,128]{2,1,0:T(8,128)(2,1)S(1)}, bf16[16,64,128]{2,1,0:T(8,128)(2,1)S(1)}, u32[]{:S(2)}, u32[]{:S(2)}) collective-permute-start(bf16[16,64,128]{2,1,0:T(8,128)(2,1)S(1)} %get-tuple-element.96), channel_id=1, source_target_pairs={{0,1},{1,0},{2,3},{3,2},{4,5},{5,4},{6,7},{7,6},{8,9},{9,8},{10,11... | collective-permute-start | bytes 786440 | tf_op jit(solution)/shard_map/ppermute | solution.py:681
  64.5 12.2 %collective-permute-start.17 = (bf16[16,64,128]{2,1,0:T(8,128)(2,1)S(1)}, bf16[16,64,128]{2,1,0:T(8,128)(2,1)S(1)}, u32[]{:S(2)}, u32[]{:S(2)}) collective-permute-start(bf16[16,64,128]{2,1,0:T(8,128)(2,1)S(1)} %get-tuple-element.97), channel_id=1, source_target_pairs={{0,1},{1,0},{2,3},{3,2},{4,5},{5,4},{6,7},{7,6},{8,9},{9,8},{10,11... | collective-permute-start | bytes 786440 | tf_op jit(solution)/shard_map/ppermute | solution.py:681
  65.3 11.3 %collective-permute-start.19 = (f32[96,128]{1,0:T(8,128)S(1)}, f32[96,128]{1,0:T(8,128)S(1)}, u32[]{:S(2)}, u32[]{:S(2)}) collective-permute-start(f32[96,128]{1,0:T(8,128)S(1)} %get-tuple-element.101), channel_id=1, source_target_pairs={{0,8},{8,0},{16,24},{24,16},{1,9},{9,1},{17,25},{25,17},{2,10},{10... | collective-permute-start | bytes 147464 | tf_op jit(solution)/shard_map/ppermute | solution.py:697
  68.4 8.3 %collective-permute-start.20 = (f32[96,128]{1,0:T(8,128)S(1)}, f32[96,128]{1,0:T(8,128)S(1)}, u32[]{:S(2)}, u32[]{:S(2)}) collective-permute-start(f32[96,128]{1,0:T(8,128)S(1)} %get-tuple-element.102), channel_id=1, source_target_pairs={{0,16},{8,24},{16,0},{24,8},{1,17},{9,25},{17,1},{25,9},{2,18},{10... | collective-permute-start | bytes 147464 | tf_op jit(solution)/shard_map/ppermute | solution.py:697
  68.9 7.8 %collective-permute-start.21 = (f32[96,128]{1,0:T(8,128)S(1)}, f32[96,128]{1,0:T(8,128)S(1)}, u32[]{:S(2)}, u32[]{:S(2)}) collective-permute-start(f32[96,128]{1,0:T(8,128)S(1)} %get-tuple-element.103), channel_id=1, source_target_pairs={{0,24},{8,16},{16,8},{24,0},{1,25},{9,17},{17,9},{25,1},{2,26},{10... | collective-permute-start | bytes 147464 | tf_op jit(solution)/shard_map/ppermute | solution.py:697
  (4 other events, 14.1 us)

commit v4 on v3

--- a/solution.py
+++ b/solution.py
@@ -330,10 +330,11 @@
         cells = jnp.concatenate(
             [jnp.concatenate([ref[i * step + j] for ref in blocks], axis=0) for j in range(step)], axis=1
         )
-        product = jnp.dot(weights, cells, preferred_element_type=F32).astype(BF16)
+        product = jnp.dot(weights, cells, preferred_element_type=F32)
         for n, out in enumerate(outs):
             for j in range(step):
-                out[i * step + j] = product[n * both : (n + 1) * both, j * width : (j + 1) * width]
+                term = product[n * both : (n + 1) * both, j * width : (j + 1) * width]
+                out[i * step + j] = term.astype(out.dtype)
 
 
 def back_terms(parts, after=()):
@@ -343,7 +344,7 @@
         part = mine.shape[0] - slices
         plans.append((len(args), len(outs), len(arrived), sends, slices, part))
         args += [mine, filter_mine, *arrived]
-        outs += [shaped((part, both, width))] * (sends + 1) + [shaped(((1 + len(arrived)) * both, slices * width))]
+        outs += [shaped((part, both, width), F32)] + [shaped((part, both, width))] * sends + [shaped(((1 + len(arrived)) * both, slices * width))]
     used = len(args)
 
     def kernel(*refs):
@@ -427,7 +428,7 @@
         chans, wide = both // 2, len(hiddens) * both
         plans.append((len(args), len(outs), len(hiddens), len(grads), over_mid))
         args += [block, *hiddens, *grads]
-        outs += [shaped((part, both, width)), shaped((both, wide), F32)]
+        outs += [shaped((part, both, width), F32), shaped((both, wide), F32)]
         outs += [shaped((part + 2 * wide // width, both, width))] * (len(grads) - 1)
         scratch += [pltpu.VMEM((wide, part * width), BF16), pltpu.VMEM((len(grads) * both, part * width), BF16)]
     used = len(args)
@@ -697,9 +698,9 @@
         return lax.ppermute(value, "space", [(i, i ^ apart) for i in range(slabs)])
 
     filter_arrived = to_core(point_filter)
-    grad_own, grad_other = relayout_grad(grad_out, count)
+    grad_own, grad_other = relayout_grad(grad_out, count, [filter_arrived])
     grad_arrived = to_core(grad_other)
-    cells, near, far = relayout_images(images, [grad_own, filter_arrived])
+    cells, near, far = relayout_images(images, [grad_own])
     image_rims = halo(near, far)
     to_hi, to_mid, filter_hi, filter_mid = pack_grad(
         grad_own, grad_arrived, point_filter, filter_arrived, count, [cells]

time: 78.7 us -> 78.8 us (level)
  no operation moved by 1% of the time
where the time goes in v4:
time: 78.8 us; the launch traced here: 78.6 us
  starting transfers between devices  28.2 us (36%)
  Pallas kernels  27.4 us (35%)
  waiting for transfers between devices  20.7 us (26%)
  local copies, waits for them, and re-layouts  1.54 us (2%)
  between operations  0.9 us (1%)
    pallas_call x16, Pallas kernels, kernel_call(): pl.pallas_call(run, out_shape=outs, in_specs=[IN_VMEM] * used + [ANYWHERE...  27.4 us
    ppermute x17, waiting for transfers between devices, moved(): return lax.ppermute(value, 'chan', pairs)  20.6 us
    ppermute x17, starting transfers between devices, moved(): return lax.ppermute(value, 'chan', pairs)  12.5 us
    ppermute x2, starting transfers between devices, halo(): lax.ppermute(near, 'space', swaps[0])  8.69 us
    ppermute x3, starting transfers between devices, exchanged(): return lax.ppermute(value, 'space', [(i, i ^ apart) for i in range(slabs)])  5.6 us
  transfers between devices with their start and end apart: 24, of which 8 were waited for; matrix products, arithmetic and copies ran while one was open for 0% of the time, Pallas kernels for 32%

profile of v4, /device:TPU:0, one launch (start us, length us, event | category | flops | bytes accessed | tf_op | source)
XLA Modules:
  0.0 78.6 jit_solution(6716084744067397251)
XLA Ops:
  2.3 1.2 %copy-done.2 = bf16[64,16,4,128]{3,2,1,0:T(4,128)(2,1)S(1)} copy-done((bf16[64,16,4,128]{3,2,1,0:T(4,128)(2,1)S(1)}, bf16[64,16,4,128]{3,2,1,0:T(4,128)(2,1)}, u32[]{:S(2)}) %copy-start.2) | copy-done | bytes 1048600
  5.3 3.0 %collective-permute-start.4 = (bf16[16,64,128]{2,1,0:T(8,128)(2,1)S(1)}, bf16[16,64,128]{2,1,0:T(8,128)(2,1)S(1)}, u32[]{:S(2)}, u32[]{:S(2)}) collective-permute-start(bf16[16,64,128]{2,1,0:T(8,128)(2,1)S(1)} %get-tuple-element.66), channel_id=1, source_target_pairs={{0,8},{8,0},{16,24},{24,16},{1,9},{9,1},{17,25},{25,17},{2,10},{10... | collective-permute-start | bytes 786440 | tf_op jit(solution)/shard_map/ppermute | solution.py:695
  9.6 1.6 %collective-permute-start.3 = (bf16[18,128,128]{2,1,0:T(8,128)(2,1)S(1)}, bf16[18,128,128]{2,1,0:T(8,128)(2,1)S(1)}, u32[]{:S(2)}, u32[]{:S(2)}) collective-permute-start(bf16[18,128,128]{2,1,0:T(8,128)(2,1)S(1)} %get-tuple-element.63.refs_3_.refs_8_), channel_id=1, source_target_pairs={{0,2},{1,3},{2,0},{3,1},{4,6},{5,7},{6,4},{7,5},{8,10},{9,11},{10,... | collective-permute-start | bytes 1769480 | tf_op jit(solution)/shard_map/ppermute | solution.py:682
  11.1 1.5 %collective-permute-start.2 = (bf16[18,128,128]{2,1,0:T(8,128)(2,1)S(1)}, bf16[18,128,128]{2,1,0:T(8,128)(2,1)S(1)}, u32[]{:S(2)}, u32[]{:S(2)}) collective-permute-start(bf16[18,128,128]{2,1,0:T(8,128)(2,1)S(1)} %get-tuple-element.61.refs_2_.refs_0_.refs_3_), channel_id=1, source_target_pairs={{0,4},{1,5},{2,6},{3,7},{4,0},{5,1},{6,2},{7,3},{8,12},{9,13},{10,... | collective-permute-start | bytes 1769480 | tf_op jit(solution)/shard_map/ppermute | solution.py:682
  12.7 2.8 %shard_map.78 = (bf16[16,64,128]{2,1,0:T(8,128)(2,1)S(1)}, bf16[16,64,128]{2,1,0:T(8,128)(2,1)S(1)}, f32[27,64,128]{2,1,0:T(8,128)S(1)}) custom-call(bf16[64,64,128]{2,1,0:T(8,128)(2,1)S(1)} %get-tuple-element.60.refs_4_.refs_0_, f32[27,64]{1,0:T(8,128)S(1)} %copy-done.1, bf16[18,128,128]{2,1,0:T(8,128)(2,1)S(1)} %get-tuple-element.61.refs_2_.refs_0_.refs_3_), custom_call_target="tpu_custom_call" | custom-call | flops 100000000 | tf_op jit(solution)/shard_map/pallas_call | solution.py:62
  15.6 2.7 %shard_map.79 = (bf16[16,64,128]{2,1,0:T(8,128)(2,1)S(1)}, bf16[16,64,128]{2,1,0:T(8,128)(2,1)S(1)}, f32[108,64,128]{2,1,0:T(8,128)S(1)}) custom-call(bf16[64,64,128]{2,1,0:T(8,128)(2,1)S(1)} %get-tuple-element.60.refs_4_.refs_0_, bf16[16,64,128]{2,1,0:T(8,128)(2,1)S(1)} %collective-permute-done.4.refs_1_, ...), custom_call_target="tpu_custom_call" | custom-call | flops 100000000 | tf_op jit(solution)/shard_map/pallas_call | solution.py:62
  18.9 1.2 %collective-permute-done.7.refs_3_ = bf16[16,64,128]{2,1,0:T(8,128)(2,1)S(1)} collective-permute-done((bf16[16,64,128]{2,1,0:T(8,128)(2,1)S(1)}, bf16[16,64,128]{2,1,0:T(8,128)(2,1)S(1)}, u32[]{:S(2)}, u32[]{:S(2)}) %collective-permute-start.7) | collective-permute-done | bytes 262176 | tf_op jit(solution)/shard_map/ppermute | solution.py:682
  21.1 1.5 %collective-permute-start.8 = (bf16[16,128,128]{2,1,0:T(8,128)(2,1)S(1)}, bf16[16,128,128]{2,1,0:T(8,128)(2,1)S(1)}, u32[]{:S(2)}, u32[]{:S(2)}) collective-permute-start(bf16[16,128,128]{2,1,0:T(8,128)(2,1)S(1)} %get-tuple-element.72.refs_6_.refs_1_), channel_id=1, source_target_pairs={{0,2},{1,3},{2,0},{3,1},{4,6},{5,7},{6,4},{7,5},{8,10},{9,11},{10,... | collective-permute-start | bytes 1572872 | tf_op jit(solution)/shard_map/ppermute | solution.py:682
  22.6 3.2 %collective-permute-done.3.refs_5_.refs_9_ = bf16[18,128,128]{2,1,0:T(8,128)(2,1)S(1)} collective-permute-done((bf16[18,128,128]{2,1,0:T(8,128)(2,1)S(1)}, bf16[18,128,128]{2,1,0:T(8,128)(2,1)S(1)}, u32[]{:S(2)}, u32[]{:S(2)}) %collective-permute-start.3) | collective-permute-done | bytes 589856 | tf_op jit(solution)/shard_map/ppermute | solution.py:682
  25.9 1.5 %collective-permute-done.2.refs_2_.refs_4_ = bf16[18,128,128]{2,1,0:T(8,128)(2,1)S(1)} collective-permute-done((bf16[18,128,128]{2,1,0:T(8,128)(2,1)S(1)}, bf16[18,128,128]{2,1,0:T(8,128)(2,1)S(1)}, u32[]{:S(2)}, u32[]{:S(2)}) %collective-permute-start.2) | collective-permute-done | bytes 589856 | tf_op jit(solution)/shard_map/ppermute | solution.py:682
  27.4 2.0 %shard_map.81 = (f32[16,128,128]{2,1,0:T(8,128)S(1)}, bf16[16,128,128]{2,1,0:T(8,128)(2,1)S(1)}, bf16[256,256]{1,0:T(8,128)(2,1)S(1)}, f32[16,128,128]{2,1,0:T(8...) custom-call(bf16[18,128,128]{2,1,0:T(8,128)(2,1)S(1)} %get-tuple-element.61.refs_2_.refs_0_.refs_3_, ...), custom_call_target="tpu_custom_call" | custom-call | flops 100000000 | tf_op jit(solution)/shard_map/pallas_call | solution.py:62
  30.0 1.5 %collective-permute-start.13 = (bf16[16,128,128]{2,1,0:T(8,128)(2,1)S(1)}, bf16[16,128,128]{2,1,0:T(8,128)(2,1)S(1)}, u32[]{:S(2)}, u32[]{:S(2)}) collective-permute-start(bf16[16,128,128]{2,1,0:T(8,128)(2,1)S(1)} %get-tuple-element.86), channel_id=1, source_target_pairs={{0,4},{1,5},{2,6},{3,7},{4,0},{5,1},{6,2},{7,3},{8,12},{9,13},{10,... | collective-permute-start | bytes 1572872 | tf_op jit(solution)/shard_map/ppermute | solution.py:682
  31.6 7.1 %collective-permute-done.9.refs_7_ = bf16[16,128,128]{2,1,0:T(8,128)(2,1)S(1)} collective-permute-done((bf16[16,128,128]{2,1,0:T(8,128)(2,1)S(1)}, bf16[16,128,128]{2,1,0:T(8,128)(2,1)S(1)}, u32[]{:S(2)}, u32[]{:S(2)}) %collective-permute-start.9) | collective-permute-done | bytes 524320 | tf_op jit(solution)/shard_map/ppermute | solution.py:682
  38.6 3.4 %shard_map.82 = (f32[16,128,128]{2,1,0:T(8,128)S(1)}, f32[128,256]{1,0:T(8,128)S(1)}, bf16[20,128,128]{2,1,0:T(8,128)(2,1)S(1)}, f32[16,128,128]{2,1,0:T(8,128)S...) custom-call(bf16[256,256]{1,0:T(8,128)(2,1)S(1)} %get-tuple-element.73.refs_0_, ...), custom_call_target="tpu_custom_call" | custom-call | flops 100000000 | tf_op jit(solution)/shard_map/pallas_call | solution.py:62
  42.0 1.6 %collective-permute-start.10 = (bf16[20,128,128]{2,1,0:T(8,128)(2,1)S(1)}, bf16[20,128,128]{2,1,0:T(8,128)(2,1)S(1)}, u32[]{:S(2)}, u32[]{:S(2)}) collective-permute-start(bf16[20,128,128]{2,1,0:T(8,128)(2,1)S(1)} %get-tuple-element.78), channel_id=1, source_target_pairs={{0,4},{1,5},{2,6},{3,7},{4,0},{5,1},{6,2},{7,3},{8,12},{9,13},{10,... | collective-permute-start | bytes 1966088 | tf_op jit(solution)/shard_map/ppermute | solution.py:682
  44.1 4.2 %collective-permute-done.12.refs_1_ = bf16[16,128,128]{2,1,0:T(8,128)(2,1)S(1)} collective-permute-done((bf16[16,128,128]{2,1,0:T(8,128)(2,1)S(1)}, bf16[16,128,128]{2,1,0:T(8,128)(2,1)S(1)}, u32[]{:S(2)}, u32[]{:S(2)}) %collective-permute-start.12) | collective-permute-done | bytes 524320 | tf_op jit(solution)/shard_map/ppermute | solution.py:682
  48.3 1.5 %collective-permute-done.13.refs_3_ = bf16[16,128,128]{2,1,0:T(8,128)(2,1)S(1)} collective-permute-done((bf16[16,128,128]{2,1,0:T(8,128)(2,1)S(1)}, bf16[16,128,128]{2,1,0:T(8,128)(2,1)S(1)}, u32[]{:S(2)}, u32[]{:S(2)}) %collective-permute-start.13) | collective-permute-done | bytes 524320 | tf_op jit(solution)/shard_map/ppermute | solution.py:682
  50.8 3.0 %shard_map.84 = (f32[27,64,128]{2,1,0:T(8,128)S(1)}, f32[2,16,64,128]{3,2,1,0:T(8,128)S(1)}) custom-call(f32[108,64,128]{2,1,0:T(8,128)S(1)} %get-tuple-element.83.refs_0_, bf16[16,64,128]{2,1,0:T(8,128)(2,1)S(1)} %get-tuple-element.89.refs_1_, bf16[16,64,128]{2,1,0:T(8,128)(2,1)S(1)} %get-tuple-element.90.refs_2_.refs_0_), custom_call_target="tpu_custom_call" | custom-call | flops 100000000 | tf_op jit(solution)/shard_map/pallas_call | solution.py:62
  54.6 5.7 %collective-permute-start.22 = (bf16[16,64,128]{2,1,0:T(8,128)(2,1)S(1)}, bf16[16,64,128]{2,1,0:T(8,128)(2,1)S(1)}, u32[]{:S(2)}, u32[]{:S(2)}) collective-permute-start(bf16[16,64,128]{2,1,0:T(8,128)(2,1)S(1)} %get-tuple-element.92.refs_4_), channel_id=1, source_target_pairs={{0,8},{8,0},{16,24},{24,16},{1,9},{9,1},{17,25},{25,17},{2,10},{10... | collective-permute-start | bytes 786440 | tf_op jit(solution)/shard_map/ppermute | solution.py:695
  60.3 3.2 %shard_map.86 = (f32[32,128]{1,0:T(8,128)S(1)}, f32[2,16,64,128]{3,2,1,0:T(8,128)S(1)}) custom-call(f32[108,64,128]{2,1,0:T(8,128)S(1)} %get-tuple-element.83.refs_0_, bf16[16,64,128]{2,1,0:T(8,128)(2,1)S(1)} %collective-permute-done.14.refs_1_, bf16[16,64,128]{2,1,0:T(8,128)(2,1)S(1)} %collective-permute-done.15.refs_1_.refs_2_, ...), custom_call_target="tpu_custom_call" | custom-call | flops 100000000 | tf_op jit(solution)/shard_map/pallas_call | solution.py:62
  65.3 3.1 %collective-permute-start.19 = (f32[96,128]{1,0:T(8,128)S(1)}, f32[96,128]{1,0:T(8,128)S(1)}, u32[]{:S(2)}, u32[]{:S(2)}) collective-permute-start(f32[96,128]{1,0:T(8,128)S(1)} %get-tuple-element.101), channel_id=1, source_target_pairs={{0,8},{8,0},{16,24},{24,16},{1,9},{9,1},{17,25},{25,17},{2,10},{10... | collective-permute-start | bytes 147464 | tf_op jit(solution)/shard_map/ppermute | solution.py:698
  68.9 2.1 %collective-permute-start.21 = (f32[96,128]{1,0:T(8,128)S(1)}, f32[96,128]{1,0:T(8,128)S(1)}, u32[]{:S(2)}, u32[]{:S(2)}) collective-permute-start(f32[96,128]{1,0:T(8,128)S(1)} %get-tuple-element.103), channel_id=1, source_target_pairs={{0,24},{8,16},{16,8},{24,0},{1,25},{9,17},{17,9},{25,1},{2,26},{10... | collective-permute-start | bytes 147464 | tf_op jit(solution)/shard_map/ppermute | solution.py:698
  71.0 5.8 %shard_map.89 = (bf16[4096,128]{1,0:T(8,128)(2,1)}, f32[8,128]{1,0:T(8,128)S(1)}) custom-call(f32[2,16,64,128]{3,2,1,0:T(8,128)S(1)} %get-tuple-element.104.refs_0_, f32[2,16,64,128]{3,2,1,0:T(8,128)S(1)} %get-tuple-element.105.refs_1_, bf16[16,64,128]{2,1,0:T(8,128)(2,1)S(1)} %collective-permute-done.22.refs_2_, ...), custom_call_target="tpu_custom_call" | custom-call | flops 20000000000 | tf_op jit(solution)/shard_map/pallas_call | solution.py:62
  76.8 1.8 %shard_map.90 = (bf16[4096,128]{1,0:T(8,128)(2,1)}, f32[64,128]{1,0:T(8,128)}, f32[27,64]{1,0:T(8,128)}) custom-call(bf16[16,64,128]{2,1,0:T(8,128)(2,1)S(1)} %get-tuple-element.94.refs_0_, bf16[16,64,128]{2,1,0:T(8,128)(2,1)S(1)} %get-tuple-element.95.refs_1_, bf16[16,64,128]{2,1,0:T(8,128)(2,1)S(1)} %collective-permute-done.16.refs_2_, ...), custom_call_target="tpu_custom_call" | custom-call | flops 100000000 | tf_op jit(solution)/shard_map/pallas_call | solution.py:62
  (48 shorter events, 11.5 us)
Async XLA Ops:
  0.6 1.6 %collective-permute-start = (bf16[64,512]{1,0:T(8,128)(2,1)}, bf16[64,512]{1,0:T(8,128)(2,1)S(1)}, u32[]{:S(2)}, u32[]{:S(2)}) collective-permute-start(bf16[64,512]{1,0:T(8,128)(2,1)} %refs_2_.1), channel_id=1, source_target_pairs={{0,1},{1,0},{2,3},{3,2},{4,5},{5,4},{6,7},{7,6},{8,9},{9,8},{10,11... | collective-permute-start | bytes 196616 | tf_op jit(solution)/shard_map/ppermute | solution.py:682
  4.0 5.0 %collective-permute-start.1 = (bf16[32,64,128]{2,1,0:T(8,128)(2,1)S(1)}, bf16[32,64,128]{2,1,0:T(8,128)(2,1)S(1)}, u32[]{:S(2)}, u32[]{:S(2)}) collective-permute-start(bf16[32,64,128]{2,1,0:T(8,128)(2,1)S(1)} %get-tuple-element.59), channel_id=1, source_target_pairs={{0,1},{1,0},{2,3},{3,2},{4,5},{5,4},{6,7},{7,6},{8,9},{9,8},{10,11... | collective-permute-start | bytes 1572872 | tf_op jit(solution)/shard_map/ppermute | solution.py:682
  5.3 10.3 %collective-permute-start.4 = (bf16[16,64,128]{2,1,0:T(8,128)(2,1)S(1)}, bf16[16,64,128]{2,1,0:T(8,128)(2,1)S(1)}, u32[]{:S(2)}, u32[]{:S(2)}) collective-permute-start(bf16[16,64,128]{2,1,0:T(8,128)(2,1)S(1)} %get-tuple-element.66), channel_id=1, source_target_pairs={{0,8},{8,0},{16,24},{24,16},{1,9},{9,1},{17,25},{25,17},{2,10},{10... | collective-permute-start | bytes 786440 | tf_op jit(solution)/shard_map/ppermute | solution.py:695
  8.3 7.3 %collective-permute-start.5 = (bf16[16,64,128]{2,1,0:T(8,128)(2,1)S(1)}, bf16[16,64,128]{2,1,0:T(8,128)(2,1)S(1)}, u32[]{:S(2)}, u32[]{:S(2)}) collective-permute-start(bf16[16,64,128]{2,1,0:T(8,128)(2,1)S(1)} %get-tuple-element.67), channel_id=1, source_target_pairs={{8,16},{16,8},{9,17},{17,9},{10,18},{18,10},{11,19},{19,11},{12,20... | collective-permute-start | bytes 786440 | tf_op jit(solution)/shard_map/ppermute | solution.py:695
  9.6 16.3 %collective-permute-start.3 = (bf16[18,128,128]{2,1,0:T(8,128)(2,1)S(1)}, bf16[18,128,128]{2,1,0:T(8,128)(2,1)S(1)}, u32[]{:S(2)}, u32[]{:S(2)}) collective-permute-start(bf16[18,128,128]{2,1,0:T(8,128)(2,1)S(1)} %get-tuple-element.63.refs_3_.refs_8_), channel_id=1, source_target_pairs={{0,2},{1,3},{2,0},{3,1},{4,6},{5,7},{6,4},{7,5},{8,10},{9,11},{10,... | collective-permute-start | bytes 1769480 | tf_op jit(solution)/shard_map/ppermute | solution.py:682
  11.1 16.3 %collective-permute-start.2 = (bf16[18,128,128]{2,1,0:T(8,128)(2,1)S(1)}, bf16[18,128,128]{2,1,0:T(8,128)(2,1)S(1)}, u32[]{:S(2)}, u32[]{:S(2)}) collective-permute-start(bf16[18,128,128]{2,1,0:T(8,128)(2,1)S(1)} %get-tuple-element.61.refs_2_.refs_0_.refs_3_), channel_id=1, source_target_pairs={{0,4},{1,5},{2,6},{3,7},{4,0},{5,1},{6,2},{7,3},{8,12},{9,13},{10,... | collective-permute-start | bytes 1769480 | tf_op jit(solution)/shard_map/ppermute | solution.py:682
  15.5 3.4 %collective-permute-start.6 = (bf16[16,64,128]{2,1,0:T(8,128)(2,1)S(1)}, bf16[16,64,128]{2,1,0:T(8,128)(2,1)S(1)}, u32[]{:S(2)}, u32[]{:S(2)}) collective-permute-start(bf16[16,64,128]{2,1,0:T(8,128)(2,1)S(1)} %get-tuple-element.70), channel_id=1, source_target_pairs={{0,1},{1,0},{2,3},{3,2},{4,5},{5,4},{6,7},{7,6},{8,9},{9,8},{10,11... | collective-permute-start | bytes 786440 | tf_op jit(solution)/shard_map/ppermute | solution.py:682
  18.4 1.7 %collective-permute-start.7 = (bf16[16,64,128]{2,1,0:T(8,128)(2,1)S(1)}, bf16[16,64,128]{2,1,0:T(8,128)(2,1)S(1)}, u32[]{:S(2)}, u32[]{:S(2)}) collective-permute-start(bf16[16,64,128]{2,1,0:T(8,128)(2,1)S(1)} %get-tuple-element.71), channel_id=1, source_target_pairs={{0,1},{1,0},{2,3},{3,2},{4,5},{5,4},{6,7},{7,6},{8,9},{9,8},{10,11... | collective-permute-start | bytes 786440 | tf_op jit(solution)/shard_map/ppermute | solution.py:682
  20.2 18.5 %collective-permute-start.9 = (bf16[16,128,128]{2,1,0:T(8,128)(2,1)S(1)}, bf16[16,128,128]{2,1,0:T(8,128)(2,1)S(1)}, u32[]{:S(2)}, u32[]{:S(2)}) collective-permute-start(bf16[16,128,128]{2,1,0:T(8,128)(2,1)S(1)} %get-tuple-element.75.refs_6_), channel_id=1, source_target_pairs={{0,4},{1,5},{2,6},{3,7},{4,0},{5,1},{6,2},{7,3},{8,12},{9,13},{10,... | collective-permute-start | bytes 1572872 | tf_op jit(solution)/shard_map/ppermute | solution.py:682
  21.1 17.5 %collective-permute-start.8 = (bf16[16,128,128]{2,1,0:T(8,128)(2,1)S(1)}, bf16[16,128,128]{2,1,0:T(8,128)(2,1)S(1)}, u32[]{:S(2)}, u32[]{:S(2)}) collective-permute-start(bf16[16,128,128]{2,1,0:T(8,128)(2,1)S(1)} %get-tuple-element.72.refs_6_.refs_1_), channel_id=1, source_target_pairs={{0,2},{1,3},{2,0},{3,1},{4,6},{5,7},{6,4},{7,5},{8,10},{9,11},{10,... | collective-permute-start | bytes 1572872 | tf_op jit(solution)/shard_map/ppermute | solution.py:682
  29.4 18.9 %collective-permute-start.12 = (bf16[16,128,128]{2,1,0:T(8,128)(2,1)S(1)}, bf16[16,128,128]{2,1,0:T(8,128)(2,1)S(1)}, u32[]{:S(2)}, u32[]{:S(2)}) collective-permute-start(bf16[16,128,128]{2,1,0:T(8,128)(2,1)S(1)} %get-tuple-element.84), channel_id=1, source_target_pairs={{0,2},{1,3},{2,0},{3,1},{4,6},{5,7},{6,4},{7,5},{8,10},{9,11},{10,... | collective-permute-start | bytes 1572872 | tf_op jit(solution)/shard_map/ppermute | solution.py:682
  30.0 19.8 %collective-permute-start.13 = (bf16[16,128,128]{2,1,0:T(8,128)(2,1)S(1)}, bf16[16,128,128]{2,1,0:T(8,128)(2,1)S(1)}, u32[]{:S(2)}, u32[]{:S(2)}) collective-permute-start(bf16[16,128,128]{2,1,0:T(8,128)(2,1)S(1)} %get-tuple-element.86), channel_id=1, source_target_pairs={{0,4},{1,5},{2,6},{3,7},{4,0},{5,1},{6,2},{7,3},{8,12},{9,13},{10,... | collective-permute-start | bytes 1572872 | tf_op jit(solution)/shard_map/ppermute | solution.py:682
  42.0 21.5 %collective-permute-start.10 = (bf16[20,128,128]{2,1,0:T(8,128)(2,1)S(1)}, bf16[20,128,128]{2,1,0:T(8,128)(2,1)S(1)}, u32[]{:S(2)}, u32[]{:S(2)}) collective-permute-start(bf16[20,128,128]{2,1,0:T(8,128)(2,1)S(1)} %get-tuple-element.78), channel_id=1, source_target_pairs={{0,4},{1,5},{2,6},{3,7},{4,0},{5,1},{6,2},{7,3},{8,12},{9,13},{10,... | collective-permute-start | bytes 1966088 | tf_op jit(solution)/shard_map/ppermute | solution.py:682
  43.6 19.9 %collective-permute-start.11 = (bf16[20,128,128]{2,1,0:T(8,128)(2,1)S(1)}, bf16[20,128,128]{2,1,0:T(8,128)(2,1)S(1)}, u32[]{:S(2)}, u32[]{:S(2)}) collective-permute-start(bf16[20,128,128]{2,1,0:T(8,128)(2,1)S(1)} %get-tuple-element.80), channel_id=1, source_target_pairs={{0,2},{1,3},{2,0},{3,1},{4,6},{5,7},{6,4},{7,5},{8,10},{9,11},{10,... | collective-permute-start | bytes 1966088 | tf_op jit(solution)/shard_map/ppermute | solution.py:682
  50.2 3.5 %collective-permute-start.15 = (bf16[16,64,128]{2,1,0:T(8,128)(2,1)S(1)}, bf16[16,64,128]{2,1,0:T(8,128)(2,1)S(1)}, u32[]{:S(2)}, u32[]{:S(2)}) collective-permute-start(bf16[16,64,128]{2,1,0:T(8,128)(2,1)S(1)} %get-tuple-element.88), channel_id=1, source_target_pairs={{0,1},{1,0},{2,3},{3,2},{4,5},{5,4},{6,7},{7,6},{8,9},{9,8},{10,11... | collective-permute-start | bytes 786440 | tf_op jit(solution)/shard_map/ppermute | solution.py:682
  50.3 10.0 %collective-permute-start.14 = (bf16[16,64,128]{2,1,0:T(8,128)(2,1)S(1)}, bf16[16,64,128]{2,1,0:T(8,128)(2,1)S(1)}, u32[]{:S(2)}, u32[]{:S(2)}) collective-permute-start(bf16[16,64,128]{2,1,0:T(8,128)(2,1)S(1)} %get-tuple-element.87), channel_id=1, source_target_pairs={{0,1},{1,0},{2,3},{3,2},{4,5},{5,4},{6,7},{7,6},{8,9},{9,8},{10,11... | collective-permute-start | bytes 786440 | tf_op jit(solution)/shard_map/ppermute | solution.py:682
  53.9 14.6 %collective-permute-start.23 = (bf16[16,64,128]{2,1,0:T(8,128)(2,1)S(1)}, bf16[16,64,128]{2,1,0:T(8,128)(2,1)S(1)}, u32[]{:S(2)}, u32[]{:S(2)}) collective-permute-start(bf16[16,64,128]{2,1,0:T(8,128)(2,1)S(1)} %get-tuple-element.106), channel_id=1, source_target_pairs={{8,16},{16,8},{9,17},{17,9},{10,18},{18,10},{11,19},{19,11},{12,20... | collective-permute-start | bytes 786440 | tf_op jit(solution)/shard_map/ppermute | solution.py:695
  54.6 14.3 %collective-permute-start.22 = (bf16[16,64,128]{2,1,0:T(8,128)(2,1)S(1)}, bf16[16,64,128]{2,1,0:T(8,128)(2,1)S(1)}, u32[]{:S(2)}, u32[]{:S(2)}) collective-permute-start(bf16[16,64,128]{2,1,0:T(8,128)(2,1)S(1)} %get-tuple-element.92.refs_4_), channel_id=1, source_target_pairs={{0,8},{8,0},{16,24},{24,16},{1,9},{9,1},{17,25},{25,17},{2,10},{10... | collective-permute-start | bytes 786440 | tf_op jit(solution)/shard_map/ppermute | solution.py:695
  63.9 1.4 %collective-permute-start.18 = (f32[256,128]{1,0:T(8,128)S(1)}, f32[256,128]{1,0:T(8,128)S(1)}, u32[]{:S(2)}, u32[]{:S(2)}) collective-permute-start(f32[256,128]{1,0:T(8,128)S(1)} %get-tuple-element.99), channel_id=1, source_target_pairs={{0,1},{1,0},{2,3},{3,2},{4,5},{5,4},{6,7},{7,6},{8,9},{9,8},{10,11... | collective-permute-start | bytes 393224 | tf_op jit(solution)/shard_map/ppermute | solution.py:682
  64.0 12.8 %collective-permute-start.16 = (bf16[16,64,128]{2,1,0:T(8,128)(2,1)S(1)}, bf16[16,64,128]{2,1,0:T(8,128)(2,1)S(1)}, u32[]{:S(2)}, u32[]{:S(2)}) collective-permute-start(bf16[16,64,128]{2,1,0:T(8,128)(2,1)S(1)} %get-tuple-element.96), channel_id=1, source_target_pairs={{0,1},{1,0},{2,3},{3,2},{4,5},{5,4},{6,7},{7,6},{8,9},{9,8},{10,11... | collective-permute-start | bytes 786440 | tf_op jit(solution)/shard_map/ppermute | solution.py:682
  64.5 12.3 %collective-permute-start.17 = (bf16[16,64,128]{2,1,0:T(8,128)(2,1)S(1)}, bf16[16,64,128]{2,1,0:T(8,128)(2,1)S(1)}, u32[]{:S(2)}, u32[]{:S(2)}) collective-permute-start(bf16[16,64,128]{2,1,0:T(8,128)(2,1)S(1)} %get-tuple-element.97), channel_id=1, source_target_pairs={{0,1},{1,0},{2,3},{3,2},{4,5},{5,4},{6,7},{7,6},{8,9},{9,8},{10,11... | collective-permute-start | bytes 786440 | tf_op jit(solution)/shard_map/ppermute | solution.py:682
  65.3 11.4 %collective-permute-start.19 = (f32[96,128]{1,0:T(8,128)S(1)}, f32[96,128]{1,0:T(8,128)S(1)}, u32[]{:S(2)}, u32[]{:S(2)}) collective-permute-start(f32[96,128]{1,0:T(8,128)S(1)} %get-tuple-element.101), channel_id=1, source_target_pairs={{0,8},{8,0},{16,24},{24,16},{1,9},{9,1},{17,25},{25,17},{2,10},{10... | collective-permute-start | bytes 147464 | tf_op jit(solution)/shard_map/ppermute | solution.py:698
  68.5 8.3 %collective-permute-start.20 = (f32[96,128]{1,0:T(8,128)S(1)}, f32[96,128]{1,0:T(8,128)S(1)}, u32[]{:S(2)}, u32[]{:S(2)}) collective-permute-start(f32[96,128]{1,0:T(8,128)S(1)} %get-tuple-element.102), channel_id=1, source_target_pairs={{0,16},{8,24},{16,0},{24,8},{1,17},{9,25},{17,1},{25,9},{2,18},{10... | collective-permute-start | bytes 147464 | tf_op jit(solution)/shard_map/ppermute | solution.py:698
  68.9 7.9 %collective-permute-start.21 = (f32[96,128]{1,0:T(8,128)S(1)}, f32[96,128]{1,0:T(8,128)S(1)}, u32[]{:S(2)}, u32[]{:S(2)}) collective-permute-start(f32[96,128]{1,0:T(8,128)S(1)} %get-tuple-element.103), channel_id=1, source_target_pairs={{0,24},{8,16},{16,8},{24,0},{1,25},{9,17},{17,9},{25,1},{2,26},{10... | collective-permute-start | bytes 147464 | tf_op jit(solution)/shard_map/ppermute | solution.py:698
  (4 other events, 15.4 us)

commit v5 on v4

--- a/solution.py
+++ b/solution.py
@@ -429,7 +429,7 @@
         plans.append((len(args), len(outs), len(hiddens), len(grads), over_mid))
         args += [block, *hiddens, *grads]
         outs += [shaped((part, both, width), F32), shaped((both, wide), F32)]
-        outs += [shaped((part + 2 * wide // width, both, width))] * (len(grads) - 1)
+        outs += [shaped((part + wide // width, both, width))] * (len(grads) - 1)
         scratch += [pltpu.VMEM((wide, part * width), BF16), pltpu.VMEM((len(grads) * both, part * width), BF16)]
     used = len(args)
 
@@ -456,12 +456,9 @@
             gradient[...] = pairs[:both]
             slices = pairs.shape[1] // width
             for i, send in enumerate(sends, 1):
-                value = pairs[i * both : (i + 1) * both]
-                high = value.astype(BF16)
-                low = (value - high.astype(F32)).astype(BF16)
+                value = pairs[i * both : (i + 1) * both].astype(BF16)
                 for t in range(slices):
-                    send[part + t] = high[:, t * width : (t + 1) * width]
-                    send[part + slices + t] = low[:, t * width : (t + 1) * width]
+                    send[part + t] = value[:, t * width : (t + 1) * width]
 
     done = kernel_call(kernel, outs, args, scratch, after, HINTS["out"])
     return [
@@ -493,10 +490,7 @@
             if back == 0:
                 return own_rows[n][:, columns]
             slices = own_rows[n].shape[1] // width
-            value = [
-                terms[n][back][part + t].astype(F32) + terms[n][back][part + slices + t].astype(F32)
-                for t in range(slices)
-            ]
+            value = [terms[n][back][part + t].astype(F32) for t in range(slices)]
             return jnp.concatenate(value, axis=1)[:, columns]
 
         def chosen(n, at, mine, columns):

time: 78.8 us -> 78.7 us (level)
  no operation moved by 1% of the time
where the time goes in v5:
time: 78.7 us; the launch traced here: 78.5 us
  starting transfers between devices  28 us (36%)
  Pallas kernels  27.4 us (35%)
  waiting for transfers between devices  20.7 us (26%)
  local copies, waits for them, and re-layouts  1.54 us (2%)
  between operations  0.9 us (1%)
    pallas_call x16, Pallas kernels, kernel_call(): pl.pallas_call(run, out_shape=outs, in_specs=[IN_VMEM] * used + [ANYWHERE...  27.4 us
    ppermute x17, waiting for transfers between devices, moved(): return lax.ppermute(value, 'chan', pairs)  20.6 us
    ppermute x17, starting transfers between devices, moved(): return lax.ppermute(value, 'chan', pairs)  12.5 us
    ppermute x2, starting transfers between devices, halo(): lax.ppermute(near, 'space', swaps[0])  8.69 us
    ppermute x3, starting transfers between devices, exchanged(): return lax.ppermute(value, 'space', [(i, i ^ apart) for i in range(slabs)])  5.44 us
  transfers between devices with their start and end apart: 24, of which 8 were waited for; matrix products, arithmetic and copies ran while one was open for 0% of the time, Pallas kernels for 32%

profile of v5, /device:TPU:0, one launch (start us, length us, event | category | flops | bytes accessed | tf_op | source)
XLA Modules:
  0.0 78.5 jit_solution(9931465392028570242)
XLA Ops:
  2.3 1.2 %copy-done.2 = bf16[64,16,4,128]{3,2,1,0:T(4,128)(2,1)S(1)} copy-done((bf16[64,16,4,128]{3,2,1,0:T(4,128)(2,1)S(1)}, bf16[64,16,4,128]{3,2,1,0:T(4,128)(2,1)}, u32[]{:S(2)}) %copy-start.2) | copy-done | bytes 1048600
  5.3 3.0 %collective-permute-start.4 = (bf16[16,64,128]{2,1,0:T(8,128)(2,1)S(1)}, bf16[16,64,128]{2,1,0:T(8,128)(2,1)S(1)}, u32[]{:S(2)}, u32[]{:S(2)}) collective-permute-start(bf16[16,64,128]{2,1,0:T(8,128)(2,1)S(1)} %get-tuple-element.66), channel_id=1, source_target_pairs={{0,8},{8,0},{16,24},{24,16},{1,9},{9,1},{17,25},{25,17},{2,10},{10... | collective-permute-start | bytes 786440 | tf_op jit(solution)/shard_map/ppermute | solution.py:689
  9.6 1.6 %collective-permute-start.3 = (bf16[18,128,128]{2,1,0:T(8,128)(2,1)S(1)}, bf16[18,128,128]{2,1,0:T(8,128)(2,1)S(1)}, u32[]{:S(2)}, u32[]{:S(2)}) collective-permute-start(bf16[18,128,128]{2,1,0:T(8,128)(2,1)S(1)} %get-tuple-element.63.refs_3_.refs_8_), channel_id=1, source_target_pairs={{0,2},{1,3},{2,0},{3,1},{4,6},{5,7},{6,4},{7,5},{8,10},{9,11},{10,... | collective-permute-start | bytes 1769480 | tf_op jit(solution)/shard_map/ppermute | solution.py:676
  11.1 1.5 %collective-permute-start.2 = (bf16[18,128,128]{2,1,0:T(8,128)(2,1)S(1)}, bf16[18,128,128]{2,1,0:T(8,128)(2,1)S(1)}, u32[]{:S(2)}, u32[]{:S(2)}) collective-permute-start(bf16[18,128,128]{2,1,0:T(8,128)(2,1)S(1)} %get-tuple-element.61.refs_2_.refs_0_.refs_3_), channel_id=1, source_target_pairs={{0,4},{1,5},{2,6},{3,7},{4,0},{5,1},{6,2},{7,3},{8,12},{9,13},{10,... | collective-permute-start | bytes 1769480 | tf_op jit(solution)/shard_map/ppermute | solution.py:676
  12.7 2.8 %shard_map.78 = (bf16[16,64,128]{2,1,0:T(8,128)(2,1)S(1)}, bf16[16,64,128]{2,1,0:T(8,128)(2,1)S(1)}, f32[27,64,128]{2,1,0:T(8,128)S(1)}) custom-call(bf16[64,64,128]{2,1,0:T(8,128)(2,1)S(1)} %get-tuple-element.60.refs_4_.refs_0_, f32[27,64]{1,0:T(8,128)S(1)} %copy-done.1, bf16[18,128,128]{2,1,0:T(8,128)(2,1)S(1)} %get-tuple-element.61.refs_2_.refs_0_.refs_3_), custom_call_target="tpu_custom_call" | custom-call | flops 100000000 | tf_op jit(solution)/shard_map/pallas_call | solution.py:62
  15.6 2.7 %shard_map.79 = (bf16[16,64,128]{2,1,0:T(8,128)(2,1)S(1)}, bf16[16,64,128]{2,1,0:T(8,128)(2,1)S(1)}, f32[108,64,128]{2,1,0:T(8,128)S(1)}) custom-call(bf16[64,64,128]{2,1,0:T(8,128)(2,1)S(1)} %get-tuple-element.60.refs_4_.refs_0_, bf16[16,64,128]{2,1,0:T(8,128)(2,1)S(1)} %collective-permute-done.4.refs_1_, ...), custom_call_target="tpu_custom_call" | custom-call | flops 100000000 | tf_op jit(solution)/shard_map/pallas_call | solution.py:62
  21.1 1.5 %collective-permute-start.8 = (bf16[16,128,128]{2,1,0:T(8,128)(2,1)S(1)}, bf16[16,128,128]{2,1,0:T(8,128)(2,1)S(1)}, u32[]{:S(2)}, u32[]{:S(2)}) collective-permute-start(bf16[16,128,128]{2,1,0:T(8,128)(2,1)S(1)} %get-tuple-element.72.refs_6_.refs_1_), channel_id=1, source_target_pairs={{0,2},{1,3},{2,0},{3,1},{4,6},{5,7},{6,4},{7,5},{8,10},{9,11},{10,... | collective-permute-start | bytes 1572872 | tf_op jit(solution)/shard_map/ppermute | solution.py:676
  22.6 3.2 %collective-permute-done.3.refs_5_.refs_9_ = bf16[18,128,128]{2,1,0:T(8,128)(2,1)S(1)} collective-permute-done((bf16[18,128,128]{2,1,0:T(8,128)(2,1)S(1)}, bf16[18,128,128]{2,1,0:T(8,128)(2,1)S(1)}, u32[]{:S(2)}, u32[]{:S(2)}) %collective-permute-start.3) | collective-permute-done | bytes 589856 | tf_op jit(solution)/shard_map/ppermute | solution.py:676
  25.9 1.5 %collective-permute-done.2.refs_2_.refs_4_ = bf16[18,128,128]{2,1,0:T(8,128)(2,1)S(1)} collective-permute-done((bf16[18,128,128]{2,1,0:T(8,128)(2,1)S(1)}, bf16[18,128,128]{2,1,0:T(8,128)(2,1)S(1)}, u32[]{:S(2)}, u32[]{:S(2)}) %collective-permute-start.2) | collective-permute-done | bytes 589856 | tf_op jit(solution)/shard_map/ppermute | solution.py:676
  27.4 2.0 %shard_map.81 = (f32[16,128,128]{2,1,0:T(8,128)S(1)}, bf16[16,128,128]{2,1,0:T(8,128)(2,1)S(1)}, bf16[256,256]{1,0:T(8,128)(2,1)S(1)}, f32[16,128,128]{2,1,0:T(8...) custom-call(bf16[18,128,128]{2,1,0:T(8,128)(2,1)S(1)} %get-tuple-element.61.refs_2_.refs_0_.refs_3_, ...), custom_call_target="tpu_custom_call" | custom-call | flops 100000000 | tf_op jit(solution)/shard_map/pallas_call | solution.py:62
  30.0 1.5 %collective-permute-start.13 = (bf16[16,128,128]{2,1,0:T(8,128)(2,1)S(1)}, bf16[16,128,128]{2,1,0:T(8,128)(2,1)S(1)}, u32[]{:S(2)}, u32[]{:S(2)}) collective-permute-start(bf16[16,128,128]{2,1,0:T(8,128)(2,1)S(1)} %get-tuple-element.86), channel_id=1, source_target_pairs={{0,4},{1,5},{2,6},{3,7},{4,0},{5,1},{6,2},{7,3},{8,12},{9,13},{10,... | collective-permute-start | bytes 1572872 | tf_op jit(solution)/shard_map/ppermute | solution.py:676
  31.6 7.1 %collective-permute-done.9.refs_7_ = bf16[16,128,128]{2,1,0:T(8,128)(2,1)S(1)} collective-permute-done((bf16[16,128,128]{2,1,0:T(8,128)(2,1)S(1)}, bf16[16,128,128]{2,1,0:T(8,128)(2,1)S(1)}, u32[]{:S(2)}, u32[]{:S(2)}) %collective-permute-start.9) | collective-permute-done | bytes 524320 | tf_op jit(solution)/shard_map/ppermute | solution.py:676
  38.6 3.4 %shard_map.82 = (f32[16,128,128]{2,1,0:T(8,128)S(1)}, f32[128,256]{1,0:T(8,128)S(1)}, bf16[18,128,128]{2,1,0:T(8,128)(2,1)S(1)}, f32[16,128,128]{2,1,0:T(8,128)S...) custom-call(bf16[256,256]{1,0:T(8,128)(2,1)S(1)} %get-tuple-element.73.refs_0_, ...), custom_call_target="tpu_custom_call" | custom-call | flops 100000000 | tf_op jit(solution)/shard_map/pallas_call | solution.py:62
  42.0 1.6 %collective-permute-start.10 = (bf16[18,128,128]{2,1,0:T(8,128)(2,1)S(1)}, bf16[18,128,128]{2,1,0:T(8,128)(2,1)S(1)}, u32[]{:S(2)}, u32[]{:S(2)}) collective-permute-start(bf16[18,128,128]{2,1,0:T(8,128)(2,1)S(1)} %get-tuple-element.78), channel_id=1, source_target_pairs={{0,4},{1,5},{2,6},{3,7},{4,0},{5,1},{6,2},{7,3},{8,12},{9,13},{10,... | collective-permute-start | bytes 1769480 | tf_op jit(solution)/shard_map/ppermute | solution.py:676
  44.1 4.2 %collective-permute-done.12.refs_1_ = bf16[16,128,128]{2,1,0:T(8,128)(2,1)S(1)} collective-permute-done((bf16[16,128,128]{2,1,0:T(8,128)(2,1)S(1)}, bf16[16,128,128]{2,1,0:T(8,128)(2,1)S(1)}, u32[]{:S(2)}, u32[]{:S(2)}) %collective-permute-start.12) | collective-permute-done | bytes 524320 | tf_op jit(solution)/shard_map/ppermute | solution.py:676
  48.3 1.5 %collective-permute-done.13.refs_3_ = bf16[16,128,128]{2,1,0:T(8,128)(2,1)S(1)} collective-permute-done((bf16[16,128,128]{2,1,0:T(8,128)(2,1)S(1)}, bf16[16,128,128]{2,1,0:T(8,128)(2,1)S(1)}, u32[]{:S(2)}, u32[]{:S(2)}) %collective-permute-start.13) | collective-permute-done | bytes 524320 | tf_op jit(solution)/shard_map/ppermute | solution.py:676
  50.8 3.0 %shard_map.84 = (f32[27,64,128]{2,1,0:T(8,128)S(1)}, f32[2,16,64,128]{3,2,1,0:T(8,128)S(1)}) custom-call(f32[108,64,128]{2,1,0:T(8,128)S(1)} %get-tuple-element.83.refs_0_, bf16[16,64,128]{2,1,0:T(8,128)(2,1)S(1)} %get-tuple-element.89.refs_1_, bf16[16,64,128]{2,1,0:T(8,128)(2,1)S(1)} %get-tuple-element.90.refs_2_.refs_0_), custom_call_target="tpu_custom_call" | custom-call | flops 100000000 | tf_op jit(solution)/shard_map/pallas_call | solution.py:62
  54.6 5.7 %collective-permute-start.22 = (bf16[16,64,128]{2,1,0:T(8,128)(2,1)S(1)}, bf16[16,64,128]{2,1,0:T(8,128)(2,1)S(1)}, u32[]{:S(2)}, u32[]{:S(2)}) collective-permute-start(bf16[16,64,128]{2,1,0:T(8,128)(2,1)S(1)} %get-tuple-element.92.refs_4_), channel_id=1, source_target_pairs={{0,8},{8,0},{16,24},{24,16},{1,9},{9,1},{17,25},{25,17},{2,10},{10... | collective-permute-start | bytes 786440 | tf_op jit(solution)/shard_map/ppermute | solution.py:689
  60.3 3.2 %shard_map.86 = (f32[32,128]{1,0:T(8,128)S(1)}, f32[2,16,64,128]{3,2,1,0:T(8,128)S(1)}) custom-call(f32[108,64,128]{2,1,0:T(8,128)S(1)} %get-tuple-element.83.refs_0_, bf16[16,64,128]{2,1,0:T(8,128)(2,1)S(1)} %collective-permute-done.14.refs_1_, bf16[16,64,128]{2,1,0:T(8,128)(2,1)S(1)} %collective-permute-done.15.refs_1_.refs_2_, ...), custom_call_target="tpu_custom_call" | custom-call | flops 100000000 | tf_op jit(solution)/shard_map/pallas_call | solution.py:62
  65.4 1.7 %collective-permute-start.19 = (f32[96,128]{1,0:T(8,128)S(1)}, f32[96,128]{1,0:T(8,128)S(1)}, u32[]{:S(2)}, u32[]{:S(2)}) collective-permute-start(f32[96,128]{1,0:T(8,128)S(1)} %get-tuple-element.101), channel_id=1, source_target_pairs={{0,8},{8,0},{16,24},{24,16},{1,9},{9,1},{17,25},{25,17},{2,10},{10... | collective-permute-start | bytes 147464 | tf_op jit(solution)/shard_map/ppermute | solution.py:692
  67.1 1.9 %collective-permute-start.20 = (f32[96,128]{1,0:T(8,128)S(1)}, f32[96,128]{1,0:T(8,128)S(1)}, u32[]{:S(2)}, u32[]{:S(2)}) collective-permute-start(f32[96,128]{1,0:T(8,128)S(1)} %get-tuple-element.102), channel_id=1, source_target_pairs={{0,16},{8,24},{16,0},{24,8},{1,17},{9,25},{17,1},{25,9},{2,18},{10... | collective-permute-start | bytes 147464 | tf_op jit(solution)/shard_map/ppermute | solution.py:692
  69.0 1.9 %collective-permute-start.21 = (f32[96,128]{1,0:T(8,128)S(1)}, f32[96,128]{1,0:T(8,128)S(1)}, u32[]{:S(2)}, u32[]{:S(2)}) collective-permute-start(f32[96,128]{1,0:T(8,128)S(1)} %get-tuple-element.103), channel_id=1, source_target_pairs={{0,24},{8,16},{16,8},{24,0},{1,25},{9,17},{17,9},{25,1},{2,26},{10... | collective-permute-start | bytes 147464 | tf_op jit(solution)/shard_map/ppermute | solution.py:692
  70.9 5.8 %shard_map.89 = (bf16[4096,128]{1,0:T(8,128)(2,1)}, f32[8,128]{1,0:T(8,128)S(1)}) custom-call(f32[2,16,64,128]{3,2,1,0:T(8,128)S(1)} %get-tuple-element.104.refs_0_, f32[2,16,64,128]{3,2,1,0:T(8,128)S(1)} %get-tuple-element.105.refs_1_, bf16[16,64,128]{2,1,0:T(8,128)(2,1)S(1)} %collective-permute-done.22.refs_2_, ...), custom_call_target="tpu_custom_call" | custom-call | flops 20000000000 | tf_op jit(solution)/shard_map/pallas_call | solution.py:62
  76.7 1.8 %shard_map.90 = (bf16[4096,128]{1,0:T(8,128)(2,1)}, f32[64,128]{1,0:T(8,128)}, f32[27,64]{1,0:T(8,128)}) custom-call(bf16[16,64,128]{2,1,0:T(8,128)(2,1)S(1)} %get-tuple-element.94.refs_0_, bf16[16,64,128]{2,1,0:T(8,128)(2,1)S(1)} %get-tuple-element.95.refs_1_, bf16[16,64,128]{2,1,0:T(8,128)(2,1)S(1)} %collective-permute-done.16.refs_2_, ...), custom_call_target="tpu_custom_call" | custom-call | flops 100000000 | tf_op jit(solution)/shard_map/pallas_call | solution.py:62
  (48 shorter events, 12.2 us)
Async XLA Ops:
  0.6 1.6 %collective-permute-start = (bf16[64,512]{1,0:T(8,128)(2,1)}, bf16[64,512]{1,0:T(8,128)(2,1)S(1)}, u32[]{:S(2)}, u32[]{:S(2)}) collective-permute-start(bf16[64,512]{1,0:T(8,128)(2,1)} %refs_2_.1), channel_id=1, source_target_pairs={{0,1},{1,0},{2,3},{3,2},{4,5},{5,4},{6,7},{7,6},{8,9},{9,8},{10,11... | collective-permute-start | bytes 196616 | tf_op jit(solution)/shard_map/ppermute | solution.py:676
  4.0 5.0 %collective-permute-start.1 = (bf16[32,64,128]{2,1,0:T(8,128)(2,1)S(1)}, bf16[32,64,128]{2,1,0:T(8,128)(2,1)S(1)}, u32[]{:S(2)}, u32[]{:S(2)}) collective-permute-start(bf16[32,64,128]{2,1,0:T(8,128)(2,1)S(1)} %get-tuple-element.59), channel_id=1, source_target_pairs={{0,1},{1,0},{2,3},{3,2},{4,5},{5,4},{6,7},{7,6},{8,9},{9,8},{10,11... | collective-permute-start | bytes 1572872 | tf_op jit(solution)/shard_map/ppermute | solution.py:676
  5.3 10.3 %collective-permute-start.4 = (bf16[16,64,128]{2,1,0:T(8,128)(2,1)S(1)}, bf16[16,64,128]{2,1,0:T(8,128)(2,1)S(1)}, u32[]{:S(2)}, u32[]{:S(2)}) collective-permute-start(bf16[16,64,128]{2,1,0:T(8,128)(2,1)S(1)} %get-tuple-element.66), channel_id=1, source_target_pairs={{0,8},{8,0},{16,24},{24,16},{1,9},{9,1},{17,25},{25,17},{2,10},{10... | collective-permute-start | bytes 786440 | tf_op jit(solution)/shard_map/ppermute | solution.py:689
  8.3 7.3 %collective-permute-start.5 = (bf16[16,64,128]{2,1,0:T(8,128)(2,1)S(1)}, bf16[16,64,128]{2,1,0:T(8,128)(2,1)S(1)}, u32[]{:S(2)}, u32[]{:S(2)}) collective-permute-start(bf16[16,64,128]{2,1,0:T(8,128)(2,1)S(1)} %get-tuple-element.67), channel_id=1, source_target_pairs={{8,16},{16,8},{9,17},{17,9},{10,18},{18,10},{11,19},{19,11},{12,20... | collective-permute-start | bytes 786440 | tf_op jit(solution)/shard_map/ppermute | solution.py:689
  9.6 16.3 %collective-permute-start.3 = (bf16[18,128,128]{2,1,0:T(8,128)(2,1)S(1)}, bf16[18,128,128]{2,1,0:T(8,128)(2,1)S(1)}, u32[]{:S(2)}, u32[]{:S(2)}) collective-permute-start(bf16[18,128,128]{2,1,0:T(8,128)(2,1)S(1)} %get-tuple-element.63.refs_3_.refs_8_), channel_id=1, source_target_pairs={{0,2},{1,3},{2,0},{3,1},{4,6},{5,7},{6,4},{7,5},{8,10},{9,11},{10,... | collective-permute-start | bytes 1769480 | tf_op jit(solution)/shard_map/ppermute | solution.py:676
  11.1 16.3 %collective-permute-start.2 = (bf16[18,128,128]{2,1,0:T(8,128)(2,1)S(1)}, bf16[18,128,128]{2,1,0:T(8,128)(2,1)S(1)}, u32[]{:S(2)}, u32[]{:S(2)}) collective-permute-start(bf16[18,128,128]{2,1,0:T(8,128)(2,1)S(1)} %get-tuple-element.61.refs_2_.refs_0_.refs_3_), channel_id=1, source_target_pairs={{0,4},{1,5},{2,6},{3,7},{4,0},{5,1},{6,2},{7,3},{8,12},{9,13},{10,... | collective-permute-start | bytes 1769480 | tf_op jit(solution)/shard_map/ppermute | solution.py:676
  15.5 3.4 %collective-permute-start.6 = (bf16[16,64,128]{2,1,0:T(8,128)(2,1)S(1)}, bf16[16,64,128]{2,1,0:T(8,128)(2,1)S(1)}, u32[]{:S(2)}, u32[]{:S(2)}) collective-permute-start(bf16[16,64,128]{2,1,0:T(8,128)(2,1)S(1)} %get-tuple-element.70), channel_id=1, source_target_pairs={{0,1},{1,0},{2,3},{3,2},{4,5},{5,4},{6,7},{7,6},{8,9},{9,8},{10,11... | collective-permute-start | bytes 786440 | tf_op jit(solution)/shard_map/ppermute | solution.py:676
  18.4 1.7 %collective-permute-start.7 = (bf16[16,64,128]{2,1,0:T(8,128)(2,1)S(1)}, bf16[16,64,128]{2,1,0:T(8,128)(2,1)S(1)}, u32[]{:S(2)}, u32[]{:S(2)}) collective-permute-start(bf16[16,64,128]{2,1,0:T(8,128)(2,1)S(1)} %get-tuple-element.71), channel_id=1, source_target_pairs={{0,1},{1,0},{2,3},{3,2},{4,5},{5,4},{6,7},{7,6},{8,9},{9,8},{10,11... | collective-permute-start | bytes 786440 | tf_op jit(solution)/shard_map/ppermute | solution.py:676
  20.2 18.5 %collective-permute-start.9 = (bf16[16,128,128]{2,1,0:T(8,128)(2,1)S(1)}, bf16[16,128,128]{2,1,0:T(8,128)(2,1)S(1)}, u32[]{:S(2)}, u32[]{:S(2)}) collective-permute-start(bf16[16,128,128]{2,1,0:T(8,128)(2,1)S(1)} %get-tuple-element.75.refs_6_), channel_id=1, source_target_pairs={{0,4},{1,5},{2,6},{3,7},{4,0},{5,1},{6,2},{7,3},{8,12},{9,13},{10,... | collective-permute-start | bytes 1572872 | tf_op jit(solution)/shard_map/ppermute | solution.py:676
  21.1 17.5 %collective-permute-start.8 = (bf16[16,128,128]{2,1,0:T(8,128)(2,1)S(1)}, bf16[16,128,128]{2,1,0:T(8,128)(2,1)S(1)}, u32[]{:S(2)}, u32[]{:S(2)}) collective-permute-start(bf16[16,128,128]{2,1,0:T(8,128)(2,1)S(1)} %get-tuple-element.72.refs_6_.refs_1_), channel_id=1, source_target_pairs={{0,2},{1,3},{2,0},{3,1},{4,6},{5,7},{6,4},{7,5},{8,10},{9,11},{10,... | collective-permute-start | bytes 1572872 | tf_op jit(solution)/shard_map/ppermute | solution.py:676
  29.4 18.9 %collective-permute-start.12 = (bf16[16,128,128]{2,1,0:T(8,128)(2,1)S(1)}, bf16[16,128,128]{2,1,0:T(8,128)(2,1)S(1)}, u32[]{:S(2)}, u32[]{:S(2)}) collective-permute-start(bf16[16,128,128]{2,1,0:T(8,128)(2,1)S(1)} %get-tuple-element.84), channel_id=1, source_target_pairs={{0,2},{1,3},{2,0},{3,1},{4,6},{5,7},{6,4},{7,5},{8,10},{9,11},{10,... | collective-permute-start | bytes 1572872 | tf_op jit(solution)/shard_map/ppermute | solution.py:676
  30.0 19.8 %collective-permute-start.13 = (bf16[16,128,128]{2,1,0:T(8,128)(2,1)S(1)}, bf16[16,128,128]{2,1,0:T(8,128)(2,1)S(1)}, u32[]{:S(2)}, u32[]{:S(2)}) collective-permute-start(bf16[16,128,128]{2,1,0:T(8,128)(2,1)S(1)} %get-tuple-element.86), channel_id=1, source_target_pairs={{0,4},{1,5},{2,6},{3,7},{4,0},{5,1},{6,2},{7,3},{8,12},{9,13},{10,... | collective-permute-start | bytes 1572872 | tf_op jit(solution)/shard_map/ppermute | solution.py:676
  42.0 21.5 %collective-permute-start.10 = (bf16[18,128,128]{2,1,0:T(8,128)(2,1)S(1)}, bf16[18,128,128]{2,1,0:T(8,128)(2,1)S(1)}, u32[]{:S(2)}, u32[]{:S(2)}) collective-permute-start(bf16[18,128,128]{2,1,0:T(8,128)(2,1)S(1)} %get-tuple-element.78), channel_id=1, source_target_pairs={{0,4},{1,5},{2,6},{3,7},{4,0},{5,1},{6,2},{7,3},{8,12},{9,13},{10,... | collective-permute-start | bytes 1769480 | tf_op jit(solution)/shard_map/ppermute | solution.py:676
  43.6 20.0 %collective-permute-start.11 = (bf16[18,128,128]{2,1,0:T(8,128)(2,1)S(1)}, bf16[18,128,128]{2,1,0:T(8,128)(2,1)S(1)}, u32[]{:S(2)}, u32[]{:S(2)}) collective-permute-start(bf16[18,128,128]{2,1,0:T(8,128)(2,1)S(1)} %get-tuple-element.80), channel_id=1, source_target_pairs={{0,2},{1,3},{2,0},{3,1},{4,6},{5,7},{6,4},{7,5},{8,10},{9,11},{10,... | collective-permute-start | bytes 1769480 | tf_op jit(solution)/shard_map/ppermute | solution.py:676
  50.2 3.6 %collective-permute-start.15 = (bf16[16,64,128]{2,1,0:T(8,128)(2,1)S(1)}, bf16[16,64,128]{2,1,0:T(8,128)(2,1)S(1)}, u32[]{:S(2)}, u32[]{:S(2)}) collective-permute-start(bf16[16,64,128]{2,1,0:T(8,128)(2,1)S(1)} %get-tuple-element.88), channel_id=1, source_target_pairs={{0,1},{1,0},{2,3},{3,2},{4,5},{5,4},{6,7},{7,6},{8,9},{9,8},{10,11... | collective-permute-start | bytes 786440 | tf_op jit(solution)/shard_map/ppermute | solution.py:676
  50.3 10.0 %collective-permute-start.14 = (bf16[16,64,128]{2,1,0:T(8,128)(2,1)S(1)}, bf16[16,64,128]{2,1,0:T(8,128)(2,1)S(1)}, u32[]{:S(2)}, u32[]{:S(2)}) collective-permute-start(bf16[16,64,128]{2,1,0:T(8,128)(2,1)S(1)} %get-tuple-element.87), channel_id=1, source_target_pairs={{0,1},{1,0},{2,3},{3,2},{4,5},{5,4},{6,7},{7,6},{8,9},{9,8},{10,11... | collective-permute-start | bytes 786440 | tf_op jit(solution)/shard_map/ppermute | solution.py:676
  53.9 13.2 %collective-permute-start.23 = (bf16[16,64,128]{2,1,0:T(8,128)(2,1)S(1)}, bf16[16,64,128]{2,1,0:T(8,128)(2,1)S(1)}, u32[]{:S(2)}, u32[]{:S(2)}) collective-permute-start(bf16[16,64,128]{2,1,0:T(8,128)(2,1)S(1)} %get-tuple-element.106), channel_id=1, source_target_pairs={{8,16},{16,8},{9,17},{17,9},{10,18},{18,10},{11,19},{19,11},{12,20... | collective-permute-start | bytes 786440 | tf_op jit(solution)/shard_map/ppermute | solution.py:689
  54.6 14.4 %collective-permute-start.22 = (bf16[16,64,128]{2,1,0:T(8,128)(2,1)S(1)}, bf16[16,64,128]{2,1,0:T(8,128)(2,1)S(1)}, u32[]{:S(2)}, u32[]{:S(2)}) collective-permute-start(bf16[16,64,128]{2,1,0:T(8,128)(2,1)S(1)} %get-tuple-element.92.refs_4_), channel_id=1, source_target_pairs={{0,8},{8,0},{16,24},{24,16},{1,9},{9,1},{17,25},{25,17},{2,10},{10... | collective-permute-start | bytes 786440 | tf_op jit(solution)/shard_map/ppermute | solution.py:689
  64.0 1.4 %collective-permute-start.18 = (f32[256,128]{1,0:T(8,128)S(1)}, f32[256,128]{1,0:T(8,128)S(1)}, u32[]{:S(2)}, u32[]{:S(2)}) collective-permute-start(f32[256,128]{1,0:T(8,128)S(1)} %get-tuple-element.99), channel_id=1, source_target_pairs={{0,1},{1,0},{2,3},{3,2},{4,5},{5,4},{6,7},{7,6},{8,9},{9,8},{10,11... | collective-permute-start | bytes 393224 | tf_op jit(solution)/shard_map/ppermute | solution.py:676
  64.0 12.6 %collective-permute-start.16 = (bf16[16,64,128]{2,1,0:T(8,128)(2,1)S(1)}, bf16[16,64,128]{2,1,0:T(8,128)(2,1)S(1)}, u32[]{:S(2)}, u32[]{:S(2)}) collective-permute-start(bf16[16,64,128]{2,1,0:T(8,128)(2,1)S(1)} %get-tuple-element.96), channel_id=1, source_target_pairs={{0,1},{1,0},{2,3},{3,2},{4,5},{5,4},{6,7},{7,6},{8,9},{9,8},{10,11... | collective-permute-start | bytes 786440 | tf_op jit(solution)/shard_map/ppermute | solution.py:676
  64.5 12.1 %collective-permute-start.17 = (bf16[16,64,128]{2,1,0:T(8,128)(2,1)S(1)}, bf16[16,64,128]{2,1,0:T(8,128)(2,1)S(1)}, u32[]{:S(2)}, u32[]{:S(2)}) collective-permute-start(bf16[16,64,128]{2,1,0:T(8,128)(2,1)S(1)} %get-tuple-element.97), channel_id=1, source_target_pairs={{0,1},{1,0},{2,3},{3,2},{4,5},{5,4},{6,7},{7,6},{8,9},{9,8},{10,11... | collective-permute-start | bytes 786440 | tf_op jit(solution)/shard_map/ppermute | solution.py:676
  65.4 11.2 %collective-permute-start.19 = (f32[96,128]{1,0:T(8,128)S(1)}, f32[96,128]{1,0:T(8,128)S(1)}, u32[]{:S(2)}, u32[]{:S(2)}) collective-permute-start(f32[96,128]{1,0:T(8,128)S(1)} %get-tuple-element.101), channel_id=1, source_target_pairs={{0,8},{8,0},{16,24},{24,16},{1,9},{9,1},{17,25},{25,17},{2,10},{10... | collective-permute-start | bytes 147464 | tf_op jit(solution)/shard_map/ppermute | solution.py:692
  67.1 9.6 %collective-permute-start.20 = (f32[96,128]{1,0:T(8,128)S(1)}, f32[96,128]{1,0:T(8,128)S(1)}, u32[]{:S(2)}, u32[]{:S(2)}) collective-permute-start(f32[96,128]{1,0:T(8,128)S(1)} %get-tuple-element.102), channel_id=1, source_target_pairs={{0,16},{8,24},{16,0},{24,8},{1,17},{9,25},{17,1},{25,9},{2,18},{10... | collective-permute-start | bytes 147464 | tf_op jit(solution)/shard_map/ppermute | solution.py:692
  69.0 7.7 %collective-permute-start.21 = (f32[96,128]{1,0:T(8,128)S(1)}, f32[96,128]{1,0:T(8,128)S(1)}, u32[]{:S(2)}, u32[]{:S(2)}) collective-permute-start(f32[96,128]{1,0:T(8,128)S(1)} %get-tuple-element.103), channel_id=1, source_target_pairs={{0,24},{8,16},{16,8},{24,0},{1,25},{9,17},{17,9},{25,1},{2,26},{10... | collective-permute-start | bytes 147464 | tf_op jit(solution)/shard_map/ppermute | solution.py:692
  (4 other events, 15.4 us)
